TPU v7x, 128 devices: a whole 4x4x4 slice. The times are simulated.
128 devices in a mesh: half: 2 (over core), grp: 8 (over x_lo, z), exp: 8 (over x_hi, y).
Axes of the slice: x: 4 (x_hi: 2, x_lo: 2; x = x_hi * 2 + x_lo), y: 4, z: 4, core: 2. Of those that a mesh axis runs over, the one named last changes fastest.
Arguments:
- residual: bfloat16 [512, 32, 2304], P('exp', ('half', 'grp')), may hold values from -6 to 6
- queries: bfloat16 [512, 32, 4096], P(None, ('half', 'grp'), 'exp'), may hold values from -6 to 6
- key_in: bfloat16 [512, 32, 4096], P(None, ('half', 'grp'), 'exp'), may hold values from -6 to 6
- value_in: bfloat16 [512, 32, 4096], P(None, ('half', 'grp'), 'exp'), may hold values from -6 to 6
- log_decay: float32 [512, 32, 4096], P(None, ('half', 'grp'), 'exp'), may hold values from -0.8 to 0, as said below
- update_rate: float32 [512, 32, 32], P(None, ('half', 'grp'), 'exp'), may hold values from 0.1 to 0.9
- counts: int32 [32], P(('half', 'grp')), may hold values from 1 to 512, 12288 in all
- init_state: float32 [32, 32, 128, 128], P(('half', 'grp'), 'exp'), may hold values from -4 to 4
- w_out: bfloat16 [4096, 2304], P('exp'), may hold values from -0.09375 to 0.09375
- norm_gain: bfloat16 [2304], replicated, may hold values from 0.099609375 to 1.8984375
- w_router: bfloat16 [2304, 128], replicated, may hold values from -0.125 to 0.125
- expert_ids: int32 [512, 32, 8], P('exp', ('half', 'grp')), may hold values from 0 to 127, all different within a row
- w_gate: bfloat16 [128, 2304, 1024], P(('half', 'grp', 'exp')), may hold values from -0.125 to 0.125
- w_up: bfloat16 [128, 2304, 1024], P(('half', 'grp', 'exp')), may hold values from -0.125 to 0.125
- w_down: bfloat16 [128, 1024, 2304], P(('half', 'grp', 'exp')), may hold values from -0.1875 to 0.1875
- dec_query: bfloat16 [32, 2, 32, 128], P('half', None, 'grp'), may hold values from -6 to 6
- dec_key: bfloat16 [32, 2, 32, 128], P('half', None, 'grp'), may hold values from -6 to 6
- dec_value: bfloat16 [32, 2, 32, 128], P('half', None, 'grp', 'exp'), may hold values from -6 to 6
- dec_decay: float32 [32, 2, 32, 128], P('half', None, 'grp'), may hold values from -0.2 to 0, as said below
- dec_beta: float32 [32, 2, 32], P('half', None, 'grp'), may hold values from 0.1 to 0.9
Outputs:
- hidden_out: bfloat16 [512, 32, 2304], P('exp', ('half', 'grp'))
- dec_out: float32 [32, 2, 32, 128], P('half', None, 'grp', 'exp')
- dec_state: float32 [32, 32, 128, 128], P('half', 'grp', None, 'exp')
Inputs may be any that keep to these rules, and one draw needn't show every extreme that they name: `log_decay`: log forget factors, all negative. `dec_decay`: log forget factors, all negative.
All inputs are finite; a program needn't handle non-finite values. No bound on the sum of `counts` on one device may be relied on, other than what follows from the above.
Results may differ from a plain program's by a relative error of at most 0.0075.
Values may be sent and summed in bfloat16 or wider, within the bound.
No kernel may reach another device: no remote copies, remote signals or barrier semaphores. Data moves between devices by JAX's collectives and lax.ppermute only.
A program may use at most 192 MiB of HBM per device.

v0:
```python
import jax
import jax.numpy as jnp
from jax import lax
from jax.sharding import PartitionSpec as P

EPSILON = 1e-06
ROUTE_SCALE = 2.446
highest = lax.Precision.HIGHEST


def normalize_keys(key_rows):
    return key_rows * lax.rsqrt(jnp.sum(key_rows * key_rows, axis=-1, keepdims=True) + EPSILON)


def delta_step(carry_state, query_row, key_row, value_row, decay_row, rate_row):
    carry_state = jnp.exp(decay_row)[..., None] * carry_state
    guessed = jnp.einsum("...kv,...k->...v", carry_state, key_row, precision=highest)
    carry_state = (
        carry_state
        + rate_row[..., None, None] * key_row[..., :, None] * (value_row - guessed)[..., None, :]
    )
    output = jnp.einsum(
        "...kv,...k->...v", carry_state, query_row, precision=highest
    ) * query_row.shape[-1] ** (-0.5)
    return (carry_state, output)


def block_first(member):
    return jnp.moveaxis(member, 1, 0)


def shards(
    residual,
    queries,
    key_in,
    value_in,
    log_decay,
    update_rate,
    counts,
    init_state,
    w_out,
    norm_gain,
    w_router,
    expert_ids,
    w_gate,
    w_up,
    w_down,
    dec_query,
    dec_key,
    dec_value,
    dec_decay,
    dec_beta,
):
    length = queries.shape[0]
    req_here = queries.shape[1]
    heads_here = init_state.shape[1]
    key_dim = init_state.shape[2]
    value_dim = init_state.shape[3]
    model_width = residual.shape[2]
    block_len = min(64, length)
    block_count = length // block_len
    batch_size = req_here * heads_here
    live_mask = (jnp.arange(length)[:, None] < counts[None, :]).astype(jnp.float32)

    def to_blocks(member, depth):
        member = member.reshape(length, req_here, heads_here, depth).transpose(1, 2, 0, 3)
        return member.reshape(batch_size, block_count, block_len, depth)

    query_blk = to_blocks(queries.astype(jnp.float32), key_dim)
    key_blk = normalize_keys(to_blocks(key_in.astype(jnp.float32), key_dim))
    value_blk = to_blocks(value_in.astype(jnp.float32), value_dim)
    decay_blk = to_blocks(log_decay * live_mask[:, :, None], key_dim)
    rate_blk = (
        (update_rate * live_mask[:, :, None])
        .transpose(1, 2, 0)
        .reshape(batch_size, block_count, block_len)
    )
    within = jnp.cumsum(decay_blk, axis=2)
    ending = within[:, :, -1:, :]
    key_up = key_blk * jnp.exp(within)
    key_down = key_blk * jnp.exp(-within)
    query_up = query_blk * jnp.exp(within)
    key_end = key_blk * jnp.exp(ending - within)
    index_row = jnp.arange(block_len)
    strict = (index_row[:, None] > index_row[None, :]).astype(jnp.float32)
    lower_mask = (index_row[:, None] >= index_row[None, :]).astype(jnp.float32)
    pair_mat = jnp.einsum("bnck,bndk->bncd", key_up, key_down, precision=highest)
    system = jnp.eye(block_len, dtype=jnp.float32) + rate_blk[..., None] * pair_mat * strict
    solved_v = lax.linalg.triangular_solve(
        system, rate_blk[..., None] * value_blk, left_side=True, lower=True, unit_diagonal=True
    )
    solved_k = lax.linalg.triangular_solve(
        system, rate_blk[..., None] * key_up, left_side=True, lower=True, unit_diagonal=True
    )
    reach_mat = jnp.einsum("bnck,bndk->bncd", query_up, key_down, precision=highest) * lower_mask
    fade_out = jnp.exp(ending[:, :, 0, :])

    def block_step(carry_state, inputs):
        base_v, base_k, q_up, reach_b, k_end, fade_b = inputs
        update = base_v - jnp.einsum("bck,bkv->bcv", base_k, carry_state, precision=highest)
        output = jnp.einsum("bck,bkv->bcv", q_up, carry_state, precision=highest) + jnp.einsum(
            "bcd,bdv->bcv", reach_b, update, precision=highest
        )
        carry_state = fade_b[:, :, None] * carry_state + jnp.einsum(
            "bck,bcv->bkv", k_end, update, precision=highest
        )
        return (carry_state, output)

    scanned = (
        block_first(solved_v),
        block_first(solved_k),
        block_first(query_up),
        block_first(reach_mat),
        block_first(key_end),
        block_first(fade_out),
    )
    final_state, outputs = lax.scan(
        block_step, init_state.reshape(batch_size, key_dim, value_dim), scanned
    )
    attended = (outputs * key_dim ** (-0.5)).astype(jnp.bfloat16)
    attended = attended.reshape(block_count, req_here, heads_here, block_len, value_dim).transpose(
        0, 3, 1, 2, 4
    )
    attended = attended.reshape(length, req_here, heads_here * value_dim)
    rows_here = length // lax.axis_size("exp")
    projected = lax.psum_scatter(
        jnp.einsum("trk,kd->trd", attended, w_out, preferred_element_type=jnp.float32),
        "exp",
        scatter_dimension=0,
        tiled=True,
    )
    mixed_rows = residual.astype(jnp.float32) + projected
    normed = (
        mixed_rows
        * lax.rsqrt(jnp.mean(mixed_rows * mixed_rows, axis=-1, keepdims=True) + EPSILON)
        * norm_gain.astype(jnp.float32)
    ).astype(jnp.bfloat16)
    scores = jax.nn.sigmoid(
        jnp.einsum("trd,de->tre", normed, w_router, preferred_element_type=jnp.float32)
    )
    picked = jnp.take_along_axis(scores, expert_ids, axis=2)
    weights = ROUTE_SCALE * picked / jnp.sum(picked, axis=2, keepdims=True)
    experts = w_router.shape[1]
    top_count = expert_ids.shape[2]
    capacity = 3 * rows_here * req_here * top_count // (2 * experts)
    flat_ids = expert_ids.reshape(-1)
    pick_total = flat_ids.shape[0]
    onehot = (flat_ids[:, None] == jnp.arange(experts, dtype=jnp.int32)[None, :]).astype(jnp.int32)
    slot_rank = jnp.sum(
        onehot * (jnp.cumsum(onehot, axis=0, dtype=jnp.int32) - 1), axis=1, dtype=jnp.int32
    )
    is_kept = slot_rank < capacity
    position = jnp.where(is_kept, flat_ids * capacity + slot_rank, experts * capacity)
    owner_pick = (
        jnp.full((experts * capacity + 1,), pick_total, jnp.int32)
        .at[position]
        .set(jnp.arange(pick_total, dtype=jnp.int32))[:-1]
    )
    token_flat = normed.reshape(-1, model_width)
    padded = jnp.concatenate([token_flat, jnp.zeros((1, model_width), jnp.bfloat16)], axis=0)
    outgoing = padded[owner_pick // top_count].reshape(experts, capacity, model_width)
    arrived = lax.all_to_all(
        outgoing, ("half", "grp", "exp"), split_axis=0, concat_axis=0, tiled=True
    )
    gate_act = jnp.einsum("...d,df->...f", arrived, w_gate[0], preferred_element_type=jnp.float32)
    up_act = jnp.einsum("...d,df->...f", arrived, w_up[0], preferred_element_type=jnp.float32)
    inner = (jax.nn.silu(gate_act) * up_act).astype(jnp.bfloat16)
    returned = lax.all_to_all(
        jnp.einsum("...f,fd->...d", inner, w_down[0], preferred_element_type=jnp.float32).astype(
            jnp.bfloat16
        ),
        ("half", "grp", "exp"),
        split_axis=0,
        concat_axis=0,
        tiled=True,
    )
    back_rows = jnp.concatenate(
        [returned.reshape(-1, model_width), jnp.zeros((1, model_width), jnp.bfloat16)], axis=0
    )
    fetched = (
        back_rows[position].astype(jnp.float32).reshape(rows_here, req_here, top_count, model_width)
    )
    routed = jnp.sum(fetched * weights[..., None], axis=2)
    hidden_out = (mixed_rows + routed).astype(jnp.bfloat16)
    relaid = lax.all_to_all(
        lax.all_to_all(
            final_state.reshape(req_here, heads_here, key_dim, value_dim).astype(jnp.bfloat16),
            "exp",
            split_axis=3,
            concat_axis=1,
            tiled=True,
        ),
        "grp",
        split_axis=1,
        concat_axis=0,
        tiled=True,
    ).astype(jnp.float32)
    dec_q = dec_query.astype(jnp.float32)
    dec_k = normalize_keys(dec_key.astype(jnp.float32))
    dec_v = dec_value.astype(jnp.float32)
    carry_state = relaid
    outputs_dec = []
    for turn_idx in range(dec_query.shape[1]):
        carry_state, output = delta_step(
            carry_state,
            dec_q[:, turn_idx],
            dec_k[:, turn_idx],
            dec_v[:, turn_idx],
            dec_decay[:, turn_idx],
            dec_beta[:, turn_idx],
        )
        outputs_dec.append(output)
    dec_out = jnp.stack(outputs_dec, axis=1)
    return (hidden_out, dec_out, carry_state)


def solution(mesh):
    return jax.shard_map(
        shards,
        mesh=mesh,
        in_specs=(
            P("exp", ("half", "grp"), None),
            P(None, ("half", "grp"), "exp"),
            P(None, ("half", "grp"), "exp"),
            P(None, ("half", "grp"), "exp"),
            P(None, ("half", "grp"), "exp"),
            P(None, ("half", "grp"), "exp"),
            P(("half", "grp")),
            P(("half", "grp"), "exp", None, None),
            P("exp", None),
            P(),
            P(),
            P("exp", ("half", "grp"), None),
            P(("half", "grp", "exp"), None, None),
            P(("half", "grp", "exp"), None, None),
            P(("half", "grp", "exp"), None, None),
            P("half", None, "grp", None),
            P("half", None, "grp", None),
            P("half", None, "grp", "exp"),
            P("half", None, "grp", None),
            P("half", None, "grp"),
        ),
        out_specs=(
            P("exp", ("half", "grp"), None),
            P("half", None, "grp", "exp"),
            P("half", "grp", None, "exp"),
        ),
        check_vma=False,
    )
```

profile of v0, /device:TPU:24, one launch (start us, length us, event | category | flops | bytes accessed | tf_op | source)
XLA Modules:
  0.0 1062.6 jit_solution(11953470021594809113)
XLA Ops:
  7.2 4.3 copy.198
  11.6 3.2 broadcast_multiply_fusion.1
  14.8 2.9 copy.199
  17.7 2.8 fusion.32
  23.5 2.4 copy.201
  28.7 2.9 copy.202
  31.6 2.4 copy.216
  35.7 2.9 copy.217
  38.6 2.4 copy.209
  42.6 3.0 copy.210
  45.7 10.5 broadcast_multiply_fusion
  57.5 5.2 add_bitcast_fusion
  62.6 316.1 %custom-call.6 = f32[8,8,1,64,64]{3,4,2,1,0:T(8,128)} custom-call(f32[8,8,1,64,64]{4,3,2,1,0:T(8,128)} %add_bitcast_fusion), custom_call_target="InvertDiagBlocksLowerTriangular" | custom-call | tf_op jit(solution)/shard_map/triangular_solve/custom-call.1 | solution.py:89
  378.8 7.2 fusion.40
  386.1 5.0 fusion.45
  391.1 5.1 multiply_bitcast_fusion
  396.2 71.8 %while.12 = (s32[]{:T(128)}, f32[8,128,128]{2,1,0:T(8,128)S(1)}, f32[8,8,64,128]{3,2,1,0:T(8,128)}, f32[8,8,128]{2,0,1:T(8,128)}, f32[8,8,64,128]{3,0,2,1:T(8,12...) while((s32[]{:T(128)}, f32[8,128,128]{2,1,0:T(8,128)S(1)}, ...), condition=%wide.region_3.5_spmd, body=%wide.region_2.4_spmd.sunk | while | flops 352714752 | bytes 6043765 | solution.py:117
  396.6 2.7 constant_dynamic-slice_fusion.5
  405.6 2.7 constant_dynamic-slice_fusion.5
  414.5 2.7 constant_dynamic-slice_fusion.5
  423.4 2.7 constant_dynamic-slice_fusion.5
  430.2 2.1 fusion.125
  432.3 2.7 constant_dynamic-slice_fusion.5
  439.2 2.1 fusion.125
  441.2 2.7 constant_dynamic-slice_fusion.5
  450.2 2.7 constant_dynamic-slice_fusion.5
  459.1 2.7 constant_dynamic-slice_fusion.5
  465.9 2.1 fusion.125
  471.8 2.3 reshape.274
  474.0 7.5 fusion.20
  482.5 7.3 all-to-all-start.2
  491.3 4.3 scatter_custom_fusion
  495.7 112.2 %reduce-scatter.2.cloned.1.call-done = f32[64,2,2304]{2,0,1:T(8,128)} async-done(((f32[512,2,2304]{2,0,1:T(8,128)}), f32[64,2,2304]{2,0,1:T(8,128)}) %reduce-scatter.2.cloned.1.call-update) | async-done | bytes 1179664 | tf_op jit(solution)/shard_map/reduce_scatter | solution.py:126
  610.6 7.4 gather_fusion
  618.0 11.1 %reshape.277 = bf16[128,12,2304]{2,1,0:T(8,128)(2,1)} reshape(bf16[1536,2304]{1,0:T(8,128)(2,1)} %gather_fusion) | data formatting | bytes 14155776 | tf_op jit(solution)/shard_map/reshape | solution.py:161
  629.1 8.8 all-to-all-start
  638.6 152.2 %all-to-all-done = bf16[128,12,2304]{2,1,0:T(8,128)(2,1)} async-done(((bf16[128,12,2304]{2,1,0:T(8,128)(2,1)}), bf16[128,12,2304]{2,1,0:T(8,128)(2,1)}, u32[]{:S(2)}, u32[]{:S(2)}) %all-to-all-start) | async-done | bytes 7077920 | tf_op jit(solution)/shard_map/all_to_all | solution.py:162
  790.8 3.5 all-to-all-start.3
  794.3 13.2 %fusion.9 = f32[128,12,1024]{2,0,1:T(8,128)} fusion(bf16[128,12,2304]{2,1,0:T(8,128)(2,1)} %all-to-all-done, bf16[1,2304,1024]{2,1,0:T(8,128)(2,1)} %param.37), kind=kOutput, calls=%fused_computation.22 | convolution fusion | flops 7247757312 | bytes 18087936 | tf_op jit(solution)/shard_map/...d,df->...f/dot_general | solution.py:166
  807.5 24.5 %convolution_convert_fusion = bf16[128,12,2304]{2,0,1:T(8,128)(2,1)} fusion(bf16[1,1024,2304]{2,1,0:T(8,128)(2,1)} %param.38, f32[128,12,1024]{2,0,1:T(8,128)} %fusion.9, bf16[1,2304,1024]{2,1,0:T(8,128)(2,1)} %param.36, bf16[128,12,2304]{2,1,0:T(8,128)(2,1)} %all-to-all-done), kind=kOutput, calls=%fused_computation.20 | convolution fusion | flops 14508490752 | bytes 29884416 | tf_op jit(solution)/shard_map/...f,fd->...d/dot_general | solution.py:169
  832.1 10.7 %copy.236 = bf16[128,12,2304]{2,1,0:T(8,128)(2,1)} copy(bf16[128,12,2304]{2,0,1:T(8,128)(2,1)} %convolution_convert_fusion) | data formatting | bytes 14155776 | tf_op jit(solution)/shard_map/convert_element_type | solution.py:169
  842.8 15.7 %all-to-all-start.1 = ((bf16[128,12,2304]{2,1,0:T(8,128)(2,1)}), bf16[128,12,2304]{2,1,0:T(8,128)(2,1)}, u32[]{:S(2)}, u32[]{:S(2)}) async-start(bf16[128,12,2304]{2,1,0:T(8,128)(2,1)} %copy.236), calls=%async_computation.2 | async-start | bytes 18874368 | tf_op jit(solution)/shard_map/all_to_all | solution.py:168
  864.2 8.4 gather_fusion.2
  873.6 141.2 %all-to-all-done.1 = bf16[128,12,2304]{2,1,0:T(8,128)(2,1)} async-done(((bf16[128,12,2304]{2,1,0:T(8,128)(2,1)}), bf16[128,12,2304]{2,1,0:T(8,128)(2,1)}, u32[]{:S(2)}, u32[]{:S(2)}) %all-to-all-start.1) | async-done | bytes 7077920 | tf_op jit(solution)/shard_map/all_to_all | solution.py:168
  1014.8 11.2 %reshape.278 = bf16[1536,2304]{1,0:T(8,128)(2,1)} reshape(bf16[128,12,2304]{2,1,0:T(8,128)(2,1)} %all-to-all-done.1) | data formatting | bytes 14155776 | tf_op jit(solution)/shard_map/reshape | solution.py:178
  1026.0 6.4 concatenate.7
  1032.3 13.9 %gather_fusion.1 = bf16[1024,2304]{1,0:T(8,128)(2,1)} fusion(bf16[1537,2304]{1,0:T(8,128)(2,1)} %concatenate.7, s32[1024]{0:T(1024)S(1)} %broadcast_clamp_fusion), kind=kCustom, calls=%fused_computation.1 | custom fusion | bytes 9441280 | tf_op jit(solution)/shard_map/gather | solution.py:181
  1046.3 7.4 fusion.8
  (180 shorter events, 71.5 us)
Async XLA Ops:
  7.2 466.9 %copy-start = (bf16[512,2304]{1,0:T(8,128)(2,1)S(1)}, bf16[512,2304]{1,0:T(8,128)(2,1)}, u32[]{:S(2)}) copy-start(bf16[512,2304]{1,0:T(8,128)(2,1)} %param.32) | copy-start | bytes 7077892
  7.2 600.7 %reduce-scatter.2.cloned.1.call-start = ((), (), s32[]{:S(2)}) async-start(), calls=%async_computation.5 | async-start | bytes 10616832 | tf_op jit(solution)/shard_map/reduce_scatter | solution.py:126
  7.2 4.3 copy-start.25
  17.7 4.8 copy-start.22
  20.5 1.3 copy-start.7
  42.6 3.0 copy-start.13
  42.6 3.0 copy-start.14
  42.6 3.1 copy-start.17
  56.2 1.3 copy-start.3
  378.8 7.3 copy-start.8
  378.8 7.3 copy-start.9
  386.1 5.0 copy-start.4
  386.1 5.0 copy-start.5
  391.1 5.1 copy-start.2
  481.5 8.2 copy-start.16
  481.5 8.6 copy-start.23
  482.5 125.4 %copy-start.10 = (bf16[64,2,2304]{2,1,0:T(2,128)(2,1)S(1)}, bf16[64,2,2304]{2,1,0:T(2,128)(2,1)}, u32[]{:S(2)}) copy-start(bf16[64,2,2304]{2,1,0:T(2,128)(2,1)} %param.24) | copy-start | bytes 1769476
  482.5 146.6 %all-to-all-start.2 = ((bf16[2,4,128,128]{2,1,0,3:T(4,128)(2,1)}), bf16[2,4,128,128]{2,1,0,3:T(4,128)(2,1)S(1)}, u32[]{:S(2)}, u32[]{:S(2)}) async-start(bf16[2,4,128,128]{2,1,0,3:T(4,128)(2,1)} %bitcast.52), calls=%async_computation.3 | async-start | bytes 524288 | tf_op jit(solution)/shard_map/all_to_all | solution.py:186
  607.9 1.6 copy-start.6
  629.1 161.8 %all-to-all-start = ((bf16[128,12,2304]{2,1,0:T(8,128)(2,1)}), bf16[128,12,2304]{2,1,0:T(8,128)(2,1)}, u32[]{:S(2)}, u32[]{:S(2)}) async-start(bf16[128,12,2304]{2,1,0:T(8,128)(2,1)} %reshape.277), calls=%async_computation.1 | async-start | bytes 18874368 | tf_op jit(solution)/shard_map/all_to_all | solution.py:162
  790.8 51.9 %all-to-all-start.3 = ((bf16[2,32,128,16]{2,3,0,1:T(8,128)(2,1)}), bf16[2,32,128,16]{2,3,0,1:T(8,128)(2,1)S(1)}, u32[]{:S(2)}, u32[]{:S(2)}) async-start(bf16[2,32,128,16]{2,3,0,1:T(8,128)(2,1)} %copy.244), calls=%async_computation.4 | async-start | bytes 524288 | tf_op jit(solution)/shard_map/all_to_all | solution.py:185
  842.7 16.0 %copy-start.20 = (bf16[16,2,4,16]{3,2,1,0:T(4,128)(2,1)S(1)}, bf16[16,2,4,16]{3,2,1,0:T(4,128)(2,1)}, u32[]{:S(2)}) copy-start(bf16[16,2,4,16]{3,2,1,0:T(4,128)(2,1)} %param.41) | copy-start | bytes 12292
  842.7 16.0 %copy-start.24 = (f32[16,2,4]{0,2,1:T(4,128)S(1)}, f32[16,2,4]{0,2,1:T(4,128)}, u32[]{:S(2)}) copy-start(f32[16,2,4]{0,2,1:T(4,128)} %param.43) | copy-start | bytes 1540
  842.7 16.2 %copy-start.18 = (bf16[16,2,4,128]{3,2,1,0:T(4,128)(2,1)S(1)}, bf16[16,2,4,128]{3,2,1,0:T(4,128)(2,1)}, u32[]{:S(2)}) copy-start(bf16[16,2,4,128]{3,2,1,0:T(4,128)(2,1)} %param.40) | copy-start | bytes 98308
  842.7 16.4 %copy-start.21 = (bf16[16,2,4,128]{3,2,1,0:T(4,128)(2,1)S(1)}, bf16[16,2,4,128]{3,2,1,0:T(4,128)(2,1)}, u32[]{:S(2)}) copy-start(bf16[16,2,4,128]{3,2,1,0:T(4,128)(2,1)} %param.39) | copy-start | bytes 98308
  842.7 16.5 %copy-start.19 = (f32[16,2,4,128]{3,2,1,0:T(4,128)S(1)}, f32[16,2,4,128]{3,2,1,0:T(4,128)}, u32[]{:S(2)}) copy-start(f32[16,2,4,128]{3,2,1,0:T(4,128)} %param.42) | copy-start | bytes 196612
  842.8 172.0 %all-to-all-start.1 = ((bf16[128,12,2304]{2,1,0:T(8,128)(2,1)}), bf16[128,12,2304]{2,1,0:T(8,128)(2,1)}, u32[]{:S(2)}, u32[]{:S(2)}) async-start(bf16[128,12,2304]{2,1,0:T(8,128)(2,1)} %copy.236), calls=%async_computation.2 | async-start | bytes 18874368 | tf_op jit(solution)/shard_map/all_to_all | solution.py:168
  860.6 3.3 copy-start.15
  862.0 10.6 copy-start.12
  1046.3 7.4 copy-start.11
  1046.3 9.0 copy-start.1
Sparse Core Ops, SparseCore 0:
  481.7 126.1 reduce-scatter.1
where the time goes:
time: 1080 us; the launch traced here: 1060 us
  waiting for transfers between devices  406 us (38%)
  other arithmetic  351 us (32%)
  local copies, waits for them, and re-layouts  140 us (13%)
  matrix products  115 us (11%)
  starting transfers between devices  35.3 us (3%)
  between operations  15.2 us (1%)
    another operation x3, other arithmetic, shards(): lax.linalg.triangular_solve(system, rate_blk[..., None] * value_blk, left...  316 us
    all_to_all x1, waiting for transfers between devices, shards(): lax.all_to_all(outgoing, ('half', 'grp', 'exp'), split_axis=0, concat_axi...  152 us
    all_to_all x1, waiting for transfers between devices, shards(): lax.all_to_all(jnp.einsum('...f,fd->...d', inner, w_down[0], preferred_el...  141 us
    reduce_scatter x1, waiting for transfers between devices, shards(): lax.psum_scatter(jnp.einsum('trk,kd->trd', attended, w_out, preferred_ele...  112 us
    dynamic_slice x16, local copies, waits for them, and re-layouts, shards(): lax.scan(block_step, init_state.reshape(batch_size, key_dim, value_dim),...  27.7 us
    dot_general x1, matrix products, shards(): jnp.einsum('...f,fd->...d', inner, w_down[0], preferred_element_type=jnp....  24.5 us
  transfers between devices with their start and end apart: 5, of which 3 were waited for; matrix products, arithmetic and copies ran while one was open for 9% of the time, Pallas kernels for 0%

commit v1 on v0

v1 whole, which is shorter than its diff:
```python
import functools

import jax
import jax.numpy as jnp
from jax import lax
from jax.experimental import pallas as pl
from jax.experimental.pallas import tpu as pltpu
from jax.sharding import PartitionSpec as P

EPSILON = 1e-06
ROUTE_SCALE = 2.446
LANES = 128
BLOCK = 64
MIB = 1 << 20
F32 = jnp.float32
BF16 = jnp.bfloat16

NN = (((1,), (0,)), ((), ()))
NT = (((1,), (1,)), ((), ()))
TN = (((0,), (0,)), ((), ()))


def dot(left, right, dims=NN):
    return lax.dot_general(left, right, dims, preferred_element_type=F32)


def halves(member):
    high = member.astype(BF16)
    return high, (member - high.astype(F32)).astype(BF16)


def dot3(left, right, dims=NN):
    return (
        dot(left[0], right[0], dims) + dot(left[0], right[1], dims) + dot(left[1], right[0], dims)
    )


def iota(shape, dim):
    return lax.broadcasted_iota(jnp.int32, shape, dim)


def delta_kernel(
    counts, q_ref, k_ref, v_ref, d_ref, rate_ref, init_ref, w_ref,
    part_ref, final_ref,
    state, rate_col, q_all, k_all, v_all, att,
):
    step = pl.program_id(0)
    chains, key_dim, _ = init_ref.shape
    requests = chains // (w_ref.shape[0] // LANES)
    heads = chains // requests
    every = range(chains)

    @pl.when(step == 0)
    def _():
        for chain in every:
            state[chain] = init_ref[chain].T
        rate_col[...] = rate_ref[...].T

    q_all[...] = q_ref[...].astype(F32)
    k_all[...] = k_ref[...].astype(F32)
    v_all[...] = v_ref[...].astype(F32)

    row = iota((BLOCK, BLOCK), 0)
    col = iota((BLOCK, BLOCK), 1)
    lower = jnp.where(row >= col, 1.0, 0.0).astype(BF16)
    position = step * BLOCK + iota((BLOCK, 1), 0)
    rates = rate_col[pl.ds(pl.multiple_of(step * BLOCK, BLOCK), BLOCK), :]
    live = [position < counts[request] for request in range(requests)]
    live = [live[chain // heads] for chain in every]
    rows = [pl.ds((c % heads) * requests + c // heads, BLOCK, stride=chains) for c in every]

    withins = []
    for c in every:
        decay = jnp.where(live[c], d_ref[rows[c], :], 0.0)
        high, rest = decay.astype(BF16), decay - decay.astype(BF16).astype(F32)
        middle, low = halves(rest)
        withins.append(dot(lower, high) + dot(lower, middle) + dot(lower, low))
    rate = [jnp.where(live[c], rates[:, c : c + 1], 0.0) for c in every]
    key_up, key_end, query_up, fades, systems, reaches = [], [], [], [], [], []
    for c in every:
        key = k_all[rows[c], :]
        key = key * lax.rsqrt(jnp.sum(key * key, axis=-1, keepdims=True) + EPSILON)
        grow = jnp.exp(withins[c])
        fade = grow[BLOCK - 1 :, :]
        down = key * jnp.exp(-withins[c])
        up_hi, up_lo = halves(key * grow)
        down_hi, down_lo = halves(down)
        query = (q_all[rows[c], :] * grow).astype(BF16)
        both = dot(jnp.concatenate([up_hi, query], axis=0), down_hi, NT)
        pair = both[:BLOCK] + dot(up_hi, down_lo, NT) + dot(up_lo, down_hi, NT)
        reaches.append(jnp.where(row >= col, both[BLOCK:], 0.0).astype(BF16))
        systems.append(jnp.where(row > col, rate[c] * pair, 0.0))
        key_up.append(key * grow)
        key_end.append(halves(down * fade))
        query_up.append(query)
        fades.append(fade)
    near = row >> 1 == col >> 1
    inverse = [jnp.where(row == col, 1.0, 0.0) - jnp.where(near, s, 0.0) for s in systems]
    for bit in range(1, BLOCK.bit_length() - 1):
        joins = (row >> (bit + 1) == col >> (bit + 1)) & (row >> bit != col >> bit)
        split = [halves(member) for member in inverse]
        inner = [
            dot3(halves(jnp.where(joins, systems[c], 0.0)), split[c]) for c in every
        ]
        inverse = [inverse[c] - dot3(split[c], halves(inner[c])) for c in every]
    split = [halves(member) for member in inverse]
    base_v = [dot3(split[c], halves(rate[c] * v_all[rows[c], :])) for c in every]
    base_k = [halves(dot3(split[c], halves(rate[c] * key_up[c]))) for c in every]
    boths, carries, updates = [], [], []
    for c in every:
        carry = halves(state[c])
        both = dot(jnp.concatenate([base_k[c][0], query_up[c]], axis=0), carry[0], NT)
        reached = both[:BLOCK] + dot(base_k[c][0], carry[1], NT) + dot(base_k[c][1], carry[0], NT)
        updates.append(halves(base_v[c] - reached))
        boths.append(both[BLOCK:])
    for c in every:
        state[c] = fades[c] * state[c] + dot3(updates[c], key_end[c], TN)
    for c in every:
        request, head = divmod(c, heads)
        out = (boths[c] + dot(reaches[c], updates[c][0])) * key_dim ** (-0.5)
        att[request * BLOCK : (request + 1) * BLOCK, head * LANES : (head + 1) * LANES] = (
            out.astype(BF16)
        )

    width = w_ref.shape[1]
    for lane in range(0, width, 768):
        part_ref[0, :, lane : lane + 768] = dot(att[...], w_ref[:, lane : lane + 768]).astype(BF16)

    @pl.when(step == pl.num_programs(0) - 1)
    def _():
        for c in every:
            final_ref[c] = state[c].astype(BF16)


def delta(counts, queries, key_in, value_in, log_decay, update_rate, init_state, w_out):
    length, requests, features = queries.shape
    heads, key_dim, value_dim = init_state.shape[1:]
    chains = requests * heads
    width = w_out.shape[1]

    def rows_of(member):
        member = member.reshape(length, requests, heads, key_dim)
        return member.transpose(0, 2, 1, 3).reshape(length * chains, key_dim)

    def whole(*shape):
        return pl.BlockSpec(shape, lambda n, *_: (0,) * len(shape))

    tall = BLOCK * chains
    block = pl.BlockSpec((tall, key_dim), lambda n, *_: (n, 0))
    steps = length // BLOCK
    return pl.pallas_call(
        delta_kernel,
        grid_spec=pltpu.PrefetchScalarGridSpec(
            num_scalar_prefetch=1,
            grid=(steps,),
            in_specs=[block] * 4
            + [
                whole(chains, length),
                whole(chains, key_dim, value_dim),
                whole(features, width),
            ],
            out_specs=[
                pl.BlockSpec((1, requests * BLOCK, width), lambda n, *_: (n, 0, 0)),
                whole(chains, value_dim, key_dim),
            ],
            scratch_shapes=[
                pltpu.VMEM((chains, value_dim, key_dim), F32),
                pltpu.VMEM((length, chains), F32),
                pltpu.VMEM((tall, key_dim), F32),
                pltpu.VMEM((tall, key_dim), F32),
                pltpu.VMEM((tall, value_dim), F32),
                pltpu.VMEM((requests * BLOCK, features), BF16),
            ],
        ),
        out_shape=[
            jax.ShapeDtypeStruct((steps, requests * BLOCK, width), BF16),
            jax.ShapeDtypeStruct((chains, value_dim, key_dim), BF16),
        ],
        compiler_params=pltpu.CompilerParams(vmem_limit_bytes=40 * MIB),
        name="delta",
    )(
        counts,
        rows_of(queries),
        rows_of(key_in),
        rows_of(value_in),
        rows_of(log_decay),
        update_rate.transpose(1, 2, 0).reshape(chains, length),
        init_state.reshape(chains, key_dim, value_dim),
        w_out,
    )


def expand(table, rows_each):
    count = table.shape[0]
    tall = count * rows_each
    first = iota((tall, count), 1) * rows_each
    row = iota((tall, count), 0)
    pick = jnp.where((row >= first) & (row < first + rows_each), 1.0, 0.0).astype(BF16)
    return dot(pick, table)


def route_kernel(
    res_ref, part_ref, gain_ref, router_ref, ids_ref,
    mixed_ref, slot_ref, weight_ref, out_ref,
    wide, normed,
):
    members, tokens, width = part_ref.shape
    requests = tokens // BLOCK
    chunks = width // LANES
    experts = router_ref.shape[1]
    wide[...] = res_ref[...].astype(F32)
    squares = jnp.zeros((tokens, LANES), F32)
    for chunk in range(chunks):
        lanes = slice(chunk * LANES, (chunk + 1) * LANES)
        total = jnp.concatenate(
            [
                wide[pl.ds(chunk * requests + r, BLOCK, stride=chunks * requests), :]
                for r in range(requests)
            ],
            axis=0,
        )
        for member in range(members):
            total = total + part_ref[member, :, lanes].astype(F32)
        mixed_ref[:, lanes] = total
        squares = squares + total * total
    scale = lax.rsqrt(jnp.sum(squares, axis=-1, keepdims=True) / width + EPSILON)
    for chunk in range(chunks):
        lanes = slice(chunk * LANES, (chunk + 1) * LANES)
        normed[:, lanes] = (mixed_ref[:, lanes] * scale * gain_ref[:, lanes].astype(F32)).astype(
            BF16
        )

    number = iota((experts, tokens), 0)
    chosen = jnp.zeros((experts, tokens), F32)
    for pick in range(ids_ref.shape[0]):
        chosen = chosen + jnp.where(ids_ref[pick : pick + 1, :] == number, 1.0, 0.0)
    row, col = iota((tokens, tokens), 0), iota((tokens, tokens), 1)
    row = (row & (BLOCK - 1)) * requests + (row >> (BLOCK.bit_length() - 1))
    col = (col & (BLOCK - 1)) * requests + (col >> (BLOCK.bit_length() - 1))
    earlier = jnp.where(row < col, 1.0, 0.0).astype(BF16)
    slot = jnp.where(chosen > 0.0, dot(chosen.astype(BF16), earlier), -1.0)
    slot_ref[...] = slot.T

    scores = jax.nn.sigmoid(dot(normed[...], router_ref[...])) * chosen.T
    weight_ref[...] = ROUTE_SCALE * scores / jnp.sum(scores, axis=-1, keepdims=True)

    place = expand(slot.astype(BF16), 8)
    line = iota(place.shape, 0)
    head = jnp.where(place == (line & 7).astype(F32), 1.0, 0.0).astype(BF16)
    tail = place == ((line & 3) + 8).astype(F32)
    tail_a = jnp.where(tail & ((line & 4) == 0), 1.0, 0.0).astype(BF16)
    tail_b = jnp.where(tail & ((line & 4) != 0), 1.0, 0.0).astype(BF16)
    half = width // 2
    step = 3 * LANES
    for lane in range(0, width, step):
        out_ref[:, lane : lane + step] = dot(head, normed[:, lane : lane + step]).astype(BF16)
    for lane in range(0, half, step):
        out_ref[:, width + lane : width + lane + step] = (
            dot(tail_a, normed[:, lane : lane + step])
            + dot(tail_b, normed[:, half + lane : half + lane + step])
        ).astype(BF16)


def interleave(member):
    length, requests, width = member.shape
    member = member.reshape(length, requests, width // LANES, LANES).transpose(0, 2, 1, 3)
    return member.reshape(-1, LANES)


def route(residual, parts, norm_gain, w_router, expert_ids):
    length, requests, width = residual.shape
    tokens = length * requests
    experts = w_router.shape[1]
    ids = expert_ids.transpose(2, 1, 0).reshape(-1, tokens)
    vmem = pl.BlockSpec(memory_space=pltpu.VMEM)
    return pl.pallas_call(
        route_kernel,
        in_specs=[vmem] * 5,
        out_specs=[vmem] * 4,
        scratch_shapes=[
            pltpu.VMEM((tokens * width // LANES, LANES), F32),
            pltpu.VMEM((tokens, width), BF16),
        ],
        out_shape=[
            jax.ShapeDtypeStruct((tokens, width), F32),
            jax.ShapeDtypeStruct((tokens, experts), F32),
            jax.ShapeDtypeStruct((tokens, experts), F32),
            jax.ShapeDtypeStruct((experts * 8, width * 3 // 2), BF16),
        ],
        compiler_params=pltpu.CompilerParams(vmem_limit_bytes=40 * MIB),
        name="route",
    )(interleave(residual), parts, norm_gain.reshape(1, width), w_router, ids)


GROUP = 256


def unpack_rows(dtype=BF16):
    row, col = iota((GROUP, GROUP), 0), iota((GROUP, GROUP), 1)
    half = GROUP // 2
    inside = row & (half - 1)
    source = ((inside >> 2) << 3) + (inside & 3) + jnp.where(row >= half, 4, 0)
    return jnp.where(col == source, 1.0, 0.0).astype(dtype)


def expert_kernel(x_ref, gate_ref, up_ref, down_ref, out_ref, tail_in, tail_out, inner, *, ups):
    step = pl.program_id(0)
    rows, across = x_ref.shape
    width = across * 2 // 3
    half = width // 2
    tails = rows // 2
    fold = gate_ref.shape[1]
    tile = down_ref.shape[1]

    @pl.when(step == 0)
    def _():
        order = unpack_rows()
        for group in range(rows // GROUP):
            moved = dot(order, x_ref[pl.ds(group * GROUP, GROUP), width:]).astype(BF16)
            here = pl.ds(group * GROUP // 2, GROUP // 2)
            tail_in[here, :half] = moved[: GROUP // 2]
            tail_in[here, half:] = moved[GROUP // 2 :]

    @pl.when(step < ups)
    def _():
        def act(lines):
            gate = dot(lines, gate_ref[...])
            up = dot(lines, up_ref[...])
            return (gate / (1.0 + jnp.exp(-gate)) * up).astype(BF16)

        lanes = pl.ds(pl.multiple_of(step * fold, fold), fold)

        @pl.loop(0, rows // GROUP)
        def _(group):
            here = pl.ds(pl.multiple_of(group * GROUP, GROUP), GROUP)
            inner[here, lanes] = act(x_ref[here, :width])

        @pl.loop(0, tails // GROUP)
        def _(group):
            here = pl.ds(pl.multiple_of(group * GROUP, GROUP), GROUP)
            there = pl.ds(pl.multiple_of(rows + group * GROUP, GROUP), GROUP)
            inner[there, lanes] = act(tail_in[here, :])

    @pl.when(step >= ups)
    def _():
        lanes = pl.ds(pl.multiple_of((step - ups) * tile, tile), tile)

        @pl.loop(0, rows // GROUP)
        def _(group):
            here = pl.ds(pl.multiple_of(group * GROUP, GROUP), GROUP)
            out_ref[here, lanes] = dot(inner[here, :], down_ref[...]).astype(BF16)

        @pl.loop(0, tails // GROUP)
        def _(group):
            here = pl.ds(pl.multiple_of(group * GROUP, GROUP), GROUP)
            there = pl.ds(pl.multiple_of(rows + group * GROUP, GROUP), GROUP)
            tail_out[here, lanes] = dot(inner[there, :], down_ref[...]).astype(BF16)

    @pl.when(step == pl.num_programs(0) - 1)
    def _():
        order = unpack_rows()
        for group in range(rows // GROUP):
            here = pl.ds(group * GROUP // 2, GROUP // 2)
            moved = jnp.concatenate([tail_out[here, :half], tail_out[here, half:]], axis=0)
            out_ref[pl.ds(group * GROUP, GROUP), width:] = dot(order, moved, TN).astype(BF16)


def experts_of(arrived, gate, up, down):
    rows, across = arrived.shape
    width, hidden = gate.shape
    fold, tile = 256, 384
    ups, downs = hidden // fold, width // tile
    tails = rows // 2

    def column(step):
        return (0, jnp.minimum(step, ups - 1))

    def later(step):
        return (0, jnp.maximum(step - ups, 0))

    whole = pl.BlockSpec((rows, across), lambda step: (0, 0))
    return pl.pallas_call(
        functools.partial(expert_kernel, ups=ups),
        grid=(ups + downs,),
        in_specs=[
            whole,
            pl.BlockSpec((width, fold), column),
            pl.BlockSpec((width, fold), column),
            pl.BlockSpec((hidden, tile), later),
        ],
        out_specs=whole,
        scratch_shapes=[
            pltpu.VMEM((tails, width), BF16),
            pltpu.VMEM((tails, width), BF16),
            pltpu.VMEM((rows + tails, hidden), BF16),
        ],
        out_shape=jax.ShapeDtypeStruct((rows, across), BF16),
        compiler_params=pltpu.CompilerParams(vmem_limit_bytes=56 * MIB),
        name="experts",
    )(arrived, gate, up, down)


def combine_kernel(
    mixed_ref, slot_ref, weight_ref, head_ref, tail_ref, out_ref, total, heads, tails, wide
):
    step = pl.program_id(0)
    tokens, width = mixed_ref.shape
    rows = head_ref.shape[0]
    requests = tokens // BLOCK
    chunks = width // LANES
    half = width // 2

    @pl.when(step == 0)
    def _():
        total[...] = mixed_ref[...]
        first = iota((slot_ref.shape[1], rows), 0) * 8
        col = iota((slot_ref.shape[1], rows), 1)
        pick = jnp.where((col >= first) & (col < first + 8), 1.0, 0.0).astype(BF16)
        place = dot(slot_ref[...].astype(BF16), pick)
        line = iota(place.shape, 1)
        is_head = place == (line & 7).astype(F32)
        is_tail = place == ((line & 3) + 8).astype(F32)
        for index, part in enumerate(halves(weight_ref[...])):
            spread = dot(part, pick)
            here = slice(index * tokens, (index + 1) * tokens)
            heads[here, :] = jnp.where(is_head, spread, 0.0).astype(BF16)
            tails[0, here, :] = jnp.where(is_tail & ((line & 4) == 0), spread, 0.0).astype(BF16)
            tails[1, here, :] = jnp.where(is_tail & ((line & 4) != 0), spread, 0.0).astype(BF16)

    tile, thin = head_ref.shape[1], tail_ref.shape[1]
    lanes = pl.ds(pl.multiple_of(step * tile, tile), tile)
    both = dot(heads[...], head_ref[...])
    total[:, lanes] += both[:tokens] + both[tokens:]
    for side in range(2):
        lanes = pl.ds(pl.multiple_of(side * half + step * thin, thin), thin)
        both = dot(tails[side], tail_ref[...])
        total[:, lanes] += both[:tokens] + both[tokens:]

    @pl.when(step == pl.num_programs(0) - 1)
    def _():
        for chunk in range(chunks):
            for r in range(requests):
                rows_here = pl.ds(chunk * requests + r, BLOCK, stride=chunks * requests)
                wide[rows_here, :] = total[
                    r * BLOCK : (r + 1) * BLOCK, chunk * LANES : (chunk + 1) * LANES
                ]
        out_ref[...] = wide[...].astype(BF16)


def combine(mixed, slot, weight, back):
    tokens, width = mixed.shape
    rows, across = back.shape
    tile, thin = 256, 128
    steps = width // tile

    def whole(member):
        return pl.BlockSpec(member.shape, lambda step: (0, 0))

    lines = tokens * width // LANES
    return pl.pallas_call(
        combine_kernel,
        grid=(steps,),
        in_specs=[
            whole(mixed),
            whole(slot),
            whole(weight),
            pl.BlockSpec((rows, tile), lambda step: (0, step)),
            pl.BlockSpec((rows, thin), lambda step: (0, width // thin + step)),
        ],
        out_specs=pl.BlockSpec((lines, LANES), lambda step: (0, 0)),
        scratch_shapes=[
            pltpu.VMEM((tokens, width), F32),
            pltpu.VMEM((2 * tokens, rows), BF16),
            pltpu.VMEM((2, 2 * tokens, rows), BF16),
            pltpu.VMEM((lines, LANES), F32),
        ],
        out_shape=jax.ShapeDtypeStruct((lines, LANES), BF16),
        compiler_params=pltpu.CompilerParams(vmem_limit_bytes=40 * MIB),
        name="combine",
    )(mixed, slot, weight, back, back)


def decode(relaid, dec_query, dec_key, dec_value, dec_decay, dec_beta):
    query = dec_query.astype(F32)
    key = dec_key.astype(F32)
    key = key * lax.rsqrt(jnp.sum(key * key, axis=-1, keepdims=True) + EPSILON)
    value = dec_value.astype(F32)
    state = relaid.astype(F32)
    outs = []
    for turn in range(dec_query.shape[1]):
        state = jnp.exp(dec_decay[:, turn])[..., None, :] * state
        guessed = jnp.sum(state * key[:, turn, :, None, :], axis=-1)
        update = dec_beta[:, turn, :, None] * (value[:, turn] - guessed)
        state = state + update[..., None] * key[:, turn, :, None, :]
        outs.append(jnp.sum(state * query[:, turn, :, None, :], axis=-1))
    out = jnp.stack(outs, axis=1) * dec_query.shape[-1] ** (-0.5)
    return out, state.transpose(0, 1, 3, 2)


def shards(
    residual, queries, key_in, value_in, log_decay, update_rate, counts, init_state, w_out,
    norm_gain, w_router, expert_ids, w_gate, w_up, w_down,
    dec_query, dec_key, dec_value, dec_decay, dec_beta,
):
    rows_here, requests, width = residual.shape
    heads, key_dim, value_dim = init_state.shape[1:]
    members = lax.axis_size("exp")
    experts = w_router.shape[1]
    parts, final = delta(
        counts, queries, key_in, value_in, log_decay, update_rate, init_state, w_out
    )
    parts = lax.all_to_all(parts, "exp", split_axis=0, concat_axis=0, tiled=True)
    mixed, slot, weight, outgoing = route(residual, parts, norm_gain, w_router, expert_ids)

    def exchange(member):
        member = member.reshape(experts, 8, -1)
        member = lax.all_to_all(
            member, ("half", "grp", "exp"), split_axis=0, concat_axis=0, tiled=True
        )
        return member.reshape(experts * 8, -1)

    arrived = exchange(outgoing)
    back = exchange(experts_of(arrived, w_gate[0], w_up[0], w_down[0]))

    final = final.reshape(requests, heads, members, value_dim // members, key_dim)
    final = lax.all_to_all(final, "exp", split_axis=2, concat_axis=1, tiled=True)
    final = final.reshape(requests, members * heads, value_dim // members, key_dim)
    relaid = lax.all_to_all(final, "grp", split_axis=1, concat_axis=0, tiled=True)
    dec_out, dec_state = decode(relaid, dec_query, dec_key, dec_value, dec_decay, dec_beta)

    hidden = combine(mixed, slot, weight, back)
    hidden = hidden.reshape(rows_here, width // LANES, requests, LANES).transpose(0, 2, 1, 3)
    return hidden.reshape(rows_here, requests, width), dec_out, dec_state


def solution(mesh):
    return jax.shard_map(
        shards,
        mesh=mesh,
        in_specs=(
            P("exp", ("half", "grp"), None),
            P(None, ("half", "grp"), "exp"),
            P(None, ("half", "grp"), "exp"),
            P(None, ("half", "grp"), "exp"),
            P(None, ("half", "grp"), "exp"),
            P(None, ("half", "grp"), "exp"),
            P(("half", "grp")),
            P(("half", "grp"), "exp", None, None),
            P("exp", None),
            P(),
            P(),
            P("exp", ("half", "grp"), None),
            P(("half", "grp", "exp"), None, None),
            P(("half", "grp", "exp"), None, None),
            P(("half", "grp", "exp"), None, None),
            P("half", None, "grp", None),
            P("half", None, "grp", None),
            P("half", None, "grp", "exp"),
            P("half", None, "grp", None),
            P("half", None, "grp"),
        ),
        out_specs=(
            P("exp", ("half", "grp"), None),
            P("half", None, "grp", "exp"),
            P("half", "grp", None, "exp"),
        ),
        check_vma=False,
    )
```

time: 1080 us -> 430 us (0.40)
  the two profiles are of different devices: /device:TPU:24 before, /device:TPU:7 now
where the time goes in v1:
time: 430 us; the launch traced here: 429 us
  waiting for transfers between devices  279 us (65%)
  Pallas kernels  91.7 us (21%)
  starting transfers between devices  34.1 us (8%)
  local copies, waits for them, and re-layouts  20.1 us (5%)
    all_to_all x2, waiting for transfers between devices, exchange(): lax.all_to_all(member, ('half', 'grp', 'exp'), split_axis=0, concat_axis=...  226 us
    all_to_all x1, waiting for transfers between devices, shards(): lax.all_to_all(parts, 'exp', split_axis=0, concat_axis=0, tiled=True)  53.3 us
    pallas_call x1, Pallas kernels, experts_of(): pl.pallas_call(functools.partial(expert_kernel, ups=ups), grid=(ups + dow...  44.4 us
    pallas_call x1, Pallas kernels, delta(): pl.pallas_call(delta_kernel, grid_spec=pltpu.PrefetchScalarGridSpec(num_s...  31.5 us
    all_to_all x2, starting transfers between devices, exchange(): lax.all_to_all(member, ('half', 'grp', 'exp'), split_axis=0, concat_axis=...  18.1 us
    unnamed x39, local copies, waits for them, and re-layouts  15.9 us
    pallas_call x1, Pallas kernels, combine(): pl.pallas_call(combine_kernel, grid=(steps,), in_specs=[whole(mixed), who...  9.51 us
  transfers between devices with their start and end apart: 5, of which 3 were waited for; matrix products, arithmetic and copies ran while one was open for 2% of the time, Pallas kernels for 12%

profile of v1, /device:TPU:7, one launch (start us, length us, event | category | flops | bytes accessed | tf_op | source)
XLA Modules:
  0.0 428.8 jit_solution(9971411931314760037)
XLA Ops:
  0.6 0.7 reshape.187.rate_ref
  1.4 1.7 copy-done.2
  3.0 1.6 copy-done.3
  4.6 1.2 copy-done.4
  5.8 1.2 copy-done.5
  7.1 1.2 copy-done.6
  8.3 1.0 copy-done.8
  9.3 0.7 copy-done.9
  10.0 31.5 %delta.1 = (bf16[8,128,2304]{2,1,0:T(8,128)(2,1)S(1)}, bf16[8,128,128]{2,1,0:T(8,128)(2,1)S(1)}) custom-call(s32[2]{0:T(128)S(1)} %copy-done.9, bf16[4096,128]{1,0:T(8,128)(2,1)S(1)} %bitcast.187, bf16[4096,128]{1,0:T(8,128)(2,1)S(1)} %bitcast.188, bf16[4096,128]{1,0:T(8,128)(2,1)S(1)} %bitcast.189, f32[4096,128]{1,0:T(8,128)S(1)} %bitcast.186, ...), custom_call_target="tpu_custom_call" | custom-call | tf_op jit(solution)/shard_map/delta/pallas_call | solution.py:151
  41.6 2.2 copy-done.1
  43.7 7.0 %all-to-all-start = ((bf16[8,128,2304]{2,1,0:T(8,128)(2,1)}), bf16[8,128,2304]{2,1,0:T(8,128)(2,1)}, u32[]{:S(2)}, u32[]{:S(2)}) async-start(bf16[8,128,2304]{2,1,0:T(8,128)(2,1)} %copy-done.1), calls=%async_computation | async-start | bytes 9437184 | tf_op jit(solution)/shard_map/all_to_all | solution.py:512
  50.7 0.7 copy.126
  51.5 53.3 %all-to-all-done.part_ref = bf16[8,128,2304]{2,1,0:T(8,128)(2,1)} async-done(((bf16[8,128,2304]{2,1,0:T(8,128)(2,1)}), bf16[8,128,2304]{2,1,0:T(8,128)(2,1)}, u32[]{:S(2)}, u32[]{:S(2)}) %all-to-all-start) | async-done | bytes 4718624 | tf_op jit(solution)/shard_map/all_to_all | solution.py:512
  104.8 5.5 %all-to-all-start.3 = ((bf16[2,4,8,16,128]{4,3,1,0,2:T(8,128)(2,1)}), bf16[2,4,8,16,128]{4,3,1,0,2:T(8,128)(2,1)S(1)}, u32[]{:S(2)}, u32[]{:S(2)}) async-start(bf16[2,4,8,16,128]{4,3,1,0,2:T(8,128)(2,1)} %copy.126), calls=%async_computation.3 | async-start | bytes 524288 | tf_op jit(solution)/shard_map/all_to_all | solution.py:526
  110.3 0.1 copy.117
  110.4 0.3 reshape.177
  110.7 0.6 copy.118
  111.3 0.1 reshape.190.ids_ref
  111.4 6.2 %route.1 = (f32[128,2304]{1,0:T(8,128)S(1)}, f32[128,128]{1,0:T(8,128)S(1)}, f32[128,128]{1,0:T(8,128)S(1)}, bf16[1024,3456]{1,0:T(8,128)(2,1)S(1)}) custom-call(bf16[2304,128]{1,0:T(8,128)(2,1)S(1)} %bitcast.185, bf16[8,128,2304]{2,1,0:T(8,128)(2,1)} %all-to-all-done.part_ref, bf16[1,2304]{1,0:T(2,128)(2,1)S(1)} %reshape.189.gain_ref, ...), custom_call_target="tpu_custom_call" | custom-call | tf_op jit(solution)/shard_map/route/pallas_call | solution.py:276
  117.6 2.9 copy-done
  120.6 11.4 %all-to-all-start.1 = ((bf16[128,8,3456]{2,1,0:T(8,128)(2,1)}), bf16[128,8,3456]{2,1,0:T(8,128)(2,1)}, u32[]{:S(2)}, u32[]{:S(2)}) async-start(bf16[128,8,3456]{2,1,0:T(8,128)(2,1)} %bitcast.183), calls=%async_computation.1 | async-start | bytes 14155776 | tf_op jit(solution)/shard_map/all_to_all | solution.py:517
  132.0 0.7 copy.128
  132.7 114.6 %all-to-all-done.1 = bf16[128,8,3456]{2,1,0:T(8,128)(2,1)} async-done(((bf16[128,8,3456]{2,1,0:T(8,128)(2,1)}), bf16[128,8,3456]{2,1,0:T(8,128)(2,1)}, u32[]{:S(2)}, u32[]{:S(2)}) %all-to-all-start.1) | async-done | bytes 7077920 | tf_op jit(solution)/shard_map/all_to_all | solution.py:517
  247.3 3.5 all-to-all-start.4
  250.9 44.4 %experts.1 = bf16[1024,3456]{1,0:T(8,128)(2,1)} custom-call(bf16[1024,3456]{1,0:T(8,128)(2,1)} %bitcast.18.x_ref, bf16[2304,1024]{1,0:T(8,128)(2,1)} %bitcast.197, bf16[2304,1024]{1,0:T(8,128)(2,1)} %bitcast.198, bf16[1024,2304]{1,0:T(8,128)(2,1)} %bitcast.199), custom_call_target="tpu_custom_call" | custom-call | tf_op jit(solution)/shard_map/experts/pallas_call | solution.py:382
  295.3 0.0 copy-start.12
  295.3 0.0 copy-start.13
  295.3 0.0 copy-start.14
  295.3 6.7 %all-to-all-start.2 = ((bf16[128,8,3456]{2,1,0:T(8,128)(2,1)}), bf16[128,8,3456]{2,1,0:T(8,128)(2,1)}, u32[]{:S(2)}, u32[]{:S(2)}) async-start(bf16[128,8,3456]{2,1,0:T(8,128)(2,1)} %bitcast.192), calls=%async_computation.2 | async-start | bytes 14155776 | tf_op jit(solution)/shard_map/all_to_all | solution.py:517
  302.1 0.1 copy.130
  302.2 0.1 copy.137
  302.3 0.1 copy.144
  302.4 0.1 copy.146
  302.4 0.1 fusion.3
  302.6 0.1 convert_multiply_fusion
  302.8 0.2 multiply_reduce_fusion.3
  303.1 0.1 fusion.7
  303.2 0.5 multiply_reduce_fusion.1
  303.6 0.1 fusion.6
  303.7 0.7 multiply_reduce_fusion.2
  304.5 0.7 copy.149
  305.3 0.1 fusion.5
  305.4 1.1 fusion.2
  306.5 110.9 %all-to-all-done.2 = bf16[128,8,3456]{2,1,0:T(8,128)(2,1)} async-done(((bf16[128,8,3456]{2,1,0:T(8,128)(2,1)}), bf16[128,8,3456]{2,1,0:T(8,128)(2,1)}, u32[]{:S(2)}, u32[]{:S(2)}) %all-to-all-start.2) | async-done | bytes 7077920 | tf_op jit(solution)/shard_map/all_to_all | solution.py:517
  417.4 9.5 %combine.1 = bf16[2304,128]{1,0:T(8,128)(2,1)S(1)} custom-call(f32[128,2304]{1,0:T(8,128)S(1)} %get-tuple-element.10.mixed_ref, f32[128,128]{1,0:T(8,128)S(1)} %get-tuple-element.11.slot_ref, f32[128,128]{1,0:T(8,128)S(1)} %get-tuple-element.12.weight_ref, bf16[1024,3456]{1,0:T(8,128)(2,1)} %bitcast.23.head_ref.tail_ref, ...), custom_call_target="tpu_custom_call" | custom-call | tf_op jit(solution)/shard_map/combine/pallas_call | solution.py:460
  426.9 0.1 copy.181
  427.1 0.3 reshape.196
  427.4 1.4 copy.148
  (45 shorter events, 0.4 us)
Async XLA Ops:
  1.4 1.7 copy-start.2
  3.0 1.6 copy-start.3
  4.6 1.2 copy-start.4
  5.8 1.2 copy-start.5
  7.1 1.2 copy-start.6
  8.3 1.0 copy-start.8
  9.3 0.7 copy-start.9
  41.5 2.2 copy-start.1
  43.7 66.6 %copy-start.10 = (bf16[64,2,2304]{2,1,0:T(2,128)(2,1)S(1)}, bf16[64,2,2304]{2,1,0:T(2,128)(2,1)}, u32[]{:S(2)}) copy-start(bf16[64,2,2304]{2,1,0:T(2,128)(2,1)} %param.20) | copy-start | bytes 1769476
  43.7 61.1 %all-to-all-start = ((bf16[8,128,2304]{2,1,0:T(8,128)(2,1)}), bf16[8,128,2304]{2,1,0:T(8,128)(2,1)}, u32[]{:S(2)}, u32[]{:S(2)}) async-start(bf16[8,128,2304]{2,1,0:T(8,128)(2,1)} %copy-done.1), calls=%async_computation | async-start | bytes 9437184 | tf_op jit(solution)/shard_map/all_to_all | solution.py:512
  50.7 60.6 %copy-start.16 = (bf16[2304]{0:T(1024)(128)(2,1)S(1)}, bf16[2304]{0:T(1024)(128)(2,1)}, u32[]{:S(2)}) copy-start(bf16[2304]{0:T(1024)(128)(2,1)} %param.29) | copy-start | bytes 13828
  50.7 60.6 %copy-start.15 = (s32[64,2,8]{0,2,1:T(8,128)S(1)}, s32[64,2,8]{0,2,1:T(8,128)}, u32[]{:S(2)}) copy-start(s32[64,2,8]{0,2,1:T(8,128)} %param.31) | copy-start | bytes 12292
  50.7 60.7 %copy-start.7 = (bf16[2304,128]{1,0:T(8,128)(2,1)S(1)}, bf16[2304,128]{1,0:T(8,128)(2,1)}, u32[]{:S(2)}) copy-start(bf16[2304,128]{1,0:T(8,128)(2,1)} %router_ref.1) | copy-start | bytes 1769476
  104.8 15.8 %all-to-all-start.3 = ((bf16[2,4,8,16,128]{4,3,1,0,2:T(8,128)(2,1)}), bf16[2,4,8,16,128]{4,3,1,0,2:T(8,128)(2,1)S(1)}, u32[]{:S(2)}, u32[]{:S(2)}) async-start(bf16[2,4,8,16,128]{4,3,1,0,2:T(8,128)(2,1)} %copy.126), calls=%async_computation.3 | async-start | bytes 524288 | tf_op jit(solution)/shard_map/all_to_all | solution.py:526
  117.6 2.9 copy-start
  120.6 126.7 %all-to-all-start.1 = ((bf16[128,8,3456]{2,1,0:T(8,128)(2,1)}), bf16[128,8,3456]{2,1,0:T(8,128)(2,1)}, u32[]{:S(2)}, u32[]{:S(2)}) async-start(bf16[128,8,3456]{2,1,0:T(8,128)(2,1)} %bitcast.183), calls=%async_computation.1 | async-start | bytes 14155776 | tf_op jit(solution)/shard_map/all_to_all | solution.py:517
  247.3 48.0 %all-to-all-start.4 = ((bf16[2,32,16,128]{3,2,0,1:T(8,128)(2,1)}), bf16[2,32,16,128]{3,2,0,1:T(8,128)(2,1)S(1)}, u32[]{:S(2)}, u32[]{:S(2)}) async-start(bf16[2,32,16,128]{3,2,0,1:T(8,128)(2,1)} %copy.128), calls=%async_computation.4 | async-start | bytes 524288 | tf_op jit(solution)/shard_map/all_to_all | solution.py:528
  295.3 6.8 %copy-start.17 = (f32[16,2,4]{0,2,1:T(4,128)S(1)}, f32[16,2,4]{0,2,1:T(4,128)}, u32[]{:S(2)}) copy-start(f32[16,2,4]{0,2,1:T(4,128)} %param.39) | copy-start | bytes 1540
  295.3 7.1 %copy-start.11 = (bf16[16,2,4,16]{3,2,1,0:T(4,128)(2,1)S(1)}, bf16[16,2,4,16]{3,2,1,0:T(4,128)(2,1)}, u32[]{:S(2)}) copy-start(bf16[16,2,4,16]{3,2,1,0:T(4,128)(2,1)} %param.37) | copy-start | bytes 12292
  295.3 7.2 %copy-start.12 = (bf16[16,2,4,128]{3,2,1,0:T(4,128)(2,1)S(1)}, bf16[16,2,4,128]{3,2,1,0:T(4,128)(2,1)}, u32[]{:S(2)}) copy-start(bf16[16,2,4,128]{3,2,1,0:T(4,128)(2,1)} %param.36) | copy-start | bytes 98308
  295.3 7.3 %copy-start.13 = (bf16[16,2,4,128]{3,2,1,0:T(4,128)(2,1)S(1)}, bf16[16,2,4,128]{3,2,1,0:T(4,128)(2,1)}, u32[]{:S(2)}) copy-start(bf16[16,2,4,128]{3,2,1,0:T(4,128)(2,1)} %param.35) | copy-start | bytes 98308
  295.3 7.4 %copy-start.14 = (f32[16,2,4,128]{3,2,1,0:T(4,128)S(1)}, f32[16,2,4,128]{3,2,1,0:T(4,128)}, u32[]{:S(2)}) copy-start(f32[16,2,4,128]{3,2,1,0:T(4,128)} %param.38) | copy-start | bytes 196612
  295.3 122.1 %all-to-all-start.2 = ((bf16[128,8,3456]{2,1,0:T(8,128)(2,1)}), bf16[128,8,3456]{2,1,0:T(8,128)(2,1)}, u32[]{:S(2)}, u32[]{:S(2)}) async-start(bf16[128,8,3456]{2,1,0:T(8,128)(2,1)} %bitcast.192), calls=%async_computation.2 | async-start | bytes 14155776 | tf_op jit(solution)/shard_map/all_to_all | solution.py:517

commit v2 on v1

--- a/solution.py
+++ b/solution.py
@@ -11,7 +11,7 @@
 ROUTE_SCALE = 2.446
 LANES = 128
 BLOCK = 64
-MIB = 1 << 20
+VMEM = 60 << 20
 F32 = jnp.float32
 BF16 = jnp.bfloat16
 
@@ -128,11 +128,15 @@
 
     @pl.when(step == pl.num_programs(0) - 1)
     def _():
+        columns = final_ref.shape[1] // chains
         for c in every:
-            final_ref[c] = state[c].astype(BF16)
-
-
-def delta(counts, queries, key_in, value_in, log_decay, update_rate, init_state, w_out):
+            for member in range(final_ref.shape[0]):
+                final_ref[member, c * columns : (c + 1) * columns, :] = state[
+                    c, member * columns : (member + 1) * columns, :
+                ].astype(BF16)
+
+
+def delta(counts, queries, key_in, value_in, log_decay, update_rate, init_state, w_out, members):
     length, requests, features = queries.shape
     heads, key_dim, value_dim = init_state.shape[1:]
     chains = requests * heads
@@ -161,7 +165,7 @@
             ],
             out_specs=[
                 pl.BlockSpec((1, requests * BLOCK, width), lambda n, *_: (n, 0, 0)),
-                whole(chains, value_dim, key_dim),
+                whole(members, chains * value_dim // members, key_dim),
             ],
             scratch_shapes=[
                 pltpu.VMEM((chains, value_dim, key_dim), F32),
@@ -174,9 +178,9 @@
         ),
         out_shape=[
             jax.ShapeDtypeStruct((steps, requests * BLOCK, width), BF16),
-            jax.ShapeDtypeStruct((chains, value_dim, key_dim), BF16),
-        ],
-        compiler_params=pltpu.CompilerParams(vmem_limit_bytes=40 * MIB),
+            jax.ShapeDtypeStruct((members, chains * value_dim // members, key_dim), BF16),
+        ],
+        compiler_params=pltpu.CompilerParams(vmem_limit_bytes=VMEM),
         name="delta",
     )(
         counts,
@@ -190,13 +194,15 @@
     )
 
 
-def expand(table, rows_each):
-    count = table.shape[0]
-    tall = count * rows_each
-    first = iota((tall, count), 1) * rows_each
-    row = iota((tall, count), 0)
-    pick = jnp.where((row >= first) & (row < first + rows_each), 1.0, 0.0).astype(BF16)
-    return dot(pick, table)
+def place_of(expert):
+    return ((expert & 7) << 4) + (((expert >> 3) & 7) << 1) + (expert >> 6)
+
+
+def picker(experts, rows, dim):
+    shape = (experts, rows) if dim == 0 else (rows, experts)
+    first = place_of(iota(shape, dim)) * 8
+    row = iota(shape, 1 - dim)
+    return jnp.where((row >= first) & (row < first + 8), 1.0, 0.0).astype(BF16)
 
 
 def route_kernel(
@@ -244,16 +250,17 @@
     scores = jax.nn.sigmoid(dot(normed[...], router_ref[...])) * chosen.T
     weight_ref[...] = ROUTE_SCALE * scores / jnp.sum(scores, axis=-1, keepdims=True)
 
-    place = expand(slot.astype(BF16), 8)
+    place = dot(picker(experts, experts * 8, 1), slot.astype(BF16))
     line = iota(place.shape, 0)
     head = jnp.where(place == (line & 7).astype(F32), 1.0, 0.0).astype(BF16)
     tail = place == ((line & 3) + 8).astype(F32)
     tail_a = jnp.where(tail & ((line & 4) == 0), 1.0, 0.0).astype(BF16)
     tail_b = jnp.where(tail & ((line & 4) != 0), 1.0, 0.0).astype(BF16)
     half = width // 2
-    step = 3 * LANES
+    step = 6 * LANES
     for lane in range(0, width, step):
         out_ref[:, lane : lane + step] = dot(head, normed[:, lane : lane + step]).astype(BF16)
+    step = 3 * LANES
     for lane in range(0, half, step):
         out_ref[:, width + lane : width + lane + step] = (
             dot(tail_a, normed[:, lane : lane + step])
@@ -287,7 +294,7 @@
             jax.ShapeDtypeStruct((tokens, experts), F32),
             jax.ShapeDtypeStruct((experts * 8, width * 3 // 2), BF16),
         ],
-        compiler_params=pltpu.CompilerParams(vmem_limit_bytes=40 * MIB),
+        compiler_params=pltpu.CompilerParams(vmem_limit_bytes=VMEM),
         name="route",
     )(interleave(residual), parts, norm_gain.reshape(1, width), w_router, ids)
 
@@ -323,38 +330,25 @@
 
     @pl.when(step < ups)
     def _():
-        def act(lines):
+        lanes = pl.ds(pl.multiple_of(step * fold, fold), fold)
+        for start in range(0, rows + tails, 256):
+            if start < rows:
+                lines = x_ref[start : start + 256, :width]
+            else:
+                lines = tail_in[start - rows : start - rows + 256, :]
             gate = dot(lines, gate_ref[...])
             up = dot(lines, up_ref[...])
-            return (gate / (1.0 + jnp.exp(-gate)) * up).astype(BF16)
-
-        lanes = pl.ds(pl.multiple_of(step * fold, fold), fold)
-
-        @pl.loop(0, rows // GROUP)
-        def _(group):
-            here = pl.ds(pl.multiple_of(group * GROUP, GROUP), GROUP)
-            inner[here, lanes] = act(x_ref[here, :width])
-
-        @pl.loop(0, tails // GROUP)
-        def _(group):
-            here = pl.ds(pl.multiple_of(group * GROUP, GROUP), GROUP)
-            there = pl.ds(pl.multiple_of(rows + group * GROUP, GROUP), GROUP)
-            inner[there, lanes] = act(tail_in[here, :])
+            inner[start : start + 256, lanes] = (gate / (1.0 + jnp.exp(-gate)) * up).astype(BF16)
 
     @pl.when(step >= ups)
     def _():
         lanes = pl.ds(pl.multiple_of((step - ups) * tile, tile), tile)
-
-        @pl.loop(0, rows // GROUP)
-        def _(group):
-            here = pl.ds(pl.multiple_of(group * GROUP, GROUP), GROUP)
-            out_ref[here, lanes] = dot(inner[here, :], down_ref[...]).astype(BF16)
-
-        @pl.loop(0, tails // GROUP)
-        def _(group):
-            here = pl.ds(pl.multiple_of(group * GROUP, GROUP), GROUP)
-            there = pl.ds(pl.multiple_of(rows + group * GROUP, GROUP), GROUP)
-            tail_out[here, lanes] = dot(inner[there, :], down_ref[...]).astype(BF16)
+        for start in range(0, rows + tails, 256):
+            result = dot(inner[start : start + 256, :], down_ref[...]).astype(BF16)
+            if start < rows:
+                out_ref[start : start + 256, lanes] = result
+            else:
+                tail_out[start - rows : start - rows + 256, lanes] = result
 
     @pl.when(step == pl.num_programs(0) - 1)
     def _():
@@ -368,7 +362,7 @@
 def experts_of(arrived, gate, up, down):
     rows, across = arrived.shape
     width, hidden = gate.shape
-    fold, tile = 256, 384
+    fold, tile = 256, 768
     ups, downs = hidden // fold, width // tile
     tails = rows // 2
 
@@ -395,17 +389,46 @@
             pltpu.VMEM((rows + tails, hidden), BF16),
         ],
         out_shape=jax.ShapeDtypeStruct((rows, across), BF16),
-        compiler_params=pltpu.CompilerParams(vmem_limit_bytes=56 * MIB),
+        compiler_params=pltpu.CompilerParams(vmem_limit_bytes=VMEM),
         name="experts",
     )(arrived, gate, up, down)
 
 
-def combine_kernel(
-    mixed_ref, slot_ref, weight_ref, head_ref, tail_ref, out_ref, total, heads, tails, wide
-):
+def spread_kernel(slot_ref, weight_ref, heads, tails):
+    tokens, experts = slot_ref.shape
+    pick = picker(experts, heads.shape[1], 0)
+    place = dot(slot_ref[...].astype(BF16), pick)
+    line = iota(place.shape, 1)
+    is_head = place == (line & 7).astype(F32)
+    is_tail = place == ((line & 3) + 8).astype(F32)
+    for index, part in enumerate(halves(weight_ref[...])):
+        spread = dot(part, pick)
+        here = slice(index * tokens, (index + 1) * tokens)
+        heads[here, :] = jnp.where(is_head, spread, 0.0).astype(BF16)
+        tails[0, here, :] = jnp.where(is_tail & ((line & 4) == 0), spread, 0.0).astype(BF16)
+        tails[1, here, :] = jnp.where(is_tail & ((line & 4) != 0), spread, 0.0).astype(BF16)
+
+
+def spread_of(slot, weight):
+    tokens, experts = slot.shape
+    rows = experts * 8
+    vmem = pl.BlockSpec(memory_space=pltpu.VMEM)
+    return pl.pallas_call(
+        spread_kernel,
+        in_specs=[vmem] * 2,
+        out_specs=[vmem] * 2,
+        out_shape=[
+            jax.ShapeDtypeStruct((2 * tokens, rows), BF16),
+            jax.ShapeDtypeStruct((2, 2 * tokens, rows), BF16),
+        ],
+        compiler_params=pltpu.CompilerParams(vmem_limit_bytes=VMEM),
+        name="spread",
+    )(slot, weight)
+
+
+def combine_kernel(mixed_ref, heads, tails, head_ref, tail_ref, out_ref, total, wide):
     step = pl.program_id(0)
     tokens, width = mixed_ref.shape
-    rows = head_ref.shape[0]
     requests = tokens // BLOCK
     chunks = width // LANES
     half = width // 2
@@ -413,19 +436,6 @@
     @pl.when(step == 0)
     def _():
         total[...] = mixed_ref[...]
-        first = iota((slot_ref.shape[1], rows), 0) * 8
-        col = iota((slot_ref.shape[1], rows), 1)
-        pick = jnp.where((col >= first) & (col < first + 8), 1.0, 0.0).astype(BF16)
-        place = dot(slot_ref[...].astype(BF16), pick)
-        line = iota(place.shape, 1)
-        is_head = place == (line & 7).astype(F32)
-        is_tail = place == ((line & 3) + 8).astype(F32)
-        for index, part in enumerate(halves(weight_ref[...])):
-            spread = dot(part, pick)
-            here = slice(index * tokens, (index + 1) * tokens)
-            heads[here, :] = jnp.where(is_head, spread, 0.0).astype(BF16)
-            tails[0, here, :] = jnp.where(is_tail & ((line & 4) == 0), spread, 0.0).astype(BF16)
-            tails[1, here, :] = jnp.where(is_tail & ((line & 4) != 0), spread, 0.0).astype(BF16)
 
     tile, thin = head_ref.shape[1], tail_ref.shape[1]
     lanes = pl.ds(pl.multiple_of(step * tile, tile), tile)
@@ -447,14 +457,14 @@
         out_ref[...] = wide[...].astype(BF16)
 
 
-def combine(mixed, slot, weight, back):
+def combine(mixed, heads, tails, back):
     tokens, width = mixed.shape
     rows, across = back.shape
     tile, thin = 256, 128
     steps = width // tile
 
     def whole(member):
-        return pl.BlockSpec(member.shape, lambda step: (0, 0))
+        return pl.BlockSpec(member.shape, lambda step: (0,) * member.ndim)
 
     lines = tokens * width // LANES
     return pl.pallas_call(
@@ -462,22 +472,20 @@
         grid=(steps,),
         in_specs=[
             whole(mixed),
-            whole(slot),
-            whole(weight),
+            whole(heads),
+            whole(tails),
             pl.BlockSpec((rows, tile), lambda step: (0, step)),
             pl.BlockSpec((rows, thin), lambda step: (0, width // thin + step)),
         ],
         out_specs=pl.BlockSpec((lines, LANES), lambda step: (0, 0)),
         scratch_shapes=[
             pltpu.VMEM((tokens, width), F32),
-            pltpu.VMEM((2 * tokens, rows), BF16),
-            pltpu.VMEM((2, 2 * tokens, rows), BF16),
             pltpu.VMEM((lines, LANES), F32),
         ],
         out_shape=jax.ShapeDtypeStruct((lines, LANES), BF16),
-        compiler_params=pltpu.CompilerParams(vmem_limit_bytes=40 * MIB),
+        compiler_params=pltpu.CompilerParams(vmem_limit_bytes=VMEM),
         name="combine",
-    )(mixed, slot, weight, back, back)
+    )(mixed, heads, tails, back, back)
 
 
 def decode(relaid, dec_query, dec_key, dec_value, dec_decay, dec_beta):
@@ -506,8 +514,14 @@
     heads, key_dim, value_dim = init_state.shape[1:]
     members = lax.axis_size("exp")
     experts = w_router.shape[1]
+    groups = lax.axis_size("grp")
     parts, final = delta(
-        counts, queries, key_in, value_in, log_decay, update_rate, init_state, w_out
+        counts, queries, key_in, value_in, log_decay, update_rate, init_state, w_out, members
+    )
+    final = lax.ppermute(
+        final,
+        ("grp", "exp"),
+        [(g * members + e, e * members + g) for g in range(groups) for e in range(members)],
     )
     parts = lax.all_to_all(parts, "exp", split_axis=0, concat_axis=0, tiled=True)
     mixed, slot, weight, outgoing = route(residual, parts, norm_gain, w_router, expert_ids)
@@ -515,20 +529,19 @@
     def exchange(member):
         member = member.reshape(experts, 8, -1)
         member = lax.all_to_all(
-            member, ("half", "grp", "exp"), split_axis=0, concat_axis=0, tiled=True
+            member, ("exp", "grp", "half"), split_axis=0, concat_axis=0, tiled=True
         )
         return member.reshape(experts * 8, -1)
 
     arrived = exchange(outgoing)
+    heads_of, tails_of = spread_of(slot, weight)
     back = exchange(experts_of(arrived, w_gate[0], w_up[0], w_down[0]))
 
-    final = final.reshape(requests, heads, members, value_dim // members, key_dim)
-    final = lax.all_to_all(final, "exp", split_axis=2, concat_axis=1, tiled=True)
-    final = final.reshape(requests, members * heads, value_dim // members, key_dim)
-    relaid = lax.all_to_all(final, "grp", split_axis=1, concat_axis=0, tiled=True)
+    relaid = lax.all_to_all(final, "exp", split_axis=0, concat_axis=0, tiled=True)
+    relaid = relaid.reshape(groups * requests, heads, value_dim // members, key_dim)
     dec_out, dec_state = decode(relaid, dec_query, dec_key, dec_value, dec_decay, dec_beta)
 
-    hidden = combine(mixed, slot, weight, back)
+    hidden = combine(mixed, heads_of, tails_of, back)
     hidden = hidden.reshape(rows_here, width // LANES, requests, LANES).transpose(0, 2, 1, 3)
     return hidden.reshape(rows_here, requests, width), dec_out, dec_state
 

time: 430 us -> 363 us (0.84)
  the two profiles are of different devices: /device:TPU:7 before, /device:TPU:24 now
where the time goes in v2:
time: 363 us; the launch traced here: 362 us
  waiting for transfers between devices  218 us (60%)
  Pallas kernels  90.5 us (25%)
  starting transfers between devices  40.2 us (11%)
  local copies, waits for them, and re-layouts  8.65 us (2%)
    ppermute x1, waiting for transfers between devices, shards(): lax.ppermute(final, ('grp', 'exp'), [(g * members + e, e * members + g) f...  86.8 us
    all_to_all x2, waiting for transfers between devices, exchange(): lax.all_to_all(member, ('exp', 'grp', 'half'), split_axis=0, concat_axis=...  80 us
    all_to_all x1, waiting for transfers between devices, shards(): lax.all_to_all(parts, 'exp', split_axis=0, concat_axis=0, tiled=True)  51.3 us
    pallas_call x1, Pallas kernels, delta(): pl.pallas_call(delta_kernel, grid_spec=pltpu.PrefetchScalarGridSpec(num_s...  35.2 us
    pallas_call x1, Pallas kernels, experts_of(): pl.pallas_call(functools.partial(expert_kernel, ups=ups), grid=(ups + dow...  32.8 us
    all_to_all x2, starting transfers between devices, exchange(): lax.all_to_all(member, ('exp', 'grp', 'half'), split_axis=0, concat_axis=...  17.1 us
    all_to_all x1, starting transfers between devices, shards(): lax.all_to_all(final, 'exp', split_axis=0, concat_axis=0, tiled=True)  10.6 us
    pallas_call x1, Pallas kernels, combine(): pl.pallas_call(combine_kernel, grid=(steps,), in_specs=[whole(mixed), who...  10.5 us
  transfers between devices with their start and end apart: 5, of which 3 were waited for; matrix products, arithmetic and copies ran while one was open for 2% of the time, Pallas kernels for 10%

profile of v2, /device:TPU:24, one launch (start us, length us, event | category | flops | bytes accessed | tf_op | source)
XLA Modules:
  0.0 361.8 jit_solution(2059408623675700491)
XLA Ops:
  0.6 1.3 reshape.157.rate_ref
  2.0 35.2 %delta.1 = (bf16[8,128,2304]{2,1,0:T(8,128)(2,1)}, bf16[8,128,128]{2,1,0:T(8,128)(2,1)}) custom-call(s32[2]{0:T(128)} %counts.1, bf16[4096,128]{1,0:T(8,128)(2,1)} %bitcast.94, bf16[4096,128]{1,0:T(8,128)(2,1)} %bitcast.95, bf16[4096,128]{1,0:T(8,128)(2,1)} %bitcast.96, f32[4096,128]{1,0:T(8,128)} %bitcast.93, f32[8,512]{1,0:T(8,128)} %reshape.157.rate_ref, ...), custom_call_target="tpu_custom_call" | custom-call | tf_op jit(solution)/shard_map/delta/pallas_call | solution.py:155
  37.2 0.0 copy-start.6
  37.2 0.0 copy-start
  37.2 7.3 %all-to-all-start = ((bf16[8,128,2304]{2,1,0:T(8,128)(2,1)}), bf16[8,128,2304]{2,1,0:T(8,128)(2,1)}, u32[]{:S(2)}, u32[]{:S(2)}) async-start(bf16[8,128,2304]{2,1,0:T(8,128)(2,1)} %get-tuple-element.11), calls=%async_computation | async-start | bytes 9437184 | tf_op jit(solution)/shard_map/all_to_all | solution.py:526
  44.5 0.7 reshape.160.ids_ref
  45.2 0.6 reshape.159.gain_ref
  45.8 0.1 copy.32
  45.9 0.3 reshape.147
  46.2 1.4 copy.33
  47.6 51.3 %all-to-all-done.part_ref = bf16[8,128,2304]{2,1,0:T(8,128)(2,1)} async-done(((bf16[8,128,2304]{2,1,0:T(8,128)(2,1)}), bf16[8,128,2304]{2,1,0:T(8,128)(2,1)}, u32[]{:S(2)}, u32[]{:S(2)}) %all-to-all-start) | async-done | bytes 4718624 | tf_op jit(solution)/shard_map/all_to_all | solution.py:526
  98.9 9.3 %route.1 = (f32[128,2304]{1,0:T(8,128)}, f32[128,128]{1,0:T(8,128)}, f32[128,128]{1,0:T(8,128)}, bf16[1024,3456]{1,0:T(8,128)(2,1)}) custom-call(bf16[2304,128]{1,0:T(8,128)(2,1)} %bitcast.89, bf16[8,128,2304]{2,1,0:T(8,128)(2,1)} %all-to-all-done.part_ref, bf16[1,2304]{1,0:T(2,128)(2,1)} %reshape.159.gain_ref, bf16[2304,128]{1,0:T(8,128)(2,1)} %router_ref.1, ...), custom_call_target="tpu_custom_call" | custom-call | tf_op jit(solution)/shard_map/route/pallas_call | solution.py:283
  108.2 8.5 %all-to-all-start.1 = ((bf16[128,8,3456]{2,1,0:T(8,128)(2,1)}), bf16[128,8,3456]{2,1,0:T(8,128)(2,1)}, u32[]{:S(2)}, u32[]{:S(2)}) async-start(bf16[128,8,3456]{2,1,0:T(8,128)(2,1)} %bitcast.75), calls=%async_computation.1 | async-start | bytes 14155776 | tf_op jit(solution)/shard_map/all_to_all | solution.py:531
  116.7 5.2 %collective-permute-start = (bf16[8,128,128]{2,1,0:T(8,128)(2,1)S(1)}, bf16[8,128,128]{2,1,0:T(8,128)(2,1)}, u32[]{:S(2)}, u32[]{:S(2)}) collective-permute-start(bf16[8,128,128]{2,1,0:T(8,128)(2,1)S(1)} %copy-done.8), channel_id=1, source_target_pairs={{0,0},{1,8},{2,16},{3,24},{4,32},{5,40},{6,48},{7,56},{8,1},{9,9},... | collective-permute-start | bytes 786440 | tf_op jit(solution)/shard_map/ppermute | solution.py:521
  121.9 86.8 %collective-permute-done = bf16[8,128,128]{2,1,0:T(8,128)(2,1)} collective-permute-done((bf16[8,128,128]{2,1,0:T(8,128)(2,1)S(1)}, bf16[8,128,128]{2,1,0:T(8,128)(2,1)}, u32[]{:S(2)}, u32[]{:S(2)}) %collective-permute-start) | collective-permute-done | bytes 262176 | tf_op jit(solution)/shard_map/ppermute | solution.py:521
  208.7 0.0 all-to-all-done.1
  208.8 10.6 %all-to-all-start.3 = ((bf16[8,128,128]{2,1,0:T(8,128)(2,1)}), bf16[8,128,128]{2,1,0:T(8,128)(2,1)S(1)}, u32[]{:S(2)}, u32[]{:S(2)}) async-start(bf16[8,128,128]{2,1,0:T(8,128)(2,1)} %collective-permute-done), calls=%async_computation.3 | async-start | bytes 524288 | tf_op jit(solution)/shard_map/all_to_all | solution.py:540
  219.4 32.8 %experts.1 = bf16[1024,3456]{1,0:T(8,128)(2,1)} custom-call(bf16[1024,3456]{1,0:T(8,128)(2,1)} %bitcast.18.x_ref, bf16[2304,1024]{1,0:T(8,128)(2,1)} %bitcast.76, bf16[2304,1024]{1,0:T(8,128)(2,1)} %bitcast.77, bf16[1024,2304]{1,0:T(8,128)(2,1)} %bitcast.78), custom_call_target="tpu_custom_call" | custom-call | tf_op jit(solution)/shard_map/experts/pallas_call | solution.py:376
  252.2 0.0 copy-start.1
  252.2 0.0 copy-start.2
  252.2 0.0 copy-start.3
  252.2 8.6 %all-to-all-start.2 = ((bf16[128,8,3456]{2,1,0:T(8,128)(2,1)}), bf16[128,8,3456]{2,1,0:T(8,128)(2,1)}, u32[]{:S(2)}, u32[]{:S(2)}) async-start(bf16[128,8,3456]{2,1,0:T(8,128)(2,1)} %bitcast.74), calls=%async_computation.2 | async-start | bytes 14155776 | tf_op jit(solution)/shard_map/all_to_all | solution.py:531
  260.8 0.1 copy.41
  260.9 0.1 copy.40
  261.0 0.1 mul.175
  261.1 0.1 mul.176
  261.2 0.1 mul.195
  261.3 0.1 mul.196
  261.4 0.1 squeeze.25
  261.5 0.1 squeeze.24
  261.6 0.1 fusion.1
  261.8 0.1 convert_multiply_fusion.1
  262.0 0.2 multiply_reduce_fusion.3
  262.2 0.1 reduce_sum.54
  262.5 0.6 multiply_reduce_fusion.1
  263.1 0.1 reduce_sum.55
  263.2 0.4 multiply_reduce_fusion
  263.6 0.1 stack.10
  263.7 0.1 stack.9
  263.8 0.7 maximum_multiply_fusion
  264.5 0.1 fusion.3
  264.6 1.1 add_bitcast_fusion
  265.7 2.7 spread.1
  268.4 80.0 %all-to-all-done.2 = bf16[128,8,3456]{2,1,0:T(8,128)(2,1)} async-done(((bf16[128,8,3456]{2,1,0:T(8,128)(2,1)}), bf16[128,8,3456]{2,1,0:T(8,128)(2,1)}, u32[]{:S(2)}, u32[]{:S(2)}) %all-to-all-start.2) | async-done | bytes 7077920 | tf_op jit(solution)/shard_map/all_to_all | solution.py:531
  348.4 10.5 %combine.1 = bf16[2304,128]{1,0:T(8,128)(2,1)} custom-call(f32[128,2304]{1,0:T(8,128)} %get-tuple-element.12.mixed_ref, bf16[256,1024]{1,0:T(8,128)(2,1)} %get-tuple-element.15.heads, bf16[2,256,1024]{2,1,0:T(8,128)(2,1)} %get-tuple-element.16.tails, bf16[1024,3456]{1,0:T(8,128)(2,1)} %bitcast.23.head_ref.tail_ref, bf16[1024,3456]{1,0:T(8,128)(2,1)} %bitcast.23.head_ref.tail_ref), custom_call_target="tpu_custom_call" | custom-call | tf_op jit(solution)/shard_map/combine/pallas_call | solution.py:470
  358.9 1.2 copy.44
  360.1 0.3 reshape.166
  360.4 1.4 copy.42
  (30 shorter events, 0.4 us)
Async XLA Ops:
  37.2 7.3 %copy-start.5 = (s32[64,2,8]{0,2,1:T(8,128)S(1)}, s32[64,2,8]{0,2,1:T(8,128)}, u32[]{:S(2)}) copy-start(s32[64,2,8]{0,2,1:T(8,128)} %param.31) | copy-start | bytes 12292
  37.2 8.0 %copy-start.6 = (bf16[2304]{0:T(1024)(128)(2,1)S(1)}, bf16[2304]{0:T(1024)(128)(2,1)}, u32[]{:S(2)}) copy-start(bf16[2304]{0:T(1024)(128)(2,1)} %param.29) | copy-start | bytes 13828
  37.2 8.6 %copy-start = (bf16[64,2,2304]{2,1,0:T(2,128)(2,1)S(1)}, bf16[64,2,2304]{2,1,0:T(2,128)(2,1)}, u32[]{:S(2)}) copy-start(bf16[64,2,2304]{2,1,0:T(2,128)(2,1)} %param.20) | copy-start | bytes 1769476
  37.2 61.7 %all-to-all-start = ((bf16[8,128,2304]{2,1,0:T(8,128)(2,1)}), bf16[8,128,2304]{2,1,0:T(8,128)(2,1)}, u32[]{:S(2)}, u32[]{:S(2)}) async-start(bf16[8,128,2304]{2,1,0:T(8,128)(2,1)} %get-tuple-element.11), calls=%async_computation | async-start | bytes 9437184 | tf_op jit(solution)/shard_map/all_to_all | solution.py:526
  108.2 8.5 %copy-start.8 = (bf16[8,128,128]{2,1,0:T(8,128)(2,1)S(1)}, bf16[8,128,128]{2,1,0:T(8,128)(2,1)}, u32[]{:S(2)}) copy-start(bf16[8,128,128]{2,1,0:T(8,128)(2,1)} %get-tuple-element.18) | copy-start | bytes 786436
  108.2 100.5 %all-to-all-start.1 = ((bf16[128,8,3456]{2,1,0:T(8,128)(2,1)}), bf16[128,8,3456]{2,1,0:T(8,128)(2,1)}, u32[]{:S(2)}, u32[]{:S(2)}) async-start(bf16[128,8,3456]{2,1,0:T(8,128)(2,1)} %bitcast.75), calls=%async_computation.1 | async-start | bytes 14155776 | tf_op jit(solution)/shard_map/all_to_all | solution.py:531
  116.7 92.0 %collective-permute-start = (bf16[8,128,128]{2,1,0:T(8,128)(2,1)S(1)}, bf16[8,128,128]{2,1,0:T(8,128)(2,1)}, u32[]{:S(2)}, u32[]{:S(2)}) collective-permute-start(bf16[8,128,128]{2,1,0:T(8,128)(2,1)S(1)} %copy-done.8), channel_id=1, source_target_pairs={{0,0},{1,8},{2,16},{3,24},{4,32},{5,40},{6,48},{7,56},{8,1},{9,9},... | collective-permute-start | bytes 786440 | tf_op jit(solution)/shard_map/ppermute | solution.py:521
  208.8 43.4 %all-to-all-start.3 = ((bf16[8,128,128]{2,1,0:T(8,128)(2,1)}), bf16[8,128,128]{2,1,0:T(8,128)(2,1)S(1)}, u32[]{:S(2)}, u32[]{:S(2)}) async-start(bf16[8,128,128]{2,1,0:T(8,128)(2,1)} %collective-permute-done), calls=%async_computation.3 | async-start | bytes 524288 | tf_op jit(solution)/shard_map/all_to_all | solution.py:540
  252.2 8.7 %copy-start.7 = (f32[16,2,4]{0,2,1:T(4,128)S(1)}, f32[16,2,4]{0,2,1:T(4,128)}, u32[]{:S(2)}) copy-start(f32[16,2,4]{0,2,1:T(4,128)} %param.39) | copy-start | bytes 1540
  252.2 9.2 %copy-start.4 = (bf16[16,2,4,128]{3,2,1,0:T(4,128)(2,1)S(1)}, bf16[16,2,4,128]{3,2,1,0:T(4,128)(2,1)}, u32[]{:S(2)}) copy-start(bf16[16,2,4,128]{3,2,1,0:T(4,128)(2,1)} %param.35) | copy-start | bytes 98308
  252.2 9.2 %copy-start.1 = (bf16[16,2,4,16]{3,2,1,0:T(4,128)(2,1)S(1)}, bf16[16,2,4,16]{3,2,1,0:T(4,128)(2,1)}, u32[]{:S(2)}) copy-start(bf16[16,2,4,16]{3,2,1,0:T(4,128)(2,1)} %param.37) | copy-start | bytes 12292
  252.2 9.4 %copy-start.2 = (bf16[16,2,4,128]{3,2,1,0:T(4,128)(2,1)S(1)}, bf16[16,2,4,128]{3,2,1,0:T(4,128)(2,1)}, u32[]{:S(2)}) copy-start(bf16[16,2,4,128]{3,2,1,0:T(4,128)(2,1)} %param.36) | copy-start | bytes 98308
  252.2 9.7 %copy-start.3 = (f32[16,2,4,128]{3,2,1,0:T(4,128)S(1)}, f32[16,2,4,128]{3,2,1,0:T(4,128)}, u32[]{:S(2)}) copy-start(f32[16,2,4,128]{3,2,1,0:T(4,128)} %param.38) | copy-start | bytes 196612
  252.2 96.1 %all-to-all-start.2 = ((bf16[128,8,3456]{2,1,0:T(8,128)(2,1)}), bf16[128,8,3456]{2,1,0:T(8,128)(2,1)}, u32[]{:S(2)}, u32[]{:S(2)}) async-start(bf16[128,8,3456]{2,1,0:T(8,128)(2,1)} %bitcast.74), calls=%async_computation.2 | async-start | bytes 14155776 | tf_op jit(solution)/shard_map/all_to_all | solution.py:531

commit v3 on v2

--- a/solution.py
+++ b/solution.py
@@ -11,6 +11,7 @@
 ROUTE_SCALE = 2.446
 LANES = 128
 BLOCK = 64
+SUBS = 4
 VMEM = 60 << 20
 F32 = jnp.float32
 BF16 = jnp.bfloat16
@@ -54,7 +55,8 @@
     def _():
         for chain in every:
             state[chain] = init_ref[chain].T
-        rate_col[...] = rate_ref[...].T
+        for request in range(requests):
+            rate_col[:, request * heads : (request + 1) * heads] = rate_ref[request].T
 
     q_all[...] = q_ref[...].astype(F32)
     k_all[...] = k_ref[...].astype(F32)
@@ -63,68 +65,90 @@
     row = iota((BLOCK, BLOCK), 0)
     col = iota((BLOCK, BLOCK), 1)
     lower = jnp.where(row >= col, 1.0, 0.0).astype(BF16)
-    position = step * BLOCK + iota((BLOCK, 1), 0)
-    rates = rate_col[pl.ds(pl.multiple_of(step * BLOCK, BLOCK), BLOCK), :]
-    live = [position < counts[request] for request in range(requests)]
-    live = [live[chain // heads] for chain in every]
-    rows = [pl.ds((c % heads) * requests + c // heads, BLOCK, stride=chains) for c in every]
+    identity = jnp.where(row == col, 1.0, 0.0)
+    units = [(sub, c) for sub in range(SUBS) for c in every]
+    rows, rate, live = [], [], []
+    for sub, c in units:
+        rows.append(
+            pl.ds(
+                sub * BLOCK * chains + (c % heads) * requests + c // heads, BLOCK, stride=chains
+            )
+        )
+        first = pl.multiple_of((step * SUBS + sub) * BLOCK, BLOCK)
+        live.append(first + iota((BLOCK, 1), 0) < counts[c // heads])
+        rate.append(jnp.where(live[-1], rate_col[pl.ds(first, BLOCK), c : c + 1], 0.0))
+    count = range(len(units))
 
     withins = []
-    for c in every:
-        decay = jnp.where(live[c], d_ref[rows[c], :], 0.0)
+    for u in count:
+        decay = jnp.where(live[u], d_ref[rows[u], :], 0.0)
         high, rest = decay.astype(BF16), decay - decay.astype(BF16).astype(F32)
         middle, low = halves(rest)
         withins.append(dot(lower, high) + dot(lower, middle) + dot(lower, low))
-    rate = [jnp.where(live[c], rates[:, c : c + 1], 0.0) for c in every]
     key_up, key_end, query_up, fades, systems, reaches = [], [], [], [], [], []
-    for c in every:
-        key = k_all[rows[c], :]
+    for u in count:
+        key = k_all[rows[u], :]
         key = key * lax.rsqrt(jnp.sum(key * key, axis=-1, keepdims=True) + EPSILON)
-        grow = jnp.exp(withins[c])
+        grow = jnp.exp(withins[u])
         fade = grow[BLOCK - 1 :, :]
-        down = key * jnp.exp(-withins[c])
+        down = key * jnp.exp(-withins[u])
         up_hi, up_lo = halves(key * grow)
         down_hi, down_lo = halves(down)
-        query = (q_all[rows[c], :] * grow).astype(BF16)
+        query = (q_all[rows[u], :] * grow).astype(BF16)
         both = dot(jnp.concatenate([up_hi, query], axis=0), down_hi, NT)
         pair = both[:BLOCK] + dot(up_hi, down_lo, NT) + dot(up_lo, down_hi, NT)
         reaches.append(jnp.where(row >= col, both[BLOCK:], 0.0).astype(BF16))
-        systems.append(jnp.where(row > col, rate[c] * pair, 0.0))
+        systems.append(jnp.where(row > col, rate[u] * pair, 0.0))
         key_up.append(key * grow)
         key_end.append(halves(down * fade))
         query_up.append(query)
         fades.append(fade)
     near = row >> 1 == col >> 1
-    inverse = [jnp.where(row == col, 1.0, 0.0) - jnp.where(near, s, 0.0) for s in systems]
+    inverse = [identity - jnp.where(near, member, 0.0) for member in systems]
     for bit in range(1, BLOCK.bit_length() - 1):
         joins = (row >> (bit + 1) == col >> (bit + 1)) & (row >> bit != col >> bit)
-        split = [halves(member) for member in inverse]
+        rough = [member.astype(BF16) for member in inverse]
         inner = [
-            dot3(halves(jnp.where(joins, systems[c], 0.0)), split[c]) for c in every
+            dot(jnp.where(joins, systems[u], 0.0).astype(BF16), rough[u]).astype(BF16)
+            for u in count
         ]
-        inverse = [inverse[c] - dot3(split[c], halves(inner[c])) for c in every]
+        inverse = [inverse[u] - dot(rough[u], inner[u]) for u in count]
     split = [halves(member) for member in inverse]
-    base_v = [dot3(split[c], halves(rate[c] * v_all[rows[c], :])) for c in every]
-    base_k = [halves(dot3(split[c], halves(rate[c] * key_up[c]))) for c in every]
-    boths, carries, updates = [], [], []
-    for c in every:
-        carry = halves(state[c])
-        both = dot(jnp.concatenate([base_k[c][0], query_up[c]], axis=0), carry[0], NT)
-        reached = both[:BLOCK] + dot(base_k[c][0], carry[1], NT) + dot(base_k[c][1], carry[0], NT)
-        updates.append(halves(base_v[c] - reached))
-        boths.append(both[BLOCK:])
-    for c in every:
-        state[c] = fades[c] * state[c] + dot3(updates[c], key_end[c], TN)
-    for c in every:
-        request, head = divmod(c, heads)
-        out = (boths[c] + dot(reaches[c], updates[c][0])) * key_dim ** (-0.5)
-        att[request * BLOCK : (request + 1) * BLOCK, head * LANES : (head + 1) * LANES] = (
-            out.astype(BF16)
-        )
+    missing = [
+        (identity - inverse[u] - dot3(halves(systems[u]), split[u])).astype(BF16) for u in count
+    ]
+    inverse = [inverse[u] + dot(split[u][0], missing[u]) for u in count]
+    split = [halves(member) for member in inverse]
+    base_v = [dot3(split[u], halves(rate[u] * v_all[rows[u], :])) for u in count]
+    base_k = [halves(dot3(split[u], halves(rate[u] * key_up[u]))) for u in count]
+    for sub in range(SUBS):
+        here = [sub * chains + c for c in every]
+        boths, updates = [], []
+        for c, u in enumerate(here):
+            carry = halves(state[c])
+            both = dot(jnp.concatenate([base_k[u][0], query_up[u]], axis=0), carry[0], NT)
+            reached = (
+                both[:BLOCK] + dot(base_k[u][0], carry[1], NT) + dot(base_k[u][1], carry[0], NT)
+            )
+            updates.append(halves(base_v[u] - reached))
+            boths.append(both[BLOCK:])
+        for c, u in enumerate(here):
+            state[c] = fades[u] * state[c] + dot3(updates[c], key_end[u], TN)
+        for c, u in enumerate(here):
+            request, head = divmod(c, heads)
+            out = (boths[c] + dot(reaches[u], updates[c][0])) * key_dim ** (-0.5)
+            att[
+                (sub * requests + request) * BLOCK : (sub * requests + request + 1) * BLOCK,
+                head * LANES : (head + 1) * LANES,
+            ] = out.astype(BF16)
 
     width = w_ref.shape[1]
     for lane in range(0, width, 768):
-        part_ref[0, :, lane : lane + 768] = dot(att[...], w_ref[:, lane : lane + 768]).astype(BF16)
+        done = dot(att[...], w_ref[:, lane : lane + 768]).astype(BF16)
+        for sub in range(SUBS):
+            part_ref[sub, :, lane : lane + 768] = done[
+                sub * requests * BLOCK : (sub + 1) * requests * BLOCK
+            ]
 
     @pl.when(step == pl.num_programs(0) - 1)
     def _():
@@ -149,9 +173,10 @@
     def whole(*shape):
         return pl.BlockSpec(shape, lambda n, *_: (0,) * len(shape))
 
-    tall = BLOCK * chains
+    tall = SUBS * BLOCK * chains
     block = pl.BlockSpec((tall, key_dim), lambda n, *_: (n, 0))
-    steps = length // BLOCK
+    blocks = length // BLOCK
+    steps = blocks // SUBS
     return pl.pallas_call(
         delta_kernel,
         grid_spec=pltpu.PrefetchScalarGridSpec(
@@ -159,12 +184,12 @@
             grid=(steps,),
             in_specs=[block] * 4
             + [
-                whole(chains, length),
+                whole(requests, heads, length),
                 whole(chains, key_dim, value_dim),
                 whole(features, width),
             ],
             out_specs=[
-                pl.BlockSpec((1, requests * BLOCK, width), lambda n, *_: (n, 0, 0)),
+                pl.BlockSpec((SUBS, requests * BLOCK, width), lambda n, *_: (n, 0, 0)),
                 whole(members, chains * value_dim // members, key_dim),
             ],
             scratch_shapes=[
@@ -173,11 +198,11 @@
                 pltpu.VMEM((tall, key_dim), F32),
                 pltpu.VMEM((tall, key_dim), F32),
                 pltpu.VMEM((tall, value_dim), F32),
-                pltpu.VMEM((requests * BLOCK, features), BF16),
+                pltpu.VMEM((SUBS * requests * BLOCK, features), BF16),
             ],
         ),
         out_shape=[
-            jax.ShapeDtypeStruct((steps, requests * BLOCK, width), BF16),
+            jax.ShapeDtypeStruct((blocks, requests * BLOCK, width), BF16),
             jax.ShapeDtypeStruct((members, chains * value_dim // members, key_dim), BF16),
         ],
         compiler_params=pltpu.CompilerParams(vmem_limit_bytes=VMEM),
@@ -188,7 +213,7 @@
         rows_of(key_in),
         rows_of(value_in),
         rows_of(log_decay),
-        update_rate.transpose(1, 2, 0).reshape(chains, length),
+        update_rate.transpose(1, 2, 0),
         init_state.reshape(chains, key_dim, value_dim),
         w_out,
     )
@@ -404,9 +429,10 @@
     for index, part in enumerate(halves(weight_ref[...])):
         spread = dot(part, pick)
         here = slice(index * tokens, (index + 1) * tokens)
+        there = slice((index + 2) * tokens, (index + 3) * tokens)
         heads[here, :] = jnp.where(is_head, spread, 0.0).astype(BF16)
-        tails[0, here, :] = jnp.where(is_tail & ((line & 4) == 0), spread, 0.0).astype(BF16)
-        tails[1, here, :] = jnp.where(is_tail & ((line & 4) != 0), spread, 0.0).astype(BF16)
+        tails[here, :] = jnp.where(is_tail & ((line & 4) == 0), spread, 0.0).astype(BF16)
+        tails[there, :] = jnp.where(is_tail & ((line & 4) != 0), spread, 0.0).astype(BF16)
 
 
 def spread_of(slot, weight):
@@ -419,7 +445,7 @@
         out_specs=[vmem] * 2,
         out_shape=[
             jax.ShapeDtypeStruct((2 * tokens, rows), BF16),
-            jax.ShapeDtypeStruct((2, 2 * tokens, rows), BF16),
+            jax.ShapeDtypeStruct((4 * tokens, rows), BF16),
         ],
         compiler_params=pltpu.CompilerParams(vmem_limit_bytes=VMEM),
         name="spread",
@@ -441,10 +467,11 @@
     lanes = pl.ds(pl.multiple_of(step * tile, tile), tile)
     both = dot(heads[...], head_ref[...])
     total[:, lanes] += both[:tokens] + both[tokens:]
+    both = dot(tails[...], tail_ref[...])
     for side in range(2):
         lanes = pl.ds(pl.multiple_of(side * half + step * thin, thin), thin)
-        both = dot(tails[side], tail_ref[...])
-        total[:, lanes] += both[:tokens] + both[tokens:]
+        first = 2 * side * tokens
+        total[:, lanes] += both[first : first + tokens] + both[first + tokens : first + 2 * tokens]
 
     @pl.when(step == pl.num_programs(0) - 1)
     def _():
@@ -460,7 +487,7 @@
 def combine(mixed, heads, tails, back):
     tokens, width = mixed.shape
     rows, across = back.shape
-    tile, thin = 256, 128
+    tile, thin = 768, 384
     steps = width // tile
 
     def whole(member):
@@ -486,6 +513,17 @@
         compiler_params=pltpu.CompilerParams(vmem_limit_bytes=VMEM),
         name="combine",
     )(mixed, heads, tails, back, back)
+
+
+def hand_out(member, axis):
+    size = lax.axis_size(axis)
+    here = lax.axis_index(axis)
+    ahead = lax.dynamic_slice_in_dim(jnp.concatenate([member, member]), here, size)
+    got = [ahead[0]]
+    for shift in range(1, size):
+        ring = [(i, (i + shift) % size) for i in range(size)]
+        got.append(lax.ppermute(ahead[shift], axis, ring))
+    return lax.dynamic_slice_in_dim(jnp.stack((got[::-1]) * 2), size - 1 - here, size)
 
 
 def decode(relaid, dec_query, dec_key, dec_value, dec_decay, dec_beta):
@@ -537,7 +575,7 @@
     heads_of, tails_of = spread_of(slot, weight)
     back = exchange(experts_of(arrived, w_gate[0], w_up[0], w_down[0]))
 
-    relaid = lax.all_to_all(final, "exp", split_axis=0, concat_axis=0, tiled=True)
+    relaid = hand_out(final, "exp")
     relaid = relaid.reshape(groups * requests, heads, value_dim // members, key_dim)
     dec_out, dec_state = decode(relaid, dec_query, dec_key, dec_value, dec_decay, dec_beta)
 

time: 363 us -> 361 us (level)
  Pallas kernels: 90.5 us -> 77.2 us
  starting transfers between devices: 40.2 us -> 45.9 us
  waiting for transfers between devices: 218 us -> 223 us
    ppermute x0 -> x7, waiting for transfers between devices: none -> 88.5 us  [hand_out(): got.append(lax.ppermute(ahead[shift], axis, ring))]
    ppermute x1, waiting for transfers between devices: 86.8 us -> 0.01 us  [shards(): lax.ppermute(final, ('grp', 'exp'), [(g * members + e, e * members + g) f...]
    all_to_all x1 -> x0, starting transfers between devices: 10.6 us -> none  [shards(): lax.all_to_all(final, 'exp', split_axis=0, concat_axis=0, tiled=True)]
    pallas_call x1, Pallas kernels: 35.2 us -> 25 us  [delta(): pl.pallas_call(delta_kernel, grid_spec=pltpu.PrefetchScalarGridSpec(num_s...]
    ppermute x0 -> x7, starting transfers between devices: none -> 9.64 us  [hand_out(): got.append(lax.ppermute(ahead[shift], axis, ring))]
    all_to_all x2, starting transfers between devices: 17.1 us -> 23.8 us  [exchange(): lax.all_to_all(member, ('exp', 'grp', 'half'), split_axis=0, concat_axis=...]
  transfers between devices with their start and end apart: 5 -> 11, of which waited for: 3 -> 5; matrix products, arithmetic and copies ran while one was open for 2% -> 2% of each run, Pallas kernels for 10% -> 10%
where the time goes in v3:
time: 361 us; the launch traced here: 358 us
  waiting for transfers between devices  223 us (62%)
  Pallas kernels  77.2 us (21%)
  starting transfers between devices  45.9 us (13%)
  local copies, waits for them, and re-layouts  7.49 us (2%)
    ppermute x7, waiting for transfers between devices, hand_out(): got.append(lax.ppermute(ahead[shift], axis, ring))  88.5 us
    all_to_all x2, waiting for transfers between devices, exchange(): lax.all_to_all(member, ('exp', 'grp', 'half'), split_axis=0, concat_axis=...  83.4 us
    all_to_all x1, waiting for transfers between devices, shards(): lax.all_to_all(parts, 'exp', split_axis=0, concat_axis=0, tiled=True)  51.3 us
    pallas_call x1, Pallas kernels, experts_of(): pl.pallas_call(functools.partial(expert_kernel, ups=ups), grid=(ups + dow...  32.8 us
    pallas_call x1, Pallas kernels, delta(): pl.pallas_call(delta_kernel, grid_spec=pltpu.PrefetchScalarGridSpec(num_s...  25 us
    all_to_all x2, starting transfers between devices, exchange(): lax.all_to_all(member, ('exp', 'grp', 'half'), split_axis=0, concat_axis=...  23.8 us
    ppermute x7, starting transfers between devices, hand_out(): got.append(lax.ppermute(ahead[shift], axis, ring))  9.64 us
    pallas_call x1, Pallas kernels, route(): pl.pallas_call(route_kernel, in_specs=[vmem] * 5, out_specs=[vmem] * 4, s...  9.3 us
  transfers between devices with their start and end apart: 11, of which 5 were waited for; matrix products, arithmetic and copies ran while one was open for 2% of the time, Pallas kernels for 10%

profile of v3, /device:TPU:24, one launch (start us, length us, event | category | flops | bytes accessed | tf_op | source)
XLA Modules:
  0.0 358.4 jit_solution(2970740066789502151)
XLA Ops:
  0.6 25.0 %delta.1 = (bf16[8,128,2304]{2,1,0:T(8,128)(2,1)}, bf16[8,128,128]{2,1,0:T(8,128)(2,1)}) custom-call(s32[2]{0:T(128)} %counts.1, bf16[4096,128]{1,0:T(8,128)(2,1)} %bitcast.128, bf16[4096,128]{1,0:T(8,128)(2,1)} %bitcast.129, bf16[4096,128]{1,0:T(8,128)(2,1)} %bitcast.130, f32[4096,128]{1,0:T(8,128)} %bitcast.127, f32[2,4,512]{2,1,0:T(4,128)} %bitcast.132, ...), custom_call_target="tpu_custom_call" | custom-call | tf_op jit(solution)/shard_map/delta/pallas_call | solution.py:180
  25.6 7.3 %all-to-all-start = ((bf16[8,128,2304]{2,1,0:T(8,128)(2,1)}), bf16[8,128,2304]{2,1,0:T(8,128)(2,1)}, u32[]{:S(2)}, u32[]{:S(2)}) async-start(bf16[8,128,2304]{2,1,0:T(8,128)(2,1)} %get-tuple-element.11), calls=%async_computation | async-start | bytes 9437184 | tf_op jit(solution)/shard_map/all_to_all | solution.py:564
  32.9 0.7 reshape.156.ids_ref
  33.6 0.6 reshape.155.gain_ref
  34.2 0.1 copy.32
  34.3 0.3 reshape.144
  34.6 1.4 copy.33
  36.0 51.3 %all-to-all-done.part_ref = bf16[8,128,2304]{2,1,0:T(8,128)(2,1)} async-done(((bf16[8,128,2304]{2,1,0:T(8,128)(2,1)}), bf16[8,128,2304]{2,1,0:T(8,128)(2,1)}, u32[]{:S(2)}, u32[]{:S(2)}) %all-to-all-start) | async-done | bytes 4718624 | tf_op jit(solution)/shard_map/all_to_all | solution.py:564
  87.3 9.3 %route.1 = (f32[128,2304]{1,0:T(8,128)}, f32[128,128]{1,0:T(8,128)}, f32[128,128]{1,0:T(8,128)}, bf16[1024,3456]{1,0:T(8,128)(2,1)}) custom-call(bf16[2304,128]{1,0:T(8,128)(2,1)} %bitcast.122, bf16[8,128,2304]{2,1,0:T(8,128)(2,1)} %all-to-all-done.part_ref, bf16[1,2304]{1,0:T(2,128)(2,1)} %reshape.155.gain_ref, bf16[2304,128]{1,0:T(8,128)(2,1)} %router_ref.1, ...), custom_call_target="tpu_custom_call" | custom-call | tf_op jit(solution)/shard_map/route/pallas_call | solution.py:308
  96.6 8.5 %all-to-all-start.1 = ((bf16[128,8,3456]{2,1,0:T(8,128)(2,1)}), bf16[128,8,3456]{2,1,0:T(8,128)(2,1)}, u32[]{:S(2)}, u32[]{:S(2)}) async-start(bf16[128,8,3456]{2,1,0:T(8,128)(2,1)} %bitcast.109), calls=%async_computation.1 | async-start | bytes 14155776 | tf_op jit(solution)/shard_map/all_to_all | solution.py:569
  105.2 5.2 %collective-permute-start = (bf16[8,128,128]{2,1,0:T(8,128)(2,1)S(1)}, bf16[8,128,128]{2,1,0:T(8,128)(2,1)S(1)}, u32[]{:S(2)}, u32[]{:S(2)}) collective-permute-start(bf16[8,128,128]{2,1,0:T(8,128)(2,1)S(1)} %copy-done.8), channel_id=1, source_target_pairs={{0,0},{1,8},{2,16},{3,24},{4,32},{5,40},{6,48},{7,56},{8,1},{9,9},... | collective-permute-start | bytes 786440 | tf_op jit(solution)/shard_map/ppermute | solution.py:559
  110.4 0.1 fusion.3
  110.5 83.4 %all-to-all-done.1 = bf16[128,8,3456]{2,1,0:T(8,128)(2,1)} async-done(((bf16[128,8,3456]{2,1,0:T(8,128)(2,1)}), bf16[128,8,3456]{2,1,0:T(8,128)(2,1)}, u32[]{:S(2)}, u32[]{:S(2)}) %all-to-all-start.1) | async-done | bytes 7077920 | tf_op jit(solution)/shard_map/all_to_all | solution.py:569
  193.9 32.8 %experts.1 = bf16[1024,3456]{1,0:T(8,128)(2,1)} custom-call(bf16[1024,3456]{1,0:T(8,128)(2,1)} %bitcast.18.x_ref, bf16[2304,1024]{1,0:T(8,128)(2,1)} %bitcast.110, bf16[2304,1024]{1,0:T(8,128)(2,1)} %bitcast.111, bf16[1024,2304]{1,0:T(8,128)(2,1)} %bitcast.112), custom_call_target="tpu_custom_call" | custom-call | tf_op jit(solution)/shard_map/experts/pallas_call | solution.py:401
  226.7 15.3 %all-to-all-start.2 = ((bf16[128,8,3456]{2,1,0:T(8,128)(2,1)}), bf16[128,8,3456]{2,1,0:T(8,128)(2,1)}, u32[]{:S(2)}, u32[]{:S(2)}) async-start(bf16[128,8,3456]{2,1,0:T(8,128)(2,1)} %bitcast.108), calls=%async_computation.2 | async-start | bytes 14155776 | tf_op jit(solution)/shard_map/all_to_all | solution.py:569
  242.1 0.1 convert_multiply_fusion
  242.3 0.1 fusion
  242.4 0.9 collective-permute-start.1
  243.3 0.1 copy.41
  243.4 0.1 copy.40
  243.5 0.1 mul.175
  243.6 0.1 mul.176
  243.7 0.1 mul.195
  243.7 0.1 mul.196
  243.8 0.1 squeeze.53
  243.9 0.1 squeeze.52
  244.0 4.8 %collective-permute-start.7 = (bf16[128,128]{1,0:T(8,128)(2,1)S(1)}, bf16[128,128]{1,0:T(8,128)(2,1)S(1)}, u32[]{:S(2)}, u32[]{:S(2)}) collective-permute-start(bf16[128,128]{1,0:T(8,128)(2,1)S(1)} %get-tuple-element.25), channel_id=1, source_target_pairs={{0,1},{1,2},{2,3},{3,4},{4,5},{5,6},{6,7},{7,0},{8,9},{9,10},{10,1... | collective-permute-start | bytes 98312 | tf_op jit(solution)/shard_map/ppermute | solution.py:525
  248.9 0.2 collective-permute-start.6
  249.1 3.2 collective-permute-start.5
  252.2 0.5 collective-permute-start.4
  252.8 74.4 %collective-permute-done.1 = bf16[128,128]{1,0:T(8,128)(2,1)S(1)} collective-permute-done((bf16[128,128]{1,0:T(8,128)(2,1)S(1)}, bf16[128,128]{1,0:T(8,128)(2,1)S(1)}, u32[]{:S(2)}, u32[]{:S(2)}) %collective-permute-start.1) | collective-permute-done | bytes 32800 | tf_op jit(solution)/shard_map/ppermute | solution.py:525
  327.2 7.8 %collective-permute-done.2 = bf16[128,128]{1,0:T(8,128)(2,1)S(1)} collective-permute-done((bf16[128,128]{1,0:T(8,128)(2,1)S(1)}, bf16[128,128]{1,0:T(8,128)(2,1)S(1)}, u32[]{:S(2)}, u32[]{:S(2)}) %collective-permute-start.2) | collective-permute-done | bytes 32800 | tf_op jit(solution)/shard_map/ppermute | solution.py:525
  335.0 6.3 %collective-permute-done.3 = bf16[128,128]{1,0:T(8,128)(2,1)S(1)} collective-permute-done((bf16[128,128]{1,0:T(8,128)(2,1)S(1)}, bf16[128,128]{1,0:T(8,128)(2,1)S(1)}, u32[]{:S(2)}, u32[]{:S(2)}) %collective-permute-start.3) | collective-permute-done | bytes 32800 | tf_op jit(solution)/shard_map/ppermute | solution.py:525
  341.6 0.2 multiply_reduce_fusion.3
  341.9 0.1 reduce_sum.54
  342.1 0.6 multiply_reduce_fusion.1
  342.7 0.1 reduce_sum.55
  342.8 0.4 multiply_reduce_fusion
  343.2 0.1 stack.49
  343.3 0.1 stack.48
  343.4 0.7 maximum_multiply_fusion
  344.1 0.1 fusion.5
  344.2 1.1 add_bitcast_fusion
  345.3 2.7 spread.1
  348.1 7.4 %combine.1 = bf16[2304,128]{1,0:T(8,128)(2,1)} custom-call(f32[128,2304]{1,0:T(8,128)} %get-tuple-element.12.mixed_ref, bf16[256,1024]{1,0:T(8,128)(2,1)} %get-tuple-element.15.heads, bf16[512,1024]{1,0:T(8,128)(2,1)} %get-tuple-element.16.tails, bf16[1024,3456]{1,0:T(8,128)(2,1)} %bitcast.23.head_ref.tail_ref, bf16[1024,3456]{1,0:T(8,128)(2,1)} %bitcast.23.head_ref.tail_ref), custom_call_target="tpu_custom_call" | custom-call | tf_op jit(solution)/shard_map/combine/pallas_call | solution.py:497
  355.5 1.2 copy.44
  356.6 0.3 reshape.162
  356.9 1.4 copy.42
  (60 shorter events, 0.6 us)
Async XLA Ops:
  25.6 7.3 %copy-start.5 = (s32[64,2,8]{0,2,1:T(8,128)S(1)}, s32[64,2,8]{0,2,1:T(8,128)}, u32[]{:S(2)}) copy-start(s32[64,2,8]{0,2,1:T(8,128)} %param.31) | copy-start | bytes 12292
  25.6 8.0 %copy-start.6 = (bf16[2304]{0:T(1024)(128)(2,1)S(1)}, bf16[2304]{0:T(1024)(128)(2,1)}, u32[]{:S(2)}) copy-start(bf16[2304]{0:T(1024)(128)(2,1)} %param.29) | copy-start | bytes 13828
  25.6 8.6 %copy-start = (bf16[64,2,2304]{2,1,0:T(2,128)(2,1)S(1)}, bf16[64,2,2304]{2,1,0:T(2,128)(2,1)}, u32[]{:S(2)}) copy-start(bf16[64,2,2304]{2,1,0:T(2,128)(2,1)} %param.20) | copy-start | bytes 1769476
  25.6 61.7 %all-to-all-start = ((bf16[8,128,2304]{2,1,0:T(8,128)(2,1)}), bf16[8,128,2304]{2,1,0:T(8,128)(2,1)}, u32[]{:S(2)}, u32[]{:S(2)}) async-start(bf16[8,128,2304]{2,1,0:T(8,128)(2,1)} %get-tuple-element.11), calls=%async_computation | async-start | bytes 9437184 | tf_op jit(solution)/shard_map/all_to_all | solution.py:564
  96.6 8.5 %copy-start.8 = (bf16[8,128,128]{2,1,0:T(8,128)(2,1)S(1)}, bf16[8,128,128]{2,1,0:T(8,128)(2,1)}, u32[]{:S(2)}) copy-start(bf16[8,128,128]{2,1,0:T(8,128)(2,1)} %get-tuple-element.18) | copy-start | bytes 786436
  96.6 13.7 %copy-start.4 = (bf16[16,2,4,128]{3,2,1,0:T(4,128)(2,1)S(1)}, bf16[16,2,4,128]{3,2,1,0:T(4,128)(2,1)}, u32[]{:S(2)}) copy-start(bf16[16,2,4,128]{3,2,1,0:T(4,128)(2,1)} %param.35) | copy-start | bytes 98308
  96.6 13.8 %copy-start.2 = (bf16[16,2,4,128]{3,2,1,0:T(4,128)(2,1)S(1)}, bf16[16,2,4,128]{3,2,1,0:T(4,128)(2,1)}, u32[]{:S(2)}) copy-start(bf16[16,2,4,128]{3,2,1,0:T(4,128)(2,1)} %param.36) | copy-start | bytes 98308
  96.6 97.3 %all-to-all-start.1 = ((bf16[128,8,3456]{2,1,0:T(8,128)(2,1)}), bf16[128,8,3456]{2,1,0:T(8,128)(2,1)}, u32[]{:S(2)}, u32[]{:S(2)}) async-start(bf16[128,8,3456]{2,1,0:T(8,128)(2,1)} %bitcast.109), calls=%async_computation.1 | async-start | bytes 14155776 | tf_op jit(solution)/shard_map/all_to_all | solution.py:569
  105.2 137.1 %collective-permute-start = (bf16[8,128,128]{2,1,0:T(8,128)(2,1)S(1)}, bf16[8,128,128]{2,1,0:T(8,128)(2,1)S(1)}, u32[]{:S(2)}, u32[]{:S(2)}) collective-permute-start(bf16[8,128,128]{2,1,0:T(8,128)(2,1)S(1)} %copy-done.8), channel_id=1, source_target_pairs={{0,0},{1,8},{2,16},{3,24},{4,32},{5,40},{6,48},{7,56},{8,1},{9,9},... | collective-permute-start | bytes 786440 | tf_op jit(solution)/shard_map/ppermute | solution.py:559
  226.7 15.5 %copy-start.1 = (bf16[16,2,4,16]{3,2,1,0:T(4,128)(2,1)S(1)}, bf16[16,2,4,16]{3,2,1,0:T(4,128)(2,1)}, u32[]{:S(2)}) copy-start(bf16[16,2,4,16]{3,2,1,0:T(4,128)(2,1)} %param.37) | copy-start | bytes 12292
  226.7 15.5 %copy-start.3 = (f32[16,2,4,128]{3,2,1,0:T(4,128)S(1)}, f32[16,2,4,128]{3,2,1,0:T(4,128)}, u32[]{:S(2)}) copy-start(f32[16,2,4,128]{3,2,1,0:T(4,128)} %param.38) | copy-start | bytes 196612
  226.7 16.6 %copy-start.7 = (f32[16,2,4]{0,2,1:T(4,128)S(1)}, f32[16,2,4]{0,2,1:T(4,128)}, u32[]{:S(2)}) copy-start(f32[16,2,4]{0,2,1:T(4,128)} %param.39) | copy-start | bytes 1540
  226.7 121.3 %all-to-all-start.2 = ((bf16[128,8,3456]{2,1,0:T(8,128)(2,1)}), bf16[128,8,3456]{2,1,0:T(8,128)(2,1)}, u32[]{:S(2)}, u32[]{:S(2)}) async-start(bf16[128,8,3456]{2,1,0:T(8,128)(2,1)} %bitcast.108), calls=%async_computation.2 | async-start | bytes 14155776 | tf_op jit(solution)/shard_map/all_to_all | solution.py:569
  242.4 84.7 %collective-permute-start.1 = (bf16[128,128]{1,0:T(8,128)(2,1)S(1)}, bf16[128,128]{1,0:T(8,128)(2,1)S(1)}, u32[]{:S(2)}, u32[]{:S(2)}) collective-permute-start(bf16[128,128]{1,0:T(8,128)(2,1)S(1)} %get-tuple-element.31), channel_id=1, source_target_pairs={{0,7},{1,0},{2,1},{3,2},{4,3},{5,4},{6,5},{7,6},{8,15},{9,8},{10,9... | collective-permute-start | bytes 98312 | tf_op jit(solution)/shard_map/ppermute | solution.py:525
  244.0 97.4 %collective-permute-start.7 = (bf16[128,128]{1,0:T(8,128)(2,1)S(1)}, bf16[128,128]{1,0:T(8,128)(2,1)S(1)}, u32[]{:S(2)}, u32[]{:S(2)}) collective-permute-start(bf16[128,128]{1,0:T(8,128)(2,1)S(1)} %get-tuple-element.25), channel_id=1, source_target_pairs={{0,1},{1,2},{2,3},{3,4},{4,5},{5,6},{6,7},{7,0},{8,9},{9,10},{10,1... | collective-permute-start | bytes 98312 | tf_op jit(solution)/shard_map/ppermute | solution.py:525
  248.9 92.5 %collective-permute-start.6 = (bf16[128,128]{1,0:T(8,128)(2,1)S(1)}, bf16[128,128]{1,0:T(8,128)(2,1)S(1)}, u32[]{:S(2)}, u32[]{:S(2)}) collective-permute-start(bf16[128,128]{1,0:T(8,128)(2,1)S(1)} %get-tuple-element.26), channel_id=1, source_target_pairs={{0,2},{1,3},{2,4},{3,5},{4,6},{5,7},{6,0},{7,1},{8,10},{9,11},{10,... | collective-permute-start | bytes 98312 | tf_op jit(solution)/shard_map/ppermute | solution.py:525
  249.1 92.3 %collective-permute-start.5 = (bf16[128,128]{1,0:T(8,128)(2,1)S(1)}, bf16[128,128]{1,0:T(8,128)(2,1)S(1)}, u32[]{:S(2)}, u32[]{:S(2)}) collective-permute-start(bf16[128,128]{1,0:T(8,128)(2,1)S(1)} %get-tuple-element.27), channel_id=1, source_target_pairs={{0,3},{1,4},{2,5},{3,6},{4,7},{5,0},{6,1},{7,2},{8,11},{9,12},{10,... | collective-permute-start | bytes 98312 | tf_op jit(solution)/shard_map/ppermute | solution.py:525
  252.2 89.1 %collective-permute-start.4 = (bf16[128,128]{1,0:T(8,128)(2,1)S(1)}, bf16[128,128]{1,0:T(8,128)(2,1)S(1)}, u32[]{:S(2)}, u32[]{:S(2)}) collective-permute-start(bf16[128,128]{1,0:T(8,128)(2,1)S(1)} %get-tuple-element.28), channel_id=1, source_target_pairs={{0,4},{1,5},{2,6},{3,7},{4,0},{5,1},{6,2},{7,3},{8,12},{9,13},{10,... | collective-permute-start | bytes 98312 | tf_op jit(solution)/shard_map/ppermute | solution.py:525
  327.2 7.8 %collective-permute-start.2 = (bf16[128,128]{1,0:T(8,128)(2,1)S(1)}, bf16[128,128]{1,0:T(8,128)(2,1)S(1)}, u32[]{:S(2)}, u32[]{:S(2)}) collective-permute-start(bf16[128,128]{1,0:T(8,128)(2,1)S(1)} %get-tuple-element.30), channel_id=1, source_target_pairs={{0,6},{1,7},{2,0},{3,1},{4,2},{5,3},{6,4},{7,5},{8,14},{9,15},{10,... | collective-permute-start | bytes 98312 | tf_op jit(solution)/shard_map/ppermute | solution.py:525
  335.0 6.3 %collective-permute-start.3 = (bf16[128,128]{1,0:T(8,128)(2,1)S(1)}, bf16[128,128]{1,0:T(8,128)(2,1)S(1)}, u32[]{:S(2)}, u32[]{:S(2)}) collective-permute-start(bf16[128,128]{1,0:T(8,128)(2,1)S(1)} %get-tuple-element.29), channel_id=1, source_target_pairs={{0,5},{1,6},{2,7},{3,0},{4,1},{5,2},{6,3},{7,4},{8,13},{9,14},{10,... | collective-permute-start | bytes 98312 | tf_op jit(solution)/shard_map/ppermute | solution.py:525

commit v4 on v3

--- a/solution.py
+++ b/solution.py
@@ -232,8 +232,8 @@
 
 def route_kernel(
     res_ref, part_ref, gain_ref, router_ref, ids_ref,
-    mixed_ref, slot_ref, weight_ref, out_ref,
-    wide, normed,
+    mixed_ref, slot_ref, weight_ref, head_ref, tail_ref,
+    wide, normed, head_buf, tail_buf, sems,
 ):
     members, tokens, width = part_ref.shape
     requests = tokens // BLOCK
@@ -282,15 +282,28 @@
     tail_a = jnp.where(tail & ((line & 4) == 0), 1.0, 0.0).astype(BF16)
     tail_b = jnp.where(tail & ((line & 4) != 0), 1.0, 0.0).astype(BF16)
     half = width // 2
+    copies = []
+
+    def send(buf, ref, lane, step):
+        lanes = pl.ds(lane, step)
+        copies.append(
+            pltpu.make_async_copy(buf.at[:, lanes], ref.at[:, lanes], sems.at[len(copies)])
+        )
+        copies[-1].start()
+
     step = 6 * LANES
     for lane in range(0, width, step):
-        out_ref[:, lane : lane + step] = dot(head, normed[:, lane : lane + step]).astype(BF16)
+        head_buf[:, lane : lane + step] = dot(head, normed[:, lane : lane + step]).astype(BF16)
+        send(head_buf, head_ref, lane, step)
     step = 3 * LANES
     for lane in range(0, half, step):
-        out_ref[:, width + lane : width + lane + step] = (
+        tail_buf[:, lane : lane + step] = (
             dot(tail_a, normed[:, lane : lane + step])
             + dot(tail_b, normed[:, half + lane : half + lane + step])
         ).astype(BF16)
+        send(tail_buf, tail_ref, lane, step)
+    for copy in copies:
+        copy.wait()
 
 
 def interleave(member):
@@ -308,16 +321,20 @@
     return pl.pallas_call(
         route_kernel,
         in_specs=[vmem] * 5,
-        out_specs=[vmem] * 4,
+        out_specs=[vmem] * 3 + [pl.BlockSpec(memory_space=pl.ANY)] * 2,
         scratch_shapes=[
             pltpu.VMEM((tokens * width // LANES, LANES), F32),
             pltpu.VMEM((tokens, width), BF16),
+            pltpu.VMEM((experts * 8, width), BF16),
+            pltpu.VMEM((experts * 8, width // 2), BF16),
+            pltpu.SemaphoreType.DMA((6,)),
         ],
         out_shape=[
             jax.ShapeDtypeStruct((tokens, width), F32),
             jax.ShapeDtypeStruct((tokens, experts), F32),
             jax.ShapeDtypeStruct((tokens, experts), F32),
-            jax.ShapeDtypeStruct((experts * 8, width * 3 // 2), BF16),
+            jax.ShapeDtypeStruct((experts * 8, width), BF16),
+            jax.ShapeDtypeStruct((experts * 8, width // 2), BF16),
         ],
         compiler_params=pltpu.CompilerParams(vmem_limit_bytes=VMEM),
         name="route",
@@ -335,57 +352,74 @@
     return jnp.where(col == source, 1.0, 0.0).astype(dtype)
 
 
-def expert_kernel(x_ref, gate_ref, up_ref, down_ref, out_ref, tail_in, tail_out, inner, *, ups):
+def act(lines, gate_ref, up_ref):
+    gate = dot(lines, gate_ref[...])
+    up = dot(lines, up_ref[...])
+    return (gate / (1.0 + jnp.exp(-gate)) * up).astype(BF16)
+
+
+def head_kernel(x_ref, gate_ref, up_ref, down_ref, out_ref, inner, *, ups):
     step = pl.program_id(0)
-    rows, across = x_ref.shape
-    width = across * 2 // 3
-    half = width // 2
-    tails = rows // 2
+    rows = x_ref.shape[0]
+    fold = gate_ref.shape[1]
+
+    @pl.when(step < ups)
+    def _():
+        lanes = pl.ds(pl.multiple_of(step * fold, fold), fold)
+        for start in range(0, rows, GROUP):
+            here = slice(start, start + GROUP)
+            inner[here, lanes] = act(x_ref[here, :], gate_ref, up_ref)
+
+    @pl.when(step >= ups)
+    def _():
+        for start in range(0, rows, GROUP):
+            here = slice(start, start + GROUP)
+            out_ref[here, :] = dot(inner[here, :], down_ref[...]).astype(BF16)
+
+
+def tail_kernel(
+    x_ref, gate_ref, up_ref, down_ref, done_ref, out_ref, lines_in, lines_out, inner, *, ups
+):
+    step = pl.program_id(0)
+    rows, half = x_ref.shape
     fold = gate_ref.shape[1]
     tile = down_ref.shape[1]
+    tails = rows // 2
 
     @pl.when(step == 0)
     def _():
         order = unpack_rows()
         for group in range(rows // GROUP):
-            moved = dot(order, x_ref[pl.ds(group * GROUP, GROUP), width:]).astype(BF16)
+            moved = dot(order, x_ref[pl.ds(group * GROUP, GROUP), :]).astype(BF16)
             here = pl.ds(group * GROUP // 2, GROUP // 2)
-            tail_in[here, :half] = moved[: GROUP // 2]
-            tail_in[here, half:] = moved[GROUP // 2 :]
+            lines_in[here, :half] = moved[: GROUP // 2]
+            lines_in[here, half:] = moved[GROUP // 2 :]
 
     @pl.when(step < ups)
     def _():
         lanes = pl.ds(pl.multiple_of(step * fold, fold), fold)
-        for start in range(0, rows + tails, 256):
-            if start < rows:
-                lines = x_ref[start : start + 256, :width]
-            else:
-                lines = tail_in[start - rows : start - rows + 256, :]
-            gate = dot(lines, gate_ref[...])
-            up = dot(lines, up_ref[...])
-            inner[start : start + 256, lanes] = (gate / (1.0 + jnp.exp(-gate)) * up).astype(BF16)
+        for start in range(0, tails, GROUP):
+            here = slice(start, start + GROUP)
+            inner[here, lanes] = act(lines_in[here, :], gate_ref, up_ref)
 
     @pl.when(step >= ups)
     def _():
         lanes = pl.ds(pl.multiple_of((step - ups) * tile, tile), tile)
-        for start in range(0, rows + tails, 256):
-            result = dot(inner[start : start + 256, :], down_ref[...]).astype(BF16)
-            if start < rows:
-                out_ref[start : start + 256, lanes] = result
-            else:
-                tail_out[start - rows : start - rows + 256, lanes] = result
+        for start in range(0, tails, GROUP):
+            here = slice(start, start + GROUP)
+            lines_out[here, lanes] = dot(inner[here, :], down_ref[...]).astype(BF16)
 
     @pl.when(step == pl.num_programs(0) - 1)
     def _():
         order = unpack_rows()
         for group in range(rows // GROUP):
             here = pl.ds(group * GROUP // 2, GROUP // 2)
-            moved = jnp.concatenate([tail_out[here, :half], tail_out[here, half:]], axis=0)
-            out_ref[pl.ds(group * GROUP, GROUP), width:] = dot(order, moved, TN).astype(BF16)
-
-
-def experts_of(arrived, gate, up, down):
-    rows, across = arrived.shape
+            moved = jnp.concatenate([lines_out[here, :half], lines_out[here, half:]], axis=0)
+            out_ref[pl.ds(group * GROUP, GROUP), :] = dot(order, moved, TN).astype(BF16)
+
+
+def experts_of(arrived, gate, up, down, done=None):
+    rows = arrived.shape[0]
     width, hidden = gate.shape
     fold, tile = 256, 768
     ups, downs = hidden // fold, width // tile
@@ -397,26 +431,39 @@
     def later(step):
         return (0, jnp.maximum(step - ups, 0))
 
-    whole = pl.BlockSpec((rows, across), lambda step: (0, 0))
+    in_specs = [
+        pl.BlockSpec(arrived.shape, lambda step: (0, 0)),
+        pl.BlockSpec((width, fold), column),
+        pl.BlockSpec((width, fold), column),
+        pl.BlockSpec((hidden, tile), later),
+    ]
+    common = dict(
+        grid=(ups + downs,),
+        out_shape=jax.ShapeDtypeStruct((rows, width * 3 // 2), BF16),
+        compiler_params=pltpu.CompilerParams(vmem_limit_bytes=VMEM),
+    )
+    if done is None:
+        return pl.pallas_call(
+            functools.partial(head_kernel, ups=ups),
+            in_specs=in_specs,
+            out_specs=pl.BlockSpec((rows, tile), later),
+            scratch_shapes=[pltpu.VMEM((rows, hidden), BF16)],
+            name="experts_head",
+            **common,
+        )(arrived, gate, up, down)
     return pl.pallas_call(
-        functools.partial(expert_kernel, ups=ups),
-        grid=(ups + downs,),
-        in_specs=[
-            whole,
-            pl.BlockSpec((width, fold), column),
-            pl.BlockSpec((width, fold), column),
-            pl.BlockSpec((hidden, tile), later),
-        ],
-        out_specs=whole,
+        functools.partial(tail_kernel, ups=ups),
+        in_specs=in_specs + [pl.BlockSpec(memory_space=pl.ANY)],
+        out_specs=pl.BlockSpec((rows, width // 2), lambda step: (0, 2)),
         scratch_shapes=[
             pltpu.VMEM((tails, width), BF16),
             pltpu.VMEM((tails, width), BF16),
-            pltpu.VMEM((rows + tails, hidden), BF16),
+            pltpu.VMEM((tails, hidden), BF16),
         ],
-        out_shape=jax.ShapeDtypeStruct((rows, across), BF16),
-        compiler_params=pltpu.CompilerParams(vmem_limit_bytes=VMEM),
-        name="experts",
-    )(arrived, gate, up, down)
+        input_output_aliases={4: 0},
+        name="experts_tail",
+        **common,
+    )(arrived, gate, up, down, done)
 
 
 def spread_kernel(slot_ref, weight_ref, heads, tails):
@@ -515,17 +562,6 @@
     )(mixed, heads, tails, back, back)
 
 
-def hand_out(member, axis):
-    size = lax.axis_size(axis)
-    here = lax.axis_index(axis)
-    ahead = lax.dynamic_slice_in_dim(jnp.concatenate([member, member]), here, size)
-    got = [ahead[0]]
-    for shift in range(1, size):
-        ring = [(i, (i + shift) % size) for i in range(size)]
-        got.append(lax.ppermute(ahead[shift], axis, ring))
-    return lax.dynamic_slice_in_dim(jnp.stack((got[::-1]) * 2), size - 1 - here, size)
-
-
 def decode(relaid, dec_query, dec_key, dec_value, dec_decay, dec_beta):
     query = dec_query.astype(F32)
     key = dec_key.astype(F32)
@@ -562,7 +598,7 @@
         [(g * members + e, e * members + g) for g in range(groups) for e in range(members)],
     )
     parts = lax.all_to_all(parts, "exp", split_axis=0, concat_axis=0, tiled=True)
-    mixed, slot, weight, outgoing = route(residual, parts, norm_gain, w_router, expert_ids)
+    mixed, slot, weight, head, tail = route(residual, parts, norm_gain, w_router, expert_ids)
 
     def exchange(member):
         member = member.reshape(experts, 8, -1)
@@ -571,11 +607,14 @@
         )
         return member.reshape(experts * 8, -1)
 
-    arrived = exchange(outgoing)
+    head = exchange(head)
+    head, tail = lax.optimization_barrier((head, tail))
+    tail = exchange(tail)
     heads_of, tails_of = spread_of(slot, weight)
-    back = exchange(experts_of(arrived, w_gate[0], w_up[0], w_down[0]))
-
-    relaid = hand_out(final, "exp")
+    matrices = (w_gate[0], w_up[0], w_down[0])
+    back = exchange(experts_of(tail, *matrices, done=experts_of(head, *matrices)))
+
+    relaid = lax.all_to_all(final, "exp", split_axis=0, concat_axis=0, tiled=True)
     relaid = relaid.reshape(groups * requests, heads, value_dim // members, key_dim)
     dec_out, dec_state = decode(relaid, dec_query, dec_key, dec_value, dec_decay, dec_beta)
 

time: 361 us -> 361 us (level)
  blocking collectives: 0 us -> 65.6 us
  waiting for transfers between devices: 223 us -> 167 us
  starting transfers between devices: 45.9 us -> 35.3 us
  Pallas kernels: 77.2 us -> 81.1 us
    ppermute x7 -> x0, waiting for transfers between devices: 88.5 us -> none  [hand_out(): got.append(lax.ppermute(ahead[shift], axis, ring))]
    all_to_all x0 -> x1, blocking collectives: none -> 65.6 us  [exchange(): lax.all_to_all(member, ('exp', 'grp', 'half'), split_axis=0, concat_axis=...]
    ppermute x1, waiting for transfers between devices: 0.01 us -> 35 us  [shards(): lax.ppermute(final, ('grp', 'exp'), [(g * members + e, e * members + g) f...]
    ppermute x7 -> x0, starting transfers between devices: 9.64 us -> none  [hand_out(): got.append(lax.ppermute(ahead[shift], axis, ring))]
    all_to_all x2, starting transfers between devices: 23.8 us -> 15.4 us  [exchange(): lax.all_to_all(member, ('exp', 'grp', 'half'), split_axis=0, concat_axis=...]
    all_to_all x0 -> x1, starting transfers between devices: none -> 7.48 us  [shards(): lax.all_to_all(final, 'exp', split_axis=0, concat_axis=0, tiled=True)]
    pallas_call x2 -> x3, Pallas kernels: 42.1 us -> 46.1 us  [the longest x1 21.4 us: experts_of(): pl.pallas_call(functools.partial(head_kernel, ups=ups), in_specs=in_specs...]
  transfers between devices with their start and end apart: 11 -> 5, of which waited for: 5 -> 3; matrix products, arithmetic and copies ran while one was open for 2% -> 2% of each run, Pallas kernels for 10% -> 11%
where the time goes in v4:
time: 361 us; the launch traced here: 360 us
  waiting for transfers between devices  167 us (46%)
  Pallas kernels  81.1 us (22%)
  blocking collectives  65.6 us (18%)
  starting transfers between devices  35.3 us (10%)
  local copies, waits for them, and re-layouts  7.32 us (2%)
    all_to_all x2, waiting for transfers between devices, exchange(): lax.all_to_all(member, ('exp', 'grp', 'half'), split_axis=0, concat_axis=...  80.3 us
    all_to_all x1, blocking collectives, exchange(): lax.all_to_all(member, ('exp', 'grp', 'half'), split_axis=0, concat_axis=...  65.6 us
    all_to_all x1, waiting for transfers between devices, shards(): lax.all_to_all(parts, 'exp', split_axis=0, concat_axis=0, tiled=True)  51.3 us
    ppermute x1, waiting for transfers between devices, shards(): lax.ppermute(final, ('grp', 'exp'), [(g * members + e, e * members + g) f...  35 us
    pallas_call x1, Pallas kernels, delta(): pl.pallas_call(delta_kernel, grid_spec=pltpu.PrefetchScalarGridSpec(num_s...  25 us
    pallas_call x1, Pallas kernels, experts_of(): pl.pallas_call(functools.partial(head_kernel, ups=ups), in_specs=in_specs...  21.4 us
    pallas_call x1, Pallas kernels, experts_of(): pl.pallas_call(functools.partial(tail_kernel, ups=ups), in_specs=in_specs...  16 us
    all_to_all x2, starting transfers between devices, exchange(): lax.all_to_all(member, ('exp', 'grp', 'half'), split_axis=0, concat_axis=...  15.4 us
  transfers between devices with their start and end apart: 5, of which 3 were waited for; matrix products, arithmetic and copies ran while one was open for 2% of the time, Pallas kernels for 11%

profile of v4, /device:TPU:24, one launch (start us, length us, event | category | flops | bytes accessed | tf_op | source)
XLA Modules:
  0.0 360.3 jit_solution(3296614691716680857)
XLA Ops:
  0.6 25.0 %delta.1 = (bf16[8,128,2304]{2,1,0:T(8,128)(2,1)}, bf16[8,128,128]{2,1,0:T(8,128)(2,1)}) custom-call(s32[2]{0:T(128)} %counts.1, bf16[4096,128]{1,0:T(8,128)(2,1)} %bitcast.102, bf16[4096,128]{1,0:T(8,128)(2,1)} %bitcast.103, bf16[4096,128]{1,0:T(8,128)(2,1)} %bitcast.104, f32[4096,128]{1,0:T(8,128)} %bitcast.101, f32[2,4,512]{2,1,0:T(4,128)} %bitcast.106, ...), custom_call_target="tpu_custom_call" | custom-call | tf_op jit(solution)/shard_map/delta/pallas_call | solution.py:180
  25.6 0.0 copy-start.6
  25.6 0.0 copy-start.7
  25.6 7.3 %all-to-all-start = ((bf16[8,128,2304]{2,1,0:T(8,128)(2,1)}), bf16[8,128,2304]{2,1,0:T(8,128)(2,1)}, u32[]{:S(2)}, u32[]{:S(2)}) async-start(bf16[8,128,2304]{2,1,0:T(8,128)(2,1)} %get-tuple-element.14), calls=%async_computation | async-start | bytes 9437184 | tf_op jit(solution)/shard_map/all_to_all | solution.py:600
  32.9 0.1 copy.33
  33.0 0.3 reshape.150
  33.3 1.4 copy.34
  34.8 0.7 reshape.162.ids_ref
  35.4 0.6 reshape.161.gain_ref
  36.0 51.3 %all-to-all-done.part_ref = bf16[8,128,2304]{2,1,0:T(8,128)(2,1)} async-done(((bf16[8,128,2304]{2,1,0:T(8,128)(2,1)}), bf16[8,128,2304]{2,1,0:T(8,128)(2,1)}, u32[]{:S(2)}, u32[]{:S(2)}) %all-to-all-start) | async-done | bytes 4718624 | tf_op jit(solution)/shard_map/all_to_all | solution.py:600
  87.3 8.6 %route.1 = (f32[128,2304]{1,0:T(8,128)}, f32[128,128]{1,0:T(8,128)}, f32[128,128]{1,0:T(8,128)}, bf16[1024,2304]{1,0:T(8,128)(2,1)}, bf16[1024,1152]{1,0:T(8,128)(2,1)}) custom-call(bf16[2304,128]{1,0:T(8,128)(2,1)} %bitcast.97, bf16[8,128,2304]{2,1,0:T(8,128)(2,1)} %all-to-all-done.part_ref, bf16[1,2304]{1,0:T(2,128)(2,1)} %reshape.161.gain_ref, ...), custom_call_target="tpu_custom_call" | custom-call | tf_op jit(solution)/shard_map/route/pallas_call | solution.py:321
  95.9 65.6 %all_to_all.25 = bf16[128,8,2304]{2,1,0:T(8,128)(2,1)} all-to-all(bf16[128,8,2304]{2,1,0:T(8,128)(2,1)} %bitcast.85), channel_id=1, replica_groups=mesh['half'=2,'grp'=8,'exp'=8] {'exp','grp','half'}, dimensions={0} | all-to-all | bytes 9437184 | tf_op jit(solution)/shard_map/all_to_all | solution.py:605
  161.5 6.4 %all-to-all-start.2 = ((bf16[128,8,1152]{2,1,0:T(8,128)(2,1)}), bf16[128,8,1152]{2,1,0:T(8,128)(2,1)S(1)}, u32[]{:S(2)}, u32[]{:S(2)}) async-start(bf16[128,8,1152]{2,1,0:T(8,128)(2,1)} %bitcast.96), calls=%async_computation.2 | async-start | bytes 4718592 | tf_op jit(solution)/shard_map/all_to_all | solution.py:605
  167.9 5.2 %collective-permute-start = (bf16[8,128,128]{2,1,0:T(8,128)(2,1)S(1)}, bf16[8,128,128]{2,1,0:T(8,128)(2,1)}, u32[]{:S(2)}, u32[]{:S(2)}) collective-permute-start(bf16[8,128,128]{2,1,0:T(8,128)(2,1)S(1)} %copy-done.9), channel_id=1, source_target_pairs={{0,0},{1,8},{2,16},{3,24},{4,32},{5,40},{6,48},{7,56},{8,1},{9,9},... | collective-permute-start | bytes 786440 | tf_op jit(solution)/shard_map/ppermute | solution.py:595
  173.1 35.0 %collective-permute-done = bf16[8,128,128]{2,1,0:T(8,128)(2,1)} collective-permute-done((bf16[8,128,128]{2,1,0:T(8,128)(2,1)S(1)}, bf16[8,128,128]{2,1,0:T(8,128)(2,1)}, u32[]{:S(2)}, u32[]{:S(2)}) %collective-permute-start) | collective-permute-done | bytes 262176 | tf_op jit(solution)/shard_map/ppermute | solution.py:595
  208.2 7.5 %all-to-all-start.4 = ((bf16[8,128,128]{2,1,0:T(8,128)(2,1)}), bf16[8,128,128]{2,1,0:T(8,128)(2,1)S(1)}, u32[]{:S(2)}, u32[]{:S(2)}) async-start(bf16[8,128,128]{2,1,0:T(8,128)(2,1)} %collective-permute-done), calls=%async_computation.4 | async-start | bytes 524288 | tf_op jit(solution)/shard_map/all_to_all | solution.py:617
  215.7 21.4 %experts_head.1.done_ref = bf16[1024,3456]{1,0:T(8,128)(2,1)} custom-call(bf16[1024,2304]{1,0:T(8,128)(2,1)} %bitcast.77, bf16[2304,1024]{1,0:T(8,128)(2,1)} %bitcast.78, bf16[2304,1024]{1,0:T(8,128)(2,1)} %bitcast.80, bf16[1024,2304]{1,0:T(8,128)(2,1)} %bitcast.82), custom_call_target="tpu_custom_call" | custom-call | tf_op jit(solution)/shard_map/experts_head/pallas_call | solution.py:446
  237.1 16.0 %experts_tail.1 = bf16[1024,3456]{1,0:T(8,128)(2,1)} custom-call(bf16[1024,1152]{1,0:T(8,128)(2,1)} %bitcast.84, bf16[2304,1024]{1,0:T(8,128)(2,1)} %bitcast.79, bf16[2304,1024]{1,0:T(8,128)(2,1)} %bitcast.81, bf16[1024,2304]{1,0:T(8,128)(2,1)} %bitcast.83, bf16[1024,3456]{1,0:T(8,128)(2,1)} %experts_head.1.done_ref), custom_call_target="tpu_custom_call", output_to_operand_aliasing={{}: (4, {})} | custom-call | tf_op jit(solution)/shard_map/experts_tail/pallas_call | solution.py:454
  253.2 0.0 copy-start.5
  253.2 0.0 copy-start.3
  253.2 0.0 copy-start.4
  253.2 8.9 %all-to-all-start.3 = ((bf16[128,8,3456]{2,1,0:T(8,128)(2,1)}), bf16[128,8,3456]{2,1,0:T(8,128)(2,1)}, u32[]{:S(2)}, u32[]{:S(2)}) async-start(bf16[128,8,3456]{2,1,0:T(8,128)(2,1)} %bitcast.76), calls=%async_computation.3 | async-start | bytes 14155776 | tf_op jit(solution)/shard_map/all_to_all | solution.py:605
  262.2 0.1 copy.41
  262.2 0.1 mul.175
  262.3 0.1 mul.176
  262.5 0.1 squeeze.24
  262.6 0.1 copy.42
  262.6 0.1 mul.195
  262.7 0.1 mul.196
  262.8 0.1 squeeze.25
  262.9 0.1 fusion.1
  263.1 0.1 convert_multiply_fusion.1
  263.3 0.2 multiply_reduce_fusion.3
  263.5 0.1 reduce_sum.54
  263.8 0.6 multiply_reduce_fusion.1
  264.4 0.1 reduce_sum.55
  264.6 0.4 multiply_reduce_fusion
  264.9 0.1 stack.10
  265.0 0.1 stack.9
  265.1 0.7 maximum_multiply_fusion
  265.8 0.1 fusion.3
  265.9 1.1 add_bitcast_fusion
  267.0 2.7 spread.1
  269.7 80.3 %all-to-all-done.3 = bf16[128,8,3456]{2,1,0:T(8,128)(2,1)} async-done(((bf16[128,8,3456]{2,1,0:T(8,128)(2,1)}), bf16[128,8,3456]{2,1,0:T(8,128)(2,1)}, u32[]{:S(2)}, u32[]{:S(2)}) %all-to-all-start.3) | async-done | bytes 7077920 | tf_op jit(solution)/shard_map/all_to_all | solution.py:605
  350.0 7.4 %combine.1 = bf16[2304,128]{1,0:T(8,128)(2,1)} custom-call(f32[128,2304]{1,0:T(8,128)} %get-tuple-element.15.mixed_ref, bf16[256,1024]{1,0:T(8,128)(2,1)} %get-tuple-element.18.heads, bf16[512,1024]{1,0:T(8,128)(2,1)} %get-tuple-element.19.tails, bf16[1024,3456]{1,0:T(8,128)(2,1)} %bitcast.25.head_ref.tail_ref, bf16[1024,3456]{1,0:T(8,128)(2,1)} %bitcast.25.head_ref.tail_ref), custom_call_target="tpu_custom_call" | custom-call | tf_op jit(solution)/shard_map/combine/pallas_call | solution.py:544
  357.4 1.2 copy.45
  358.6 0.3 reshape.170
  358.9 1.4 copy.43
  (33 shorter events, 0.4 us)
Async XLA Ops:
  25.6 7.3 %copy-start.1 = (bf16[64,2,2304]{2,1,0:T(2,128)(2,1)S(1)}, bf16[64,2,2304]{2,1,0:T(2,128)(2,1)}, u32[]{:S(2)}) copy-start(bf16[64,2,2304]{2,1,0:T(2,128)(2,1)} %param.20) | copy-start | bytes 1769476
  25.6 9.2 %copy-start.6 = (s32[64,2,8]{0,2,1:T(8,128)S(1)}, s32[64,2,8]{0,2,1:T(8,128)}, u32[]{:S(2)}) copy-start(s32[64,2,8]{0,2,1:T(8,128)} %param.31) | copy-start | bytes 12292
  25.6 9.8 %copy-start.7 = (bf16[2304]{0:T(1024)(128)(2,1)S(1)}, bf16[2304]{0:T(1024)(128)(2,1)}, u32[]{:S(2)}) copy-start(bf16[2304]{0:T(1024)(128)(2,1)} %param.29) | copy-start | bytes 13828
  25.6 61.7 %all-to-all-start = ((bf16[8,128,2304]{2,1,0:T(8,128)(2,1)}), bf16[8,128,2304]{2,1,0:T(8,128)(2,1)}, u32[]{:S(2)}, u32[]{:S(2)}) async-start(bf16[8,128,2304]{2,1,0:T(8,128)(2,1)} %get-tuple-element.14), calls=%async_computation | async-start | bytes 9437184 | tf_op jit(solution)/shard_map/all_to_all | solution.py:600
  161.5 6.4 %copy-start.9 = (bf16[8,128,128]{2,1,0:T(8,128)(2,1)S(1)}, bf16[8,128,128]{2,1,0:T(8,128)(2,1)}, u32[]{:S(2)}) copy-start(bf16[8,128,128]{2,1,0:T(8,128)(2,1)} %get-tuple-element.24) | copy-start | bytes 786436
  161.5 46.7 %all-to-all-start.2 = ((bf16[128,8,1152]{2,1,0:T(8,128)(2,1)}), bf16[128,8,1152]{2,1,0:T(8,128)(2,1)S(1)}, u32[]{:S(2)}, u32[]{:S(2)}) async-start(bf16[128,8,1152]{2,1,0:T(8,128)(2,1)} %bitcast.96), calls=%async_computation.2 | async-start | bytes 4718592 | tf_op jit(solution)/shard_map/all_to_all | solution.py:605
  167.9 40.2 %collective-permute-start = (bf16[8,128,128]{2,1,0:T(8,128)(2,1)S(1)}, bf16[8,128,128]{2,1,0:T(8,128)(2,1)}, u32[]{:S(2)}, u32[]{:S(2)}) collective-permute-start(bf16[8,128,128]{2,1,0:T(8,128)(2,1)S(1)} %copy-done.9), channel_id=1, source_target_pairs={{0,0},{1,8},{2,16},{3,24},{4,32},{5,40},{6,48},{7,56},{8,1},{9,9},... | collective-permute-start | bytes 786440 | tf_op jit(solution)/shard_map/ppermute | solution.py:595
  208.2 28.9 %copy-start = (bf16[128,8,1152]{2,1,0:T(8,128)(2,1)}, bf16[128,8,1152]{2,1,0:T(8,128)(2,1)S(1)}, u32[]{:S(2)}) copy-start(bf16[128,8,1152]{2,1,0:T(8,128)(2,1)S(1)} %all-to-all-done.2) | copy-start | bytes 7077892
  208.2 45.0 %all-to-all-start.4 = ((bf16[8,128,128]{2,1,0:T(8,128)(2,1)}), bf16[8,128,128]{2,1,0:T(8,128)(2,1)S(1)}, u32[]{:S(2)}, u32[]{:S(2)}) async-start(bf16[8,128,128]{2,1,0:T(8,128)(2,1)} %collective-permute-done), calls=%async_computation.4 | async-start | bytes 524288 | tf_op jit(solution)/shard_map/all_to_all | solution.py:617
  253.2 9.0 %copy-start.8 = (f32[16,2,4]{0,2,1:T(4,128)S(1)}, f32[16,2,4]{0,2,1:T(4,128)}, u32[]{:S(2)}) copy-start(f32[16,2,4]{0,2,1:T(4,128)} %param.39) | copy-start | bytes 1540
  253.2 9.3 %copy-start.2 = (bf16[16,2,4,16]{3,2,1,0:T(4,128)(2,1)S(1)}, bf16[16,2,4,16]{3,2,1,0:T(4,128)(2,1)}, u32[]{:S(2)}) copy-start(bf16[16,2,4,16]{3,2,1,0:T(4,128)(2,1)} %param.37) | copy-start | bytes 12292
  253.2 9.4 %copy-start.5 = (bf16[16,2,4,128]{3,2,1,0:T(4,128)(2,1)S(1)}, bf16[16,2,4,128]{3,2,1,0:T(4,128)(2,1)}, u32[]{:S(2)}) copy-start(bf16[16,2,4,128]{3,2,1,0:T(4,128)(2,1)} %param.35) | copy-start | bytes 98308
  253.2 9.7 %copy-start.3 = (bf16[16,2,4,128]{3,2,1,0:T(4,128)(2,1)S(1)}, bf16[16,2,4,128]{3,2,1,0:T(4,128)(2,1)}, u32[]{:S(2)}) copy-start(bf16[16,2,4,128]{3,2,1,0:T(4,128)(2,1)} %param.36) | copy-start | bytes 98308
  253.2 10.0 %copy-start.4 = (f32[16,2,4,128]{3,2,1,0:T(4,128)S(1)}, f32[16,2,4,128]{3,2,1,0:T(4,128)}, u32[]{:S(2)}) copy-start(f32[16,2,4,128]{3,2,1,0:T(4,128)} %param.38) | copy-start | bytes 196612
  253.2 96.8 %all-to-all-start.3 = ((bf16[128,8,3456]{2,1,0:T(8,128)(2,1)}), bf16[128,8,3456]{2,1,0:T(8,128)(2,1)}, u32[]{:S(2)}, u32[]{:S(2)}) async-start(bf16[128,8,3456]{2,1,0:T(8,128)(2,1)} %bitcast.76), calls=%async_computation.3 | async-start | bytes 14155776 | tf_op jit(solution)/shard_map/all_to_all | solution.py:605

commit v5 on v4

--- a/solution.py
+++ b/solution.py
@@ -206,6 +206,7 @@
             jax.ShapeDtypeStruct((members, chains * value_dim // members, key_dim), BF16),
         ],
         compiler_params=pltpu.CompilerParams(vmem_limit_bytes=VMEM),
+        cost_estimate=pl.CostEstimate(flops=8 * 10**9, bytes_accessed=16 * 10**6, transcendentals=0),
         name="delta",
     )(
         counts,
@@ -337,6 +338,7 @@
             jax.ShapeDtypeStruct((experts * 8, width // 2), BF16),
         ],
         compiler_params=pltpu.CompilerParams(vmem_limit_bytes=VMEM),
+        cost_estimate=pl.CostEstimate(flops=2 * 10**9, bytes_accessed=14 * 10**6, transcendentals=0),
         name="route",
     )(interleave(residual), parts, norm_gain.reshape(1, width), w_router, ids)
 
@@ -448,6 +450,7 @@
             in_specs=in_specs,
             out_specs=pl.BlockSpec((rows, tile), later),
             scratch_shapes=[pltpu.VMEM((rows, hidden), BF16)],
+            cost_estimate=pl.CostEstimate(flops=6 * rows * width * hidden, bytes_accessed=4 * rows * width + 6 * width * hidden, transcendentals=0),
             name="experts_head",
             **common,
         )(arrived, gate, up, down)
@@ -461,6 +464,7 @@
             pltpu.VMEM((tails, hidden), BF16),
         ],
         input_output_aliases={4: 0},
+        cost_estimate=pl.CostEstimate(flops=6 * tails * width * hidden, bytes_accessed=4 * tails * width + 6 * width * hidden, transcendentals=0),
         name="experts_tail",
         **common,
     )(arrived, gate, up, down, done)
@@ -495,6 +499,7 @@
             jax.ShapeDtypeStruct((4 * tokens, rows), BF16),
         ],
         compiler_params=pltpu.CompilerParams(vmem_limit_bytes=VMEM),
+        cost_estimate=pl.CostEstimate(flops=10**9, bytes_accessed=2 * 10**6, transcendentals=0),
         name="spread",
     )(slot, weight)
 
@@ -558,6 +563,7 @@
         ],
         out_shape=jax.ShapeDtypeStruct((lines, LANES), BF16),
         compiler_params=pltpu.CompilerParams(vmem_limit_bytes=VMEM),
+        cost_estimate=pl.CostEstimate(flops=4 * 10**9, bytes_accessed=11 * 10**6, transcendentals=0),
         name="combine",
     )(mixed, heads, tails, back, back)
 

time: 361 us -> 339 us (0.939)
  waiting for transfers between devices: 167 us -> 145 us
    ppermute x1, waiting for transfers between devices: 35 us -> 13.6 us  [shards(): lax.ppermute(final, ('grp', 'exp'), [(g * members + e, e * members + g) f...]
  transfers between devices with their start and end apart: 5 -> 5, of which waited for: 3 -> 3; matrix products, arithmetic and copies ran while one was open for 2% -> 2% of each run, Pallas kernels for 11% -> 12%
where the time goes in v5:
time: 339 us
  waiting for transfers between devices  145 us (43%)
  Pallas kernels  81.1 us (24%)
  blocking collectives  65.6 us (19%)
  starting transfers between devices  35.3 us (10%)
  local copies, waits for them, and re-layouts  7.32 us (2%)
    all_to_all x2, waiting for transfers between devices, exchange(): lax.all_to_all(member, ('exp', 'grp', 'half'), split_axis=0, concat_axis=...  80 us
    all_to_all x1, blocking collectives, exchange(): lax.all_to_all(member, ('exp', 'grp', 'half'), split_axis=0, concat_axis=...  65.6 us
    all_to_all x1, waiting for transfers between devices, shards(): lax.all_to_all(parts, 'exp', split_axis=0, concat_axis=0, tiled=True)  51.3 us
    pallas_call x1, Pallas kernels, delta(): pl.pallas_call(delta_kernel, grid_spec=pltpu.PrefetchScalarGridSpec(num_s...  25 us
    pallas_call x1, Pallas kernels, experts_of(): pl.pallas_call(functools.partial(head_kernel, ups=ups), in_specs=in_specs...  21.5 us
    pallas_call x1, Pallas kernels, experts_of(): pl.pallas_call(functools.partial(tail_kernel, ups=ups), in_specs=in_specs...  16 us
    all_to_all x2, starting transfers between devices, exchange(): lax.all_to_all(member, ('exp', 'grp', 'half'), split_axis=0, concat_axis=...  15.3 us
    ppermute x1, waiting for transfers between devices, shards(): lax.ppermute(final, ('grp', 'exp'), [(g * members + e, e * members + g) f...  13.6 us
  transfers between devices with their start and end apart: 5, of which 3 were waited for; matrix products, arithmetic and copies ran while one was open for 2% of the time, Pallas kernels for 12%

profile of v5, /device:TPU:24, one launch (start us, length us, event | category | flops | bytes accessed | tf_op | source)
XLA Modules:
  0.0 338.5 jit_solution(11049739799378843898)
XLA Ops:
  0.6 25.0 %delta.1 = (bf16[8,128,2304]{2,1,0:T(8,128)(2,1)}, bf16[8,128,128]{2,1,0:T(8,128)(2,1)}) custom-call(s32[2]{0:T(128)} %counts.1, bf16[4096,128]{1,0:T(8,128)(2,1)} %bitcast.103, bf16[4096,128]{1,0:T(8,128)(2,1)} %bitcast.104, bf16[4096,128]{1,0:T(8,128)(2,1)} %bitcast.105, f32[4096,128]{1,0:T(8,128)} %bitcast.102, f32[2,4,512]{2,1,0:T(4,128)} %bitcast.107, ...), custom_call_target="tpu_custom_call" | custom-call | flops 8000000000 | bytes 16000000 | tf_op jit(solution)/shard_map/delta/pallas_call | solution.py:180
  25.6 0.0 copy-start.6
  25.6 0.0 copy-start.7
  25.6 7.3 %all-to-all-start = ((bf16[8,128,2304]{2,1,0:T(8,128)(2,1)}), bf16[8,128,2304]{2,1,0:T(8,128)(2,1)}, u32[]{:S(2)}, u32[]{:S(2)}) async-start(bf16[8,128,2304]{2,1,0:T(8,128)(2,1)} %get-tuple-element.14), calls=%async_computation | async-start | bytes 9437184 | tf_op jit(solution)/shard_map/all_to_all | solution.py:606
  32.9 0.1 copy.33
  33.0 0.3 reshape.150
  33.3 1.4 copy.34
  34.8 0.7 reshape.162.ids_ref
  35.4 0.6 reshape.161.gain_ref
  36.0 51.3 %all-to-all-done.part_ref = bf16[8,128,2304]{2,1,0:T(8,128)(2,1)} async-done(((bf16[8,128,2304]{2,1,0:T(8,128)(2,1)}), bf16[8,128,2304]{2,1,0:T(8,128)(2,1)}, u32[]{:S(2)}, u32[]{:S(2)}) %all-to-all-start) | async-done | bytes 4718624 | tf_op jit(solution)/shard_map/all_to_all | solution.py:606
  87.3 8.6 %route.1 = (f32[128,2304]{1,0:T(8,128)}, f32[128,128]{1,0:T(8,128)}, f32[128,128]{1,0:T(8,128)}, bf16[1024,2304]{1,0:T(8,128)(2,1)}, bf16[1024,1152]{1,0:T(8,128)(2,1)}) custom-call(bf16[2304,128]{1,0:T(8,128)(2,1)} %bitcast.100, bf16[8,128,2304]{2,1,0:T(8,128)(2,1)} %all-to-all-done.part_ref, bf16[1,2304]{1,0:T(2,128)(2,1)} %reshape.161.gain_ref, ...), custom_call_target="tpu_custom_call" | custom-call | flops 2000000000 | bytes 14000000 | tf_op jit(solution)/shard_map/route/pallas_call | solution.py:322
  95.9 65.6 %all_to_all.25 = bf16[128,8,2304]{2,1,0:T(8,128)(2,1)} all-to-all(bf16[128,8,2304]{2,1,0:T(8,128)(2,1)} %bitcast.79), channel_id=1, replica_groups=mesh['half'=2,'grp'=8,'exp'=8] {'exp','grp','half'}, dimensions={0} | all-to-all | bytes 9437184 | tf_op jit(solution)/shard_map/all_to_all | solution.py:611
  161.5 6.4 %all-to-all-start.2 = ((bf16[128,8,1152]{2,1,0:T(8,128)(2,1)}), bf16[128,8,1152]{2,1,0:T(8,128)(2,1)S(1)}, u32[]{:S(2)}, u32[]{:S(2)}) async-start(bf16[128,8,1152]{2,1,0:T(8,128)(2,1)} %bitcast.96), calls=%async_computation.2 | async-start | bytes 4718592 | tf_op jit(solution)/shard_map/all_to_all | solution.py:611
  168.0 5.2 %collective-permute-start = (bf16[8,128,128]{2,1,0:T(8,128)(2,1)S(1)}, bf16[8,128,128]{2,1,0:T(8,128)(2,1)}, u32[]{:S(2)}, u32[]{:S(2)}) collective-permute-start(bf16[8,128,128]{2,1,0:T(8,128)(2,1)S(1)} %copy-done.9), channel_id=1, source_target_pairs={{0,0},{1,8},{2,16},{3,24},{4,32},{5,40},{6,48},{7,56},{8,1},{9,9},... | collective-permute-start | bytes 786440 | tf_op jit(solution)/shard_map/ppermute | solution.py:601
  173.2 21.5 %experts_head.1.done_ref = bf16[1024,3456]{1,0:T(8,128)(2,1)} custom-call(bf16[1024,2304]{1,0:T(8,128)(2,1)} %bitcast.78, bf16[2304,1024]{1,0:T(8,128)(2,1)} %bitcast.86, bf16[2304,1024]{1,0:T(8,128)(2,1)} %bitcast.88, bf16[1024,2304]{1,0:T(8,128)(2,1)} %bitcast.90), custom_call_target="tpu_custom_call" | custom-call | flops 14495514624 | bytes 23592960 | tf_op jit(solution)/shard_map/experts_head/pallas_call | solution.py:448
  194.6 13.6 %collective-permute-done = bf16[8,128,128]{2,1,0:T(8,128)(2,1)} collective-permute-done((bf16[8,128,128]{2,1,0:T(8,128)(2,1)S(1)}, bf16[8,128,128]{2,1,0:T(8,128)(2,1)}, u32[]{:S(2)}, u32[]{:S(2)}) %collective-permute-start) | collective-permute-done | bytes 262176 | tf_op jit(solution)/shard_map/ppermute | solution.py:601
  208.2 7.5 %all-to-all-start.4 = ((bf16[8,128,128]{2,1,0:T(8,128)(2,1)}), bf16[8,128,128]{2,1,0:T(8,128)(2,1)S(1)}, u32[]{:S(2)}, u32[]{:S(2)}) async-start(bf16[8,128,128]{2,1,0:T(8,128)(2,1)} %collective-permute-done), calls=%async_computation.4 | async-start | bytes 524288 | tf_op jit(solution)/shard_map/all_to_all | solution.py:623
  215.7 16.0 %experts_tail.1 = bf16[1024,3456]{1,0:T(8,128)(2,1)} custom-call(bf16[1024,1152]{1,0:T(8,128)(2,1)} %bitcast.77, bf16[2304,1024]{1,0:T(8,128)(2,1)} %bitcast.87, bf16[2304,1024]{1,0:T(8,128)(2,1)} %bitcast.89, bf16[1024,2304]{1,0:T(8,128)(2,1)} %bitcast.91, bf16[1024,3456]{1,0:T(8,128)(2,1)} %experts_head.1.done_ref), custom_call_target="tpu_custom_call", output_to_operand_aliasing={{}: (4, {})} | custom-call | flops 7247757312 | bytes 18874368 | tf_op jit(solution)/shard_map/experts_tail/pallas_call | solution.py:457
  231.7 0.0 copy-start.5
  231.7 0.0 copy-start.3
  231.8 0.0 copy-start.4
  231.8 8.9 %all-to-all-start.3 = ((bf16[128,8,3456]{2,1,0:T(8,128)(2,1)}), bf16[128,8,3456]{2,1,0:T(8,128)(2,1)}, u32[]{:S(2)}, u32[]{:S(2)}) async-start(bf16[128,8,3456]{2,1,0:T(8,128)(2,1)} %bitcast.76), calls=%async_computation.3 | async-start | bytes 14155776 | tf_op jit(solution)/shard_map/all_to_all | solution.py:611
  240.7 0.1 copy.41
  240.8 0.1 mul.175
  240.9 0.1 mul.176
  241.0 0.1 squeeze.24
  241.1 0.1 copy.42
  241.2 0.1 mul.195
  241.3 0.1 mul.196
  241.4 0.1 squeeze.25
  241.5 0.1 fusion.1
  241.6 0.1 convert_multiply_fusion.1
  241.9 0.2 multiply_reduce_fusion.3
  242.1 0.1 reduce_sum.54
  242.3 0.6 multiply_reduce_fusion.1
  243.0 0.1 reduce_sum.55
  243.1 0.4 multiply_reduce_fusion
  243.5 0.1 stack.10
  243.6 0.1 stack.9
  243.7 0.7 maximum_multiply_fusion
  244.3 0.1 fusion.3
  244.4 1.1 add_bitcast_fusion
  245.6 2.7 spread.1
  248.2 80.0 %all-to-all-done.3 = bf16[128,8,3456]{2,1,0:T(8,128)(2,1)} async-done(((bf16[128,8,3456]{2,1,0:T(8,128)(2,1)}), bf16[128,8,3456]{2,1,0:T(8,128)(2,1)}, u32[]{:S(2)}, u32[]{:S(2)}) %all-to-all-start.3) | async-done | bytes 7077920 | tf_op jit(solution)/shard_map/all_to_all | solution.py:611
  328.2 7.4 %combine.1 = bf16[2304,128]{1,0:T(8,128)(2,1)} custom-call(f32[128,2304]{1,0:T(8,128)} %get-tuple-element.15.mixed_ref, bf16[256,1024]{1,0:T(8,128)(2,1)} %get-tuple-element.18.heads, bf16[512,1024]{1,0:T(8,128)(2,1)} %get-tuple-element.19.tails, bf16[1024,3456]{1,0:T(8,128)(2,1)} %bitcast.25.head_ref.tail_ref, bf16[1024,3456]{1,0:T(8,128)(2,1)} %bitcast.25.head_ref.tail_ref), custom_call_target="tpu_custom_call" | custom-call | flops 4000000000 | bytes 11000000 | tf_op jit(solution)/shard_map/combine/pallas_call | solution.py:549
  335.6 1.2 copy.45
  336.8 0.3 reshape.170
  337.1 1.4 copy.43
  (33 shorter events, 0.4 us)
Async XLA Ops:
  25.6 7.3 %copy-start.1 = (bf16[64,2,2304]{2,1,0:T(2,128)(2,1)S(1)}, bf16[64,2,2304]{2,1,0:T(2,128)(2,1)}, u32[]{:S(2)}) copy-start(bf16[64,2,2304]{2,1,0:T(2,128)(2,1)} %param.20) | copy-start | bytes 1769476
  25.6 9.2 %copy-start.6 = (s32[64,2,8]{0,2,1:T(8,128)S(1)}, s32[64,2,8]{0,2,1:T(8,128)}, u32[]{:S(2)}) copy-start(s32[64,2,8]{0,2,1:T(8,128)} %param.31) | copy-start | bytes 12292
  25.6 9.8 %copy-start.7 = (bf16[2304]{0:T(1024)(128)(2,1)S(1)}, bf16[2304]{0:T(1024)(128)(2,1)}, u32[]{:S(2)}) copy-start(bf16[2304]{0:T(1024)(128)(2,1)} %param.29) | copy-start | bytes 13828
  25.6 61.7 %all-to-all-start = ((bf16[8,128,2304]{2,1,0:T(8,128)(2,1)}), bf16[8,128,2304]{2,1,0:T(8,128)(2,1)}, u32[]{:S(2)}, u32[]{:S(2)}) async-start(bf16[8,128,2304]{2,1,0:T(8,128)(2,1)} %get-tuple-element.14), calls=%async_computation | async-start | bytes 9437184 | tf_op jit(solution)/shard_map/all_to_all | solution.py:606
  161.5 6.4 %copy-start.9 = (bf16[8,128,128]{2,1,0:T(8,128)(2,1)S(1)}, bf16[8,128,128]{2,1,0:T(8,128)(2,1)}, u32[]{:S(2)}) copy-start(bf16[8,128,128]{2,1,0:T(8,128)(2,1)} %get-tuple-element.24) | copy-start | bytes 786436
  161.5 46.7 %all-to-all-start.2 = ((bf16[128,8,1152]{2,1,0:T(8,128)(2,1)}), bf16[128,8,1152]{2,1,0:T(8,128)(2,1)S(1)}, u32[]{:S(2)}, u32[]{:S(2)}) async-start(bf16[128,8,1152]{2,1,0:T(8,128)(2,1)} %bitcast.96), calls=%async_computation.2 | async-start | bytes 4718592 | tf_op jit(solution)/shard_map/all_to_all | solution.py:611
  168.0 40.2 %collective-permute-start = (bf16[8,128,128]{2,1,0:T(8,128)(2,1)S(1)}, bf16[8,128,128]{2,1,0:T(8,128)(2,1)}, u32[]{:S(2)}, u32[]{:S(2)}) collective-permute-start(bf16[8,128,128]{2,1,0:T(8,128)(2,1)S(1)} %copy-done.9), channel_id=1, source_target_pairs={{0,0},{1,8},{2,16},{3,24},{4,32},{5,40},{6,48},{7,56},{8,1},{9,9},... | collective-permute-start | bytes 786440 | tf_op jit(solution)/shard_map/ppermute | solution.py:601
  208.2 7.5 %copy-start = (bf16[128,8,1152]{2,1,0:T(8,128)(2,1)}, bf16[128,8,1152]{2,1,0:T(8,128)(2,1)S(1)}, u32[]{:S(2)}) copy-start(bf16[128,8,1152]{2,1,0:T(8,128)(2,1)S(1)} %all-to-all-done.2) | copy-start | bytes 7077892
  208.2 23.5 %all-to-all-start.4 = ((bf16[8,128,128]{2,1,0:T(8,128)(2,1)}), bf16[8,128,128]{2,1,0:T(8,128)(2,1)S(1)}, u32[]{:S(2)}, u32[]{:S(2)}) async-start(bf16[8,128,128]{2,1,0:T(8,128)(2,1)} %collective-permute-done), calls=%async_computation.4 | async-start | bytes 524288 | tf_op jit(solution)/shard_map/all_to_all | solution.py:623
  231.7 9.0 %copy-start.8 = (f32[16,2,4]{0,2,1:T(4,128)S(1)}, f32[16,2,4]{0,2,1:T(4,128)}, u32[]{:S(2)}) copy-start(f32[16,2,4]{0,2,1:T(4,128)} %param.39) | copy-start | bytes 1540
  231.7 9.3 %copy-start.2 = (bf16[16,2,4,16]{3,2,1,0:T(4,128)(2,1)S(1)}, bf16[16,2,4,16]{3,2,1,0:T(4,128)(2,1)}, u32[]{:S(2)}) copy-start(bf16[16,2,4,16]{3,2,1,0:T(4,128)(2,1)} %param.37) | copy-start | bytes 12292
  231.7 9.4 %copy-start.5 = (bf16[16,2,4,128]{3,2,1,0:T(4,128)(2,1)S(1)}, bf16[16,2,4,128]{3,2,1,0:T(4,128)(2,1)}, u32[]{:S(2)}) copy-start(bf16[16,2,4,128]{3,2,1,0:T(4,128)(2,1)} %param.35) | copy-start | bytes 98308
  231.7 9.7 %copy-start.3 = (bf16[16,2,4,128]{3,2,1,0:T(4,128)(2,1)S(1)}, bf16[16,2,4,128]{3,2,1,0:T(4,128)(2,1)}, u32[]{:S(2)}) copy-start(bf16[16,2,4,128]{3,2,1,0:T(4,128)(2,1)} %param.36) | copy-start | bytes 98308
  231.8 10.0 %copy-start.4 = (f32[16,2,4,128]{3,2,1,0:T(4,128)S(1)}, f32[16,2,4,128]{3,2,1,0:T(4,128)}, u32[]{:S(2)}) copy-start(f32[16,2,4,128]{3,2,1,0:T(4,128)} %param.38) | copy-start | bytes 196612
  231.8 96.5 %all-to-all-start.3 = ((bf16[128,8,3456]{2,1,0:T(8,128)(2,1)}), bf16[128,8,3456]{2,1,0:T(8,128)(2,1)}, u32[]{:S(2)}, u32[]{:S(2)}) async-start(bf16[128,8,3456]{2,1,0:T(8,128)(2,1)} %bitcast.76), calls=%async_computation.3 | async-start | bytes 14155776 | tf_op jit(solution)/shard_map/all_to_all | solution.py:611

commit v6 on v5

--- a/solution.py
+++ b/solution.py
@@ -380,7 +380,7 @@
 
 
 def tail_kernel(
-    x_ref, gate_ref, up_ref, down_ref, done_ref, out_ref, lines_in, lines_out, inner, *, ups
+    x_ref, gate_ref, up_ref, down_ref, out_ref, lines_in, lines_out, inner, *, ups
 ):
     step = pl.program_id(0)
     rows, half = x_ref.shape
@@ -420,7 +420,7 @@
             out_ref[pl.ds(group * GROUP, GROUP), :] = dot(order, moved, TN).astype(BF16)
 
 
-def experts_of(arrived, gate, up, down, done=None):
+def experts_of(arrived, gate, up, down):
     rows = arrived.shape[0]
     width, hidden = gate.shape
     fold, tile = 256, 768
@@ -441,10 +441,10 @@
     ]
     common = dict(
         grid=(ups + downs,),
-        out_shape=jax.ShapeDtypeStruct((rows, width * 3 // 2), BF16),
+        out_shape=jax.ShapeDtypeStruct(arrived.shape, BF16),
         compiler_params=pltpu.CompilerParams(vmem_limit_bytes=VMEM),
     )
-    if done is None:
+    if arrived.shape[1] == width:
         return pl.pallas_call(
             functools.partial(head_kernel, ups=ups),
             in_specs=in_specs,
@@ -456,18 +456,17 @@
         )(arrived, gate, up, down)
     return pl.pallas_call(
         functools.partial(tail_kernel, ups=ups),
-        in_specs=in_specs + [pl.BlockSpec(memory_space=pl.ANY)],
-        out_specs=pl.BlockSpec((rows, width // 2), lambda step: (0, 2)),
+        in_specs=in_specs,
+        out_specs=pl.BlockSpec(arrived.shape, lambda step: (0, 0)),
         scratch_shapes=[
             pltpu.VMEM((tails, width), BF16),
             pltpu.VMEM((tails, width), BF16),
             pltpu.VMEM((tails, hidden), BF16),
         ],
-        input_output_aliases={4: 0},
         cost_estimate=pl.CostEstimate(flops=6 * tails * width * hidden, bytes_accessed=4 * tails * width + 6 * width * hidden, transcendentals=0),
         name="experts_tail",
         **common,
-    )(arrived, gate, up, down, done)
+    )(arrived, gate, up, down)
 
 
 def spread_kernel(slot_ref, weight_ref, heads, tails):
@@ -504,68 +503,76 @@
     )(slot, weight)
 
 
-def combine_kernel(mixed_ref, heads, tails, head_ref, tail_ref, out_ref, total, wide):
+def add_kernel(mixed_ref, heads, back_ref, total_ref):
+    tokens = mixed_ref.shape[0]
+    both = dot(heads[...], back_ref[...])
+    total_ref[...] = mixed_ref[...] + both[:tokens] + both[tokens:]
+
+
+def add_heads(mixed, heads, back):
+    tokens, width = mixed.shape
+    tile = 768
+    column = pl.BlockSpec((tokens, tile), lambda step: (0, step))
+    return pl.pallas_call(
+        add_kernel,
+        grid=(width // tile,),
+        in_specs=[
+            column,
+            pl.BlockSpec(heads.shape, lambda step: (0, 0)),
+            pl.BlockSpec((back.shape[0], tile), lambda step: (0, step)),
+        ],
+        out_specs=column,
+        out_shape=jax.ShapeDtypeStruct((tokens, width), F32),
+        compiler_params=pltpu.CompilerParams(vmem_limit_bytes=VMEM),
+        cost_estimate=pl.CostEstimate(
+            flops=3 * 10**9, bytes_accessed=8 * 10**6, transcendentals=0
+        ),
+        name="add_heads",
+    )(mixed, heads, back)
+
+
+def combine_kernel(total_ref, tails, back_ref, out_ref):
     step = pl.program_id(0)
-    tokens, width = mixed_ref.shape
+    tokens, width = total_ref.shape
     requests = tokens // BLOCK
-    chunks = width // LANES
     half = width // 2
-
-    @pl.when(step == 0)
-    def _():
-        total[...] = mixed_ref[...]
-
-    tile, thin = head_ref.shape[1], tail_ref.shape[1]
-    lanes = pl.ds(pl.multiple_of(step * tile, tile), tile)
-    both = dot(heads[...], head_ref[...])
-    total[:, lanes] += both[:tokens] + both[tokens:]
-    both = dot(tails[...], tail_ref[...])
+    thin = back_ref.shape[1]
+    both = dot(tails[...], back_ref[...])
     for side in range(2):
         lanes = pl.ds(pl.multiple_of(side * half + step * thin, thin), thin)
         first = 2 * side * tokens
-        total[:, lanes] += both[first : first + tokens] + both[first + tokens : first + 2 * tokens]
-
-    @pl.when(step == pl.num_programs(0) - 1)
-    def _():
-        for chunk in range(chunks):
-            for r in range(requests):
-                rows_here = pl.ds(chunk * requests + r, BLOCK, stride=chunks * requests)
-                wide[rows_here, :] = total[
-                    r * BLOCK : (r + 1) * BLOCK, chunk * LANES : (chunk + 1) * LANES
-                ]
-        out_ref[...] = wide[...].astype(BF16)
-
-
-def combine(mixed, heads, tails, back):
-    tokens, width = mixed.shape
-    rows, across = back.shape
-    tile, thin = 768, 384
-    steps = width // tile
-
-    def whole(member):
-        return pl.BlockSpec(member.shape, lambda step: (0,) * member.ndim)
-
-    lines = tokens * width // LANES
+        done = (
+            total_ref[:, lanes]
+            + both[first : first + tokens]
+            + both[first + tokens : first + 2 * tokens]
+        )
+        pieces = [done[r * BLOCK : (r + 1) * BLOCK] for r in range(requests)]
+        out_ref[:, :, lanes] = jnp.stack(pieces, axis=1).astype(BF16)
+
+
+def combine(total, tails, back):
+    tokens, width = total.shape
+    thin = 384
+
+    def whole(*shape):
+        return pl.BlockSpec(shape, lambda step: (0,) * len(shape))
+
     return pl.pallas_call(
         combine_kernel,
-        grid=(steps,),
+        grid=(width // 2 // thin,),
         in_specs=[
-            whole(mixed),
-            whole(heads),
-            whole(tails),
-            pl.BlockSpec((rows, tile), lambda step: (0, step)),
-            pl.BlockSpec((rows, thin), lambda step: (0, width // thin + step)),
+            whole(*total.shape),
+            whole(*tails.shape),
+            pl.BlockSpec((back.shape[0], thin), lambda step: (0, step)),
         ],
-        out_specs=pl.BlockSpec((lines, LANES), lambda step: (0, 0)),
-        scratch_shapes=[
-            pltpu.VMEM((tokens, width), F32),
-            pltpu.VMEM((lines, LANES), F32),
-        ],
-        out_shape=jax.ShapeDtypeStruct((lines, LANES), BF16),
+        out_specs=whole(BLOCK, tokens // BLOCK, width),
+        out_shape=jax.ShapeDtypeStruct((BLOCK, tokens // BLOCK, width), BF16),
         compiler_params=pltpu.CompilerParams(vmem_limit_bytes=VMEM),
-        cost_estimate=pl.CostEstimate(flops=4 * 10**9, bytes_accessed=11 * 10**6, transcendentals=0),
+        cost_estimate=pl.CostEstimate(
+            flops=2 * 10**9, bytes_accessed=6 * 10**6, transcendentals=0
+        ),
         name="combine",
-    )(mixed, heads, tails, back, back)
+    )(total, tails, back)
 
 
 def decode(relaid, dec_query, dec_key, dec_value, dec_decay, dec_beta):
@@ -590,7 +597,7 @@
     norm_gain, w_router, expert_ids, w_gate, w_up, w_down,
     dec_query, dec_key, dec_value, dec_decay, dec_beta,
 ):
-    rows_here, requests, width = residual.shape
+    requests = residual.shape[1]
     heads, key_dim, value_dim = init_state.shape[1:]
     members = lax.axis_size("exp")
     experts = w_router.shape[1]
@@ -618,15 +625,17 @@
     tail = exchange(tail)
     heads_of, tails_of = spread_of(slot, weight)
     matrices = (w_gate[0], w_up[0], w_down[0])
-    back = exchange(experts_of(tail, *matrices, done=experts_of(head, *matrices)))
-
+    head, tail, final = lax.optimization_barrier((experts_of(head, *matrices), tail, final))
     relaid = lax.all_to_all(final, "exp", split_axis=0, concat_axis=0, tiled=True)
+    head, relaid = lax.optimization_barrier((head, relaid))
+    head = exchange(head)
+    head, tail = lax.optimization_barrier((head, experts_of(tail, *matrices)))
+    tail = exchange(tail)
     relaid = relaid.reshape(groups * requests, heads, value_dim // members, key_dim)
     dec_out, dec_state = decode(relaid, dec_query, dec_key, dec_value, dec_decay, dec_beta)
 
-    hidden = combine(mixed, heads_of, tails_of, back)
-    hidden = hidden.reshape(rows_here, width // LANES, requests, LANES).transpose(0, 2, 1, 3)
-    return hidden.reshape(rows_here, requests, width), dec_out, dec_state
+    hidden = combine(add_heads(mixed, heads_of, head), tails_of, tail)
+    return hidden, dec_out, dec_state
 
 
 def solution(mesh):

time: 339 us -> 334 us (0.985); the launches traced: 339 us -> 330 us
  waiting for transfers between devices: 145 us -> 124 us
  blocking collectives: 65.6 us -> 79.2 us
  Pallas kernels: 81.1 us -> 84.9 us
    all_to_all x2 -> x3, waiting for transfers between devices: 80 us -> 59.4 us  [exchange(): lax.all_to_all(member, ('exp', 'grp', 'half'), split_axis=0, concat_axis=...]
    all_to_all x0 -> x1, blocking collectives: none -> 13.6 us  [shards(): lax.all_to_all(final, 'exp', split_axis=0, concat_axis=0, tiled=True)]
    all_to_all x1 -> x0, starting transfers between devices: 7.48 us -> none  [shards(): lax.all_to_all(final, 'exp', split_axis=0, concat_axis=0, tiled=True)]
    all_to_all x2 -> x3, starting transfers between devices: 15.3 us -> 20.5 us  [exchange(): lax.all_to_all(member, ('exp', 'grp', 'half'), split_axis=0, concat_axis=...]
    pallas_call x1 -> x2, Pallas kernels: 7.38 us -> 11.2 us  [the longest x1 5.75 us: combine(): pl.pallas_call(combine_kernel, grid=(width // 2 // thin,), in_specs=[whol...]
  transfers between devices with their start and end apart: 5 -> 5, of which waited for: 3 -> 4; matrix products, arithmetic and copies ran while one was open for 2% -> 2% of each run, Pallas kernels for 12% -> 14%
where the time goes in v6:
time: 334 us; the launch traced here: 330 us
  waiting for transfers between devices  124 us (37%)
  Pallas kernels  84.9 us (25%)
  blocking collectives  79.2 us (24%)
  starting transfers between devices  33 us (10%)
  local copies, waits for them, and re-layouts  4.41 us (1%)
  other arithmetic  3.37 us (1%)
    all_to_all x1, blocking collectives, exchange(): lax.all_to_all(member, ('exp', 'grp', 'half'), split_axis=0, concat_axis=...  65.6 us
    all_to_all x3, waiting for transfers between devices, exchange(): lax.all_to_all(member, ('exp', 'grp', 'half'), split_axis=0, concat_axis=...  59.4 us
    all_to_all x1, waiting for transfers between devices, shards(): lax.all_to_all(parts, 'exp', split_axis=0, concat_axis=0, tiled=True)  51.3 us
    pallas_call x1, Pallas kernels, delta(): pl.pallas_call(delta_kernel, grid_spec=pltpu.PrefetchScalarGridSpec(num_s...  25 us
    pallas_call x1, Pallas kernels, experts_of(): pl.pallas_call(functools.partial(head_kernel, ups=ups), in_specs=in_specs...  21.5 us
    all_to_all x3, starting transfers between devices, exchange(): lax.all_to_all(member, ('exp', 'grp', 'half'), split_axis=0, concat_axis=...  20.5 us
    pallas_call x1, Pallas kernels, experts_of(): pl.pallas_call(functools.partial(tail_kernel, ups=ups), in_specs=in_specs...  16 us
    all_to_all x1, blocking collectives, shards(): lax.all_to_all(final, 'exp', split_axis=0, concat_axis=0, tiled=True)  13.6 us
  transfers between devices with their start and end apart: 5, of which 4 were waited for; matrix products, arithmetic and copies ran while one was open for 2% of the time, Pallas kernels for 14%

profile of v6, /device:TPU:24, one launch (start us, length us, event | category | flops | bytes accessed | tf_op | source)
XLA Modules:
  0.0 329.9 jit_solution(1086708920633975649)
XLA Ops:
  0.6 25.0 %delta.1 = (bf16[8,128,2304]{2,1,0:T(8,128)(2,1)}, bf16[8,128,128]{2,1,0:T(8,128)(2,1)}) custom-call(s32[2]{0:T(128)} %counts.1, bf16[4096,128]{1,0:T(8,128)(2,1)} %bitcast.98, bf16[4096,128]{1,0:T(8,128)(2,1)} %bitcast.99, bf16[4096,128]{1,0:T(8,128)(2,1)} %bitcast.100, f32[4096,128]{1,0:T(8,128)} %bitcast.97, f32[2,4,512]{2,1,0:T(4,128)} %bitcast.102, ...), custom_call_target="tpu_custom_call" | custom-call | flops 8000000000 | bytes 16000000 | tf_op jit(solution)/shard_map/delta/pallas_call | solution.py:180
  25.6 0.0 copy-start.6
  25.6 0.0 copy-start.7
  25.6 7.3 %all-to-all-start = ((bf16[8,128,2304]{2,1,0:T(8,128)(2,1)}), bf16[8,128,2304]{2,1,0:T(8,128)(2,1)}, u32[]{:S(2)}, u32[]{:S(2)}) async-start(bf16[8,128,2304]{2,1,0:T(8,128)(2,1)} %get-tuple-element.21), calls=%async_computation | async-start | bytes 9437184 | tf_op jit(solution)/shard_map/all_to_all | solution.py:613
  32.9 0.0 copy-done.1
  32.9 0.1 copy.31
  33.0 0.3 reshape.150
  33.3 1.4 copy.32
  34.8 0.7 reshape.162.ids_ref
  35.4 0.6 reshape.161.gain_ref
  36.0 51.3 %all-to-all-done.part_ref = bf16[8,128,2304]{2,1,0:T(8,128)(2,1)} async-done(((bf16[8,128,2304]{2,1,0:T(8,128)(2,1)}), bf16[8,128,2304]{2,1,0:T(8,128)(2,1)}, u32[]{:S(2)}, u32[]{:S(2)}) %all-to-all-start) | async-done | bytes 4718624 | tf_op jit(solution)/shard_map/all_to_all | solution.py:613
  87.3 8.6 %route.1 = (f32[128,2304]{1,0:T(8,128)}, f32[128,128]{1,0:T(8,128)}, f32[128,128]{1,0:T(8,128)}, bf16[1024,2304]{1,0:T(8,128)(2,1)}, bf16[1024,1152]{1,0:T(8,128)(2,1)}) custom-call(bf16[2304,128]{1,0:T(8,128)(2,1)} %bitcast.89, bf16[8,128,2304]{2,1,0:T(8,128)(2,1)} %all-to-all-done.part_ref, bf16[1,2304]{1,0:T(2,128)(2,1)} %reshape.161.gain_ref, ...), custom_call_target="tpu_custom_call" | custom-call | flops 2000000000 | bytes 14000000 | tf_op jit(solution)/shard_map/route/pallas_call | solution.py:322
  95.9 65.6 %all_to_all.30 = bf16[128,8,2304]{2,1,0:T(8,128)(2,1)} all-to-all(bf16[128,8,2304]{2,1,0:T(8,128)(2,1)} %bitcast.74), channel_id=1, replica_groups=mesh['half'=2,'grp'=8,'exp'=8] {'exp','grp','half'}, dimensions={0} | all-to-all | bytes 9437184 | tf_op jit(solution)/shard_map/all_to_all | solution.py:618
  161.5 6.4 %all-to-all-start.2 = ((bf16[128,8,1152]{2,1,0:T(8,128)(2,1)}), bf16[128,8,1152]{2,1,0:T(8,128)(2,1)S(1)}, u32[]{:S(2)}, u32[]{:S(2)}) async-start(bf16[128,8,1152]{2,1,0:T(8,128)(2,1)} %bitcast.85), calls=%async_computation.2 | async-start | bytes 4718592 | tf_op jit(solution)/shard_map/all_to_all | solution.py:618
  167.9 5.2 %collective-permute-start = (bf16[8,128,128]{2,1,0:T(8,128)(2,1)S(1)}, bf16[8,128,128]{2,1,0:T(8,128)(2,1)S(1)}, u32[]{:S(2)}, u32[]{:S(2)}) collective-permute-start(bf16[8,128,128]{2,1,0:T(8,128)(2,1)S(1)} %copy-done.9), channel_id=1, source_target_pairs={{0,0},{1,8},{2,16},{3,24},{4,32},{5,40},{6,48},{7,56},{8,1},{9,9},... | collective-permute-start | bytes 786440 | tf_op jit(solution)/shard_map/ppermute | solution.py:608
  173.1 21.5 %experts_head.1 = bf16[1024,2304]{1,0:T(8,128)(2,1)} custom-call(bf16[1024,2304]{1,0:T(8,128)(2,1)} %bitcast.73, bf16[2304,1024]{1,0:T(8,128)(2,1)} %bitcast.91, bf16[2304,1024]{1,0:T(8,128)(2,1)} %bitcast.93, bf16[1024,2304]{1,0:T(8,128)(2,1)} %bitcast.95), custom_call_target="tpu_custom_call" | custom-call | flops 14495514624 | bytes 23592960 | tf_op jit(solution)/shard_map/experts_head/pallas_call | solution.py:448
  194.6 13.5 %collective-permute-done = bf16[8,128,128]{2,1,0:T(8,128)(2,1)S(1)} collective-permute-done((bf16[8,128,128]{2,1,0:T(8,128)(2,1)S(1)}, bf16[8,128,128]{2,1,0:T(8,128)(2,1)S(1)}, u32[]{:S(2)}, u32[]{:S(2)}) %collective-permute-start) | collective-permute-done | bytes 262176 | tf_op jit(solution)/shard_map/ppermute | solution.py:608
  208.1 0.0 all-to-all-done.2
  208.1 13.6 %all_to_all.31 = bf16[8,128,128]{2,1,0:T(8,128)(2,1)S(1)} all-to-all(bf16[8,128,128]{2,1,0:T(8,128)(2,1)S(1)} %collective-permute-done), channel_id=1, replica_groups=mesh['half'=2,'grp'=8,'exp'=8] {'exp'}, dimensions={0} | all-to-all | bytes 524288 | tf_op jit(solution)/shard_map/all_to_all | solution.py:629
  221.7 7.3 %all-to-all-start.4 = ((bf16[128,8,2304]{2,1,0:T(8,128)(2,1)}), bf16[128,8,2304]{2,1,0:T(8,128)(2,1)}, u32[]{:S(2)}, u32[]{:S(2)}) async-start(bf16[128,8,2304]{2,1,0:T(8,128)(2,1)} %bitcast.72), calls=%async_computation.4 | async-start | bytes 9437184 | tf_op jit(solution)/shard_map/all_to_all | solution.py:618
  228.9 0.0 copy-done.5
  229.0 0.1 fusion.1
  229.2 0.1 convert_multiply_fusion.1
  229.3 16.0 %experts_tail.1 = bf16[1024,1152]{1,0:T(8,128)(2,1)} custom-call(bf16[1024,1152]{1,0:T(8,128)(2,1)} %bitcast.84, bf16[2304,1024]{1,0:T(8,128)(2,1)} %bitcast.92, bf16[2304,1024]{1,0:T(8,128)(2,1)} %bitcast.94, bf16[1024,2304]{1,0:T(8,128)(2,1)} %bitcast.96), custom_call_target="tpu_custom_call" | custom-call | flops 7247757312 | bytes 18874368 | tf_op jit(solution)/shard_map/experts_tail/pallas_call | solution.py:457
  245.3 41.6 %all-to-all-done.4 = bf16[128,8,2304]{2,1,0:T(8,128)(2,1)} async-done(((bf16[128,8,2304]{2,1,0:T(8,128)(2,1)}), bf16[128,8,2304]{2,1,0:T(8,128)(2,1)}, u32[]{:S(2)}, u32[]{:S(2)}) %all-to-all-start.4) | async-done | bytes 4718624 | tf_op jit(solution)/shard_map/all_to_all | solution.py:618
  286.9 6.8 %all-to-all-start.5 = ((bf16[128,8,1152]{2,1,0:T(8,128)(2,1)}), bf16[128,8,1152]{2,1,0:T(8,128)(2,1)}, u32[]{:S(2)}, u32[]{:S(2)}) async-start(bf16[128,8,1152]{2,1,0:T(8,128)(2,1)} %bitcast.83), calls=%async_computation.5 | async-start | bytes 4718592 | tf_op jit(solution)/shard_map/all_to_all | solution.py:618
  293.7 0.1 copy.38
  293.7 0.1 mul.175
  293.8 0.1 mul.176
  293.9 0.1 squeeze.24
  294.0 0.1 copy.39
  294.1 0.1 mul.195
  294.2 0.1 mul.196
  294.3 0.1 squeeze.25
  294.4 2.7 spread.1
  297.2 0.2 multiply_reduce_fusion.3
  297.4 0.1 reduce_sum.54
  297.7 0.6 multiply_reduce_fusion.1
  298.3 0.1 reduce_sum.55
  298.5 0.4 multiply_reduce_fusion
  298.8 0.1 stack.10
  298.9 0.1 stack.9
  299.0 0.7 maximum_multiply_fusion
  299.7 0.1 fusion.3
  299.8 1.1 add_bitcast_fusion
  300.9 5.4 %add_heads.1.total_ref = f32[128,2304]{1,0:T(8,128)} custom-call(f32[128,2304]{1,0:T(8,128)} %get-tuple-element.22.mixed_ref, bf16[256,1024]{1,0:T(8,128)(2,1)} %get-tuple-element.25.heads, bf16[1024,2304]{1,0:T(8,128)(2,1)} %bitcast.25.back_ref), custom_call_target="tpu_custom_call" | custom-call | flops 3000000000 | bytes 8000000 | tf_op jit(solution)/shard_map/add_heads/pallas_call | solution.py:516
  306.3 17.8 %all-to-all-done.5 = bf16[128,8,1152]{2,1,0:T(8,128)(2,1)} async-done(((bf16[128,8,1152]{2,1,0:T(8,128)(2,1)}), bf16[128,8,1152]{2,1,0:T(8,128)(2,1)}, u32[]{:S(2)}, u32[]{:S(2)}) %all-to-all-start.5) | async-done | bytes 2359328 | tf_op jit(solution)/shard_map/all_to_all | solution.py:618
  324.2 5.8 %combine.1 = bf16[64,2,2304]{2,1,0:T(2,128)(2,1)} custom-call(f32[128,2304]{1,0:T(8,128)} %add_heads.1.total_ref, bf16[512,1024]{1,0:T(8,128)(2,1)} %get-tuple-element.36.tails, bf16[1024,1152]{1,0:T(8,128)(2,1)} %bitcast.27.back_ref), custom_call_target="tpu_custom_call" | custom-call | flops 2000000000 | bytes 6000000 | tf_op jit(solution)/shard_map/combine/pallas_call | solution.py:560
  (32 shorter events, 0.4 us)
Async XLA Ops:
  25.6 7.3 %copy-start.1 = (bf16[64,2,2304]{2,1,0:T(2,128)(2,1)S(1)}, bf16[64,2,2304]{2,1,0:T(2,128)(2,1)}, u32[]{:S(2)}) copy-start(bf16[64,2,2304]{2,1,0:T(2,128)(2,1)} %param.20) | copy-start | bytes 1769476
  25.6 9.2 %copy-start.6 = (s32[64,2,8]{0,2,1:T(8,128)S(1)}, s32[64,2,8]{0,2,1:T(8,128)}, u32[]{:S(2)}) copy-start(s32[64,2,8]{0,2,1:T(8,128)} %param.31) | copy-start | bytes 12292
  25.6 9.8 %copy-start.7 = (bf16[2304]{0:T(1024)(128)(2,1)S(1)}, bf16[2304]{0:T(1024)(128)(2,1)}, u32[]{:S(2)}) copy-start(bf16[2304]{0:T(1024)(128)(2,1)} %param.29) | copy-start | bytes 13828
  25.6 61.7 %all-to-all-start = ((bf16[8,128,2304]{2,1,0:T(8,128)(2,1)}), bf16[8,128,2304]{2,1,0:T(8,128)(2,1)}, u32[]{:S(2)}, u32[]{:S(2)}) async-start(bf16[8,128,2304]{2,1,0:T(8,128)(2,1)} %get-tuple-element.21), calls=%async_computation | async-start | bytes 9437184 | tf_op jit(solution)/shard_map/all_to_all | solution.py:613
  161.5 6.4 %copy-start.9 = (bf16[8,128,128]{2,1,0:T(8,128)(2,1)S(1)}, bf16[8,128,128]{2,1,0:T(8,128)(2,1)}, u32[]{:S(2)}) copy-start(bf16[8,128,128]{2,1,0:T(8,128)(2,1)} %get-tuple-element.30) | copy-start | bytes 786436
  161.5 46.6 %all-to-all-start.2 = ((bf16[128,8,1152]{2,1,0:T(8,128)(2,1)}), bf16[128,8,1152]{2,1,0:T(8,128)(2,1)S(1)}, u32[]{:S(2)}, u32[]{:S(2)}) async-start(bf16[128,8,1152]{2,1,0:T(8,128)(2,1)} %bitcast.85), calls=%async_computation.2 | async-start | bytes 4718592 | tf_op jit(solution)/shard_map/all_to_all | solution.py:618
  167.9 40.1 %collective-permute-start = (bf16[8,128,128]{2,1,0:T(8,128)(2,1)S(1)}, bf16[8,128,128]{2,1,0:T(8,128)(2,1)S(1)}, u32[]{:S(2)}, u32[]{:S(2)}) collective-permute-start(bf16[8,128,128]{2,1,0:T(8,128)(2,1)S(1)} %copy-done.9), channel_id=1, source_target_pairs={{0,0},{1,8},{2,16},{3,24},{4,32},{5,40},{6,48},{7,56},{8,1},{9,9},... | collective-permute-start | bytes 786440 | tf_op jit(solution)/shard_map/ppermute | solution.py:608
  208.1 13.6 %copy-start = (bf16[128,8,1152]{2,1,0:T(8,128)(2,1)}, bf16[128,8,1152]{2,1,0:T(8,128)(2,1)S(1)}, u32[]{:S(2)}) copy-start(bf16[128,8,1152]{2,1,0:T(8,128)(2,1)S(1)} %all-to-all-done.2) | copy-start | bytes 7077892
  221.6 7.3 %copy-start.5 = (bf16[16,2,4,128]{3,2,1,0:T(4,128)(2,1)S(1)}, bf16[16,2,4,128]{3,2,1,0:T(4,128)(2,1)}, u32[]{:S(2)}) copy-start(bf16[16,2,4,128]{3,2,1,0:T(4,128)(2,1)} %param.35) | copy-start | bytes 98308
  221.6 7.3 %copy-start.3 = (bf16[16,2,4,128]{3,2,1,0:T(4,128)(2,1)S(1)}, bf16[16,2,4,128]{3,2,1,0:T(4,128)(2,1)}, u32[]{:S(2)}) copy-start(bf16[16,2,4,128]{3,2,1,0:T(4,128)(2,1)} %param.36) | copy-start | bytes 98308
  221.6 7.5 %copy-start.2 = (bf16[16,2,4,16]{3,2,1,0:T(4,128)(2,1)S(1)}, bf16[16,2,4,16]{3,2,1,0:T(4,128)(2,1)}, u32[]{:S(2)}) copy-start(bf16[16,2,4,16]{3,2,1,0:T(4,128)(2,1)} %param.37) | copy-start | bytes 12292
  221.7 65.2 %all-to-all-start.4 = ((bf16[128,8,2304]{2,1,0:T(8,128)(2,1)}), bf16[128,8,2304]{2,1,0:T(8,128)(2,1)}, u32[]{:S(2)}, u32[]{:S(2)}) async-start(bf16[128,8,2304]{2,1,0:T(8,128)(2,1)} %bitcast.72), calls=%async_computation.4 | async-start | bytes 9437184 | tf_op jit(solution)/shard_map/all_to_all | solution.py:618
  245.3 48.4 %copy-start.8 = (f32[16,2,4]{0,2,1:T(4,128)S(1)}, f32[16,2,4]{0,2,1:T(4,128)}, u32[]{:S(2)}) copy-start(f32[16,2,4]{0,2,1:T(4,128)} %param.39) | copy-start | bytes 1540
  245.3 49.1 %copy-start.4 = (f32[16,2,4,128]{3,2,1,0:T(4,128)S(1)}, f32[16,2,4,128]{3,2,1,0:T(4,128)}, u32[]{:S(2)}) copy-start(f32[16,2,4,128]{3,2,1,0:T(4,128)} %param.38) | copy-start | bytes 196612
  286.9 37.3 %all-to-all-start.5 = ((bf16[128,8,1152]{2,1,0:T(8,128)(2,1)}), bf16[128,8,1152]{2,1,0:T(8,128)(2,1)}, u32[]{:S(2)}, u32[]{:S(2)}) async-start(bf16[128,8,1152]{2,1,0:T(8,128)(2,1)} %bitcast.83), calls=%async_computation.5 | async-start | bytes 4718592 | tf_op jit(solution)/shard_map/all_to_all | solution.py:618

commit v7 on v6

--- a/solution.py
+++ b/solution.py
@@ -625,11 +625,11 @@
     tail = exchange(tail)
     heads_of, tails_of = spread_of(slot, weight)
     matrices = (w_gate[0], w_up[0], w_down[0])
-    head, tail, final = lax.optimization_barrier((experts_of(head, *matrices), tail, final))
+    head, tail, final = lax.optimization_barrier(
+        (exchange(experts_of(head, *matrices)), experts_of(tail, *matrices), final)
+    )
     relaid = lax.all_to_all(final, "exp", split_axis=0, concat_axis=0, tiled=True)
-    head, relaid = lax.optimization_barrier((head, relaid))
-    head = exchange(head)
-    head, tail = lax.optimization_barrier((head, experts_of(tail, *matrices)))
+    tail, relaid = lax.optimization_barrier((tail, relaid))
     tail = exchange(tail)
     relaid = relaid.reshape(groups * requests, heads, value_dim // members, key_dim)
     dec_out, dec_state = decode(relaid, dec_query, dec_key, dec_value, dec_decay, dec_beta)

time: 334 us -> 336 us (level)
  blocking collectives: 79.2 us -> 65.6 us
  starting transfers between devices: 33 us -> 42.8 us
  waiting for transfers between devices: 124 us -> 128 us
    all_to_all x3, waiting for transfers between devices: 59.4 us -> 27.2 us  [exchange(): lax.all_to_all(member, ('exp', 'grp', 'half'), split_axis=0, concat_axis=...]
    ppermute x1, waiting for transfers between devices: 13.5 us -> 43.7 us  [shards(): lax.ppermute(final, ('grp', 'exp'), [(g * members + e, e * members + g) f...]
    all_to_all x1 -> x0, blocking collectives: 13.6 us -> none  [shards(): lax.all_to_all(final, 'exp', split_axis=0, concat_axis=0, tiled=True)]
    all_to_all x0 -> x1, starting transfers between devices: none -> 8.75 us  [shards(): lax.all_to_all(final, 'exp', split_axis=0, concat_axis=0, tiled=True)]
    all_to_all x0 -> x1, waiting for transfers between devices: none -> 6.19 us  [shards(): lax.all_to_all(final, 'exp', split_axis=0, concat_axis=0, tiled=True)]
  transfers between devices with their start and end apart: 5 -> 6, of which waited for: 4 -> 5; matrix products, arithmetic and copies ran while one was open for 2% -> 2% of each run, Pallas kernels for 14% -> 14%
where the time goes in v7:
time: 336 us; the launch traced here: 332 us
  waiting for transfers between devices  128 us (38%)
  Pallas kernels  84.9 us (25%)
  blocking collectives  65.6 us (20%)
  starting transfers between devices  42.8 us (13%)
  local copies, waits for them, and re-layouts  5.86 us (2%)
  other arithmetic  3.37 us (1%)
    all_to_all x1, blocking collectives, exchange(): lax.all_to_all(member, ('exp', 'grp', 'half'), split_axis=0, concat_axis=...  65.6 us
    all_to_all x1, waiting for transfers between devices, shards(): lax.all_to_all(parts, 'exp', split_axis=0, concat_axis=0, tiled=True)  51.3 us
    ppermute x1, waiting for transfers between devices, shards(): lax.ppermute(final, ('grp', 'exp'), [(g * members + e, e * members + g) f...  43.7 us
    all_to_all x3, waiting for transfers between devices, exchange(): lax.all_to_all(member, ('exp', 'grp', 'half'), split_axis=0, concat_axis=...  27.2 us
    pallas_call x1, Pallas kernels, delta(): pl.pallas_call(delta_kernel, grid_spec=pltpu.PrefetchScalarGridSpec(num_s...  25 us
    pallas_call x1, Pallas kernels, experts_of(): pl.pallas_call(functools.partial(head_kernel, ups=ups), in_specs=in_specs...  21.5 us
    all_to_all x3, starting transfers between devices, exchange(): lax.all_to_all(member, ('exp', 'grp', 'half'), split_axis=0, concat_axis=...  21.3 us
    pallas_call x1, Pallas kernels, experts_of(): pl.pallas_call(functools.partial(tail_kernel, ups=ups), in_specs=in_specs...  16 us
  transfers between devices with their start and end apart: 6, of which 5 were waited for; matrix products, arithmetic and copies ran while one was open for 2% of the time, Pallas kernels for 14%

profile of v7, /device:TPU:24, one launch (start us, length us, event | category | flops | bytes accessed | tf_op | source)
XLA Modules:
  0.0 331.8 jit_solution(8439187330018997652)
XLA Ops:
  0.6 25.0 %delta.1 = (bf16[8,128,2304]{2,1,0:T(8,128)(2,1)}, bf16[8,128,128]{2,1,0:T(8,128)(2,1)}) custom-call(s32[2]{0:T(128)} %counts.1, bf16[4096,128]{1,0:T(8,128)(2,1)} %bitcast.98, bf16[4096,128]{1,0:T(8,128)(2,1)} %bitcast.99, bf16[4096,128]{1,0:T(8,128)(2,1)} %bitcast.100, f32[4096,128]{1,0:T(8,128)} %bitcast.97, f32[2,4,512]{2,1,0:T(4,128)} %bitcast.102, ...), custom_call_target="tpu_custom_call" | custom-call | flops 8000000000 | bytes 16000000 | tf_op jit(solution)/shard_map/delta/pallas_call | solution.py:180
  25.6 0.0 copy-start.6
  25.6 0.0 copy-start.7
  25.6 7.3 %all-to-all-start = ((bf16[8,128,2304]{2,1,0:T(8,128)(2,1)}), bf16[8,128,2304]{2,1,0:T(8,128)(2,1)}, u32[]{:S(2)}, u32[]{:S(2)}) async-start(bf16[8,128,2304]{2,1,0:T(8,128)(2,1)} %get-tuple-element.19), calls=%async_computation | async-start | bytes 9437184 | tf_op jit(solution)/shard_map/all_to_all | solution.py:613
  32.9 0.1 copy.31
  33.0 0.3 reshape.150
  33.3 1.4 copy.32
  34.8 0.7 reshape.162.ids_ref
  35.4 0.6 reshape.161.gain_ref
  36.0 51.3 %all-to-all-done.part_ref = bf16[8,128,2304]{2,1,0:T(8,128)(2,1)} async-done(((bf16[8,128,2304]{2,1,0:T(8,128)(2,1)}), bf16[8,128,2304]{2,1,0:T(8,128)(2,1)}, u32[]{:S(2)}, u32[]{:S(2)}) %all-to-all-start) | async-done | bytes 4718624 | tf_op jit(solution)/shard_map/all_to_all | solution.py:613
  87.3 8.5 %route.1 = (f32[128,2304]{1,0:T(8,128)}, f32[128,128]{1,0:T(8,128)}, f32[128,128]{1,0:T(8,128)}, bf16[1024,2304]{1,0:T(8,128)(2,1)}, bf16[1024,1152]{1,0:T(8,128)(2,1)}) custom-call(bf16[2304,128]{1,0:T(8,128)(2,1)} %bitcast.89, bf16[8,128,2304]{2,1,0:T(8,128)(2,1)} %all-to-all-done.part_ref, bf16[1,2304]{1,0:T(2,128)(2,1)} %reshape.161.gain_ref, ...), custom_call_target="tpu_custom_call" | custom-call | flops 2000000000 | bytes 14000000 | tf_op jit(solution)/shard_map/route/pallas_call | solution.py:322
  95.9 65.6 %all_to_all.30 = bf16[128,8,2304]{2,1,0:T(8,128)(2,1)} all-to-all(bf16[128,8,2304]{2,1,0:T(8,128)(2,1)} %bitcast.73), channel_id=1, replica_groups=mesh['half'=2,'grp'=8,'exp'=8] {'exp','grp','half'}, dimensions={0} | all-to-all | bytes 9437184 | tf_op jit(solution)/shard_map/all_to_all | solution.py:618
  161.5 6.4 %all-to-all-start.3 = ((bf16[128,8,1152]{2,1,0:T(8,128)(2,1)}), bf16[128,8,1152]{2,1,0:T(8,128)(2,1)S(1)}, u32[]{:S(2)}, u32[]{:S(2)}) async-start(bf16[128,8,1152]{2,1,0:T(8,128)(2,1)} %bitcast.85), calls=%async_computation.3 | async-start | bytes 4718592 | tf_op jit(solution)/shard_map/all_to_all | solution.py:618
  167.9 21.5 %experts_head.1 = bf16[1024,2304]{1,0:T(8,128)(2,1)} custom-call(bf16[1024,2304]{1,0:T(8,128)(2,1)} %bitcast.74, bf16[2304,1024]{1,0:T(8,128)(2,1)} %bitcast.91, bf16[2304,1024]{1,0:T(8,128)(2,1)} %bitcast.93, bf16[1024,2304]{1,0:T(8,128)(2,1)} %bitcast.95), custom_call_target="tpu_custom_call" | custom-call | flops 14495514624 | bytes 23592960 | tf_op jit(solution)/shard_map/experts_head/pallas_call | solution.py:448
  189.4 9.4 %all-to-all-done.3 = bf16[128,8,1152]{2,1,0:T(8,128)(2,1)S(1)} async-done(((bf16[128,8,1152]{2,1,0:T(8,128)(2,1)}), bf16[128,8,1152]{2,1,0:T(8,128)(2,1)S(1)}, u32[]{:S(2)}, u32[]{:S(2)}) %all-to-all-start.3) | async-done | bytes 2359328 | tf_op jit(solution)/shard_map/all_to_all | solution.py:618
  198.8 0.0 copy-start.2
  198.8 1.4 copy-done
  200.2 7.8 %all-to-all-start.2 = ((bf16[128,8,2304]{2,1,0:T(8,128)(2,1)}), bf16[128,8,2304]{2,1,0:T(8,128)(2,1)}, u32[]{:S(2)}, u32[]{:S(2)}) async-start(bf16[128,8,2304]{2,1,0:T(8,128)(2,1)} %bitcast.72), calls=%async_computation.2 | async-start | bytes 9437184 | tf_op jit(solution)/shard_map/all_to_all | solution.py:618
  208.0 5.4 %collective-permute-start = (bf16[8,128,128]{2,1,0:T(8,128)(2,1)S(1)}, bf16[8,128,128]{2,1,0:T(8,128)(2,1)}, u32[]{:S(2)}, u32[]{:S(2)}) collective-permute-start(bf16[8,128,128]{2,1,0:T(8,128)(2,1)S(1)} %copy-done.9), channel_id=1, source_target_pairs={{0,0},{1,8},{2,16},{3,24},{4,32},{5,40},{6,48},{7,56},{8,1},{9,9},... | collective-permute-start | bytes 786440 | tf_op jit(solution)/shard_map/ppermute | solution.py:608
  213.5 0.1 fusion.1
  213.7 16.0 %experts_tail.1 = bf16[1024,1152]{1,0:T(8,128)(2,1)} custom-call(bf16[1024,1152]{1,0:T(8,128)(2,1)} %bitcast.84, bf16[2304,1024]{1,0:T(8,128)(2,1)} %bitcast.92, bf16[2304,1024]{1,0:T(8,128)(2,1)} %bitcast.94, bf16[1024,2304]{1,0:T(8,128)(2,1)} %bitcast.96), custom_call_target="tpu_custom_call" | custom-call | flops 7247757312 | bytes 18874368 | tf_op jit(solution)/shard_map/experts_tail/pallas_call | solution.py:457
  229.7 43.7 %collective-permute-done = bf16[8,128,128]{2,1,0:T(8,128)(2,1)} collective-permute-done((bf16[8,128,128]{2,1,0:T(8,128)(2,1)S(1)}, bf16[8,128,128]{2,1,0:T(8,128)(2,1)}, u32[]{:S(2)}, u32[]{:S(2)}) %collective-permute-start) | collective-permute-done | bytes 262176 | tf_op jit(solution)/shard_map/ppermute | solution.py:608
  273.4 8.8 %all-to-all-start.4 = ((bf16[8,128,128]{2,1,0:T(8,128)(2,1)}), bf16[8,128,128]{2,1,0:T(8,128)(2,1)S(1)}, u32[]{:S(2)}, u32[]{:S(2)}) async-start(bf16[8,128,128]{2,1,0:T(8,128)(2,1)} %collective-permute-done), calls=%async_computation.4 | async-start | bytes 524288 | tf_op jit(solution)/shard_map/all_to_all | solution.py:631
  282.2 0.1 convert_multiply_fusion.1
  282.3 6.2 %all-to-all-done.4 = bf16[8,128,128]{2,1,0:T(8,128)(2,1)S(1)} async-done(((bf16[8,128,128]{2,1,0:T(8,128)(2,1)}), bf16[8,128,128]{2,1,0:T(8,128)(2,1)S(1)}, u32[]{:S(2)}, u32[]{:S(2)}) %all-to-all-start.4) | async-done | bytes 262176 | tf_op jit(solution)/shard_map/all_to_all | solution.py:631
  288.4 7.1 %all-to-all-start.5 = ((bf16[128,8,1152]{2,1,0:T(8,128)(2,1)}), bf16[128,8,1152]{2,1,0:T(8,128)(2,1)}, u32[]{:S(2)}, u32[]{:S(2)}) async-start(bf16[128,8,1152]{2,1,0:T(8,128)(2,1)} %bitcast.83), calls=%async_computation.5 | async-start | bytes 4718592 | tf_op jit(solution)/shard_map/all_to_all | solution.py:618
  295.6 0.1 copy.38
  295.6 0.1 mul.175
  295.7 0.1 mul.176
  295.8 0.1 squeeze.24
  295.9 0.1 copy.39
  296.0 0.1 mul.195
  296.1 0.1 mul.196
  296.2 0.1 squeeze.25
  296.3 2.7 spread.1
  299.0 5.4 %add_heads.1.total_ref = f32[128,2304]{1,0:T(8,128)} custom-call(f32[128,2304]{1,0:T(8,128)} %get-tuple-element.20.mixed_ref, bf16[256,1024]{1,0:T(8,128)(2,1)} %get-tuple-element.23.heads, bf16[1024,2304]{1,0:T(8,128)(2,1)} %bitcast.23.back_ref), custom_call_target="tpu_custom_call" | custom-call | flops 3000000000 | bytes 8000000 | tf_op jit(solution)/shard_map/add_heads/pallas_call | solution.py:516
  304.6 0.2 multiply_reduce_fusion.3
  304.8 0.1 reduce_sum.54
  305.0 0.6 multiply_reduce_fusion.1
  305.6 0.1 reduce_sum.55
  305.8 0.4 multiply_reduce_fusion
  306.2 0.1 stack.10
  306.3 0.1 stack.9
  306.3 0.7 maximum_multiply_fusion
  307.0 0.1 fusion.3
  307.1 1.1 add_bitcast_fusion
  308.2 17.8 %all-to-all-done.5 = bf16[128,8,1152]{2,1,0:T(8,128)(2,1)} async-done(((bf16[128,8,1152]{2,1,0:T(8,128)(2,1)}), bf16[128,8,1152]{2,1,0:T(8,128)(2,1)}, u32[]{:S(2)}, u32[]{:S(2)}) %all-to-all-start.5) | async-done | bytes 2359328 | tf_op jit(solution)/shard_map/all_to_all | solution.py:618
  326.1 5.8 %combine.1 = bf16[64,2,2304]{2,1,0:T(2,128)(2,1)} custom-call(f32[128,2304]{1,0:T(8,128)} %add_heads.1.total_ref, bf16[512,1024]{1,0:T(8,128)(2,1)} %get-tuple-element.30.tails, bf16[1024,1152]{1,0:T(8,128)(2,1)} %bitcast.27.back_ref), custom_call_target="tpu_custom_call" | custom-call | flops 2000000000 | bytes 6000000 | tf_op jit(solution)/shard_map/combine/pallas_call | solution.py:560
  (33 shorter events, 0.4 us)
Async XLA Ops:
  25.6 7.3 %copy-start.1 = (bf16[64,2,2304]{2,1,0:T(2,128)(2,1)S(1)}, bf16[64,2,2304]{2,1,0:T(2,128)(2,1)}, u32[]{:S(2)}) copy-start(bf16[64,2,2304]{2,1,0:T(2,128)(2,1)} %param.20) | copy-start | bytes 1769476
  25.6 9.2 %copy-start.6 = (s32[64,2,8]{0,2,1:T(8,128)S(1)}, s32[64,2,8]{0,2,1:T(8,128)}, u32[]{:S(2)}) copy-start(s32[64,2,8]{0,2,1:T(8,128)} %param.31) | copy-start | bytes 12292
  25.6 9.8 %copy-start.7 = (bf16[2304]{0:T(1024)(128)(2,1)S(1)}, bf16[2304]{0:T(1024)(128)(2,1)}, u32[]{:S(2)}) copy-start(bf16[2304]{0:T(1024)(128)(2,1)} %param.29) | copy-start | bytes 13828
  25.6 61.7 %all-to-all-start = ((bf16[8,128,2304]{2,1,0:T(8,128)(2,1)}), bf16[8,128,2304]{2,1,0:T(8,128)(2,1)}, u32[]{:S(2)}, u32[]{:S(2)}) async-start(bf16[8,128,2304]{2,1,0:T(8,128)(2,1)} %get-tuple-element.19), calls=%async_computation | async-start | bytes 9437184 | tf_op jit(solution)/shard_map/all_to_all | solution.py:613
  161.5 37.3 %all-to-all-start.3 = ((bf16[128,8,1152]{2,1,0:T(8,128)(2,1)}), bf16[128,8,1152]{2,1,0:T(8,128)(2,1)S(1)}, u32[]{:S(2)}, u32[]{:S(2)}) async-start(bf16[128,8,1152]{2,1,0:T(8,128)(2,1)} %bitcast.85), calls=%async_computation.3 | async-start | bytes 4718592 | tf_op jit(solution)/shard_map/all_to_all | solution.py:618
  198.8 1.5 copy-start
  198.8 9.3 %copy-start.9 = (bf16[8,128,128]{2,1,0:T(8,128)(2,1)S(1)}, bf16[8,128,128]{2,1,0:T(8,128)(2,1)}, u32[]{:S(2)}) copy-start(bf16[8,128,128]{2,1,0:T(8,128)(2,1)} %get-tuple-element.28) | copy-start | bytes 786436
  198.8 14.7 %copy-start.5 = (bf16[16,2,4,128]{3,2,1,0:T(4,128)(2,1)S(1)}, bf16[16,2,4,128]{3,2,1,0:T(4,128)(2,1)}, u32[]{:S(2)}) copy-start(bf16[16,2,4,128]{3,2,1,0:T(4,128)(2,1)} %param.35) | copy-start | bytes 98308
  198.8 14.7 %copy-start.3 = (bf16[16,2,4,128]{3,2,1,0:T(4,128)(2,1)S(1)}, bf16[16,2,4,128]{3,2,1,0:T(4,128)(2,1)}, u32[]{:S(2)}) copy-start(bf16[16,2,4,128]{3,2,1,0:T(4,128)(2,1)} %param.36) | copy-start | bytes 98308
  198.8 14.8 %copy-start.2 = (bf16[16,2,4,16]{3,2,1,0:T(4,128)(2,1)S(1)}, bf16[16,2,4,16]{3,2,1,0:T(4,128)(2,1)}, u32[]{:S(2)}) copy-start(bf16[16,2,4,16]{3,2,1,0:T(4,128)(2,1)} %param.37) | copy-start | bytes 12292
  200.2 73.2 %all-to-all-start.2 = ((bf16[128,8,2304]{2,1,0:T(8,128)(2,1)}), bf16[128,8,2304]{2,1,0:T(8,128)(2,1)}, u32[]{:S(2)}, u32[]{:S(2)}) async-start(bf16[128,8,2304]{2,1,0:T(8,128)(2,1)} %bitcast.72), calls=%async_computation.2 | async-start | bytes 9437184 | tf_op jit(solution)/shard_map/all_to_all | solution.py:618
  208.0 65.3 %collective-permute-start = (bf16[8,128,128]{2,1,0:T(8,128)(2,1)S(1)}, bf16[8,128,128]{2,1,0:T(8,128)(2,1)}, u32[]{:S(2)}, u32[]{:S(2)}) collective-permute-start(bf16[8,128,128]{2,1,0:T(8,128)(2,1)S(1)} %copy-done.9), channel_id=1, source_target_pairs={{0,0},{1,8},{2,16},{3,24},{4,32},{5,40},{6,48},{7,56},{8,1},{9,9},... | collective-permute-start | bytes 786440 | tf_op jit(solution)/shard_map/ppermute | solution.py:608
  229.7 65.9 %copy-start.8 = (f32[16,2,4]{0,2,1:T(4,128)S(1)}, f32[16,2,4]{0,2,1:T(4,128)}, u32[]{:S(2)}) copy-start(f32[16,2,4]{0,2,1:T(4,128)} %param.39) | copy-start | bytes 1540
  229.7 66.6 %copy-start.4 = (f32[16,2,4,128]{3,2,1,0:T(4,128)S(1)}, f32[16,2,4,128]{3,2,1,0:T(4,128)}, u32[]{:S(2)}) copy-start(f32[16,2,4,128]{3,2,1,0:T(4,128)} %param.38) | copy-start | bytes 196612
  273.4 15.1 %all-to-all-start.4 = ((bf16[8,128,128]{2,1,0:T(8,128)(2,1)}), bf16[8,128,128]{2,1,0:T(8,128)(2,1)S(1)}, u32[]{:S(2)}, u32[]{:S(2)}) async-start(bf16[8,128,128]{2,1,0:T(8,128)(2,1)} %collective-permute-done), calls=%async_computation.4 | async-start | bytes 524288 | tf_op jit(solution)/shard_map/all_to_all | solution.py:631
  288.4 37.6 %all-to-all-start.5 = ((bf16[128,8,1152]{2,1,0:T(8,128)(2,1)}), bf16[128,8,1152]{2,1,0:T(8,128)(2,1)}, u32[]{:S(2)}, u32[]{:S(2)}) async-start(bf16[128,8,1152]{2,1,0:T(8,128)(2,1)} %bitcast.83), calls=%async_computation.5 | async-start | bytes 4718592 | tf_op jit(solution)/shard_map/all_to_all | solution.py:618
